TPU v7x, 512 devices: a whole 4x8x8 slice. The times are simulated.
512 devices in a mesh: section: 32 (over y, z_hi), tensor: 16 (over x, z_lo, core).
Axes of the slice: x: 4, y: 8, z: 8 (z_hi: 4, z_lo: 2; z = z_hi * 2 + z_lo), core: 2. Of those that a mesh axis runs over, the one named last changes fastest.
Arguments:
- queries: bfloat16 [16384, 8192], P('section', 'tensor'), may hold values from -160 to 160
- keys: bfloat16 [4096, 1024], P('section'), may hold values from -8 to 8
- values: bfloat16 [4096, 1024], P('section'), may hold values from -6 to 6
- d_out: bfloat16 [16384, 8192], P('section', 'tensor'), may hold values from -6 to 6
- gate: float32 [1], replicated, may hold values from 0.3 to 1.5
- tiles: int32 [8], replicated, may hold values from 1 to 4, as said below
- text_len: int32 [8], replicated, may hold values from 512 to 2048, as said below
Outputs:
- d_queries: bfloat16 [16384, 8192], P('section', 'tensor')
- d_keys: float32 [4096, 1024], P(('section', 'tensor'))
- d_values: float32 [4096, 1024], P(('section', 'tensor'))
Inputs may be any that keep to these rules, and one draw needn't show every extreme that they name: Sample 0 has 4 tiles and at least one other sample has 1. `text_len`: at least one sample fills all 2048 text positions.
All inputs are finite; a program needn't handle non-finite values.
Results may differ from a plain program's by a relative error of at most 0.013.
Values may be sent and summed in bfloat16 or wider, within the bound.
No kernel may reach another device: no remote copies, remote signals or barrier semaphores. Data moves between devices by JAX's collectives and lax.ppermute only.
A program may use at most 64 MiB of HBM per device.

v0:
```python
import jax
import jax.numpy as jnp
from jax import lax
from jax.sharding import PartitionSpec as P

KVH = 8
HD = 128
SAMPLES = 8
TILE = 128


def from_partner(value, axis, distance):
    mask = 2**distance
    pairs = [(source, source ^ mask) for source in range(lax.axis_size(axis))]
    return lax.ppermute(value, axis, pairs)


def local(queries, keys, values, d_out, gate, tiles, text_len):
    n_tensor = lax.axis_size("tensor")
    n_section = lax.axis_size("section")
    group = n_section // SAMPLES
    sharing = max(1, n_tensor // KVH)
    local_kv = max(1, KVH // n_tensor)
    width = local_kv * HD
    tensor_idx = lax.axis_index("tensor")
    section_idx = lax.axis_index("section")
    sample = section_idx // group
    place = section_idx % group
    section_bits = group.bit_length() - 1
    scale = HD ** (-0.5)
    column_start = tensor_idx // sharing * width
    stacked = jnp.stack([keys, values])
    stacked = lax.dynamic_slice_in_dim(stacked, column_start, width, 2)
    for bit in range(section_bits):
        other = from_partner(stacked, "section", bit)
        lower = section_idx >> bit & 1 == 0
        stacked = jnp.where(
            lower, jnp.concatenate([stacked, other], 1), jnp.concatenate([other, stacked], 1)
        )
    img_rows = stacked.shape[1]
    txt_rows = queries.shape[0]
    local_q = queries.shape[1] // HD
    per_kv = local_q // local_kv
    whole_keys = stacked[0].reshape(img_rows, local_kv, HD)
    whole_values = stacked[1].reshape(img_rows, local_kv, HD)
    picked = jnp.arange(SAMPLES, dtype=jnp.int32) == sample
    n_tiles = jnp.sum(jnp.where(picked, tiles, 0))
    n_text = jnp.sum(jnp.where(picked, text_len, 0))
    live_rows = place * txt_rows + jnp.arange(txt_rows, dtype=jnp.int32) < n_text
    live_cols = jnp.arange(img_rows, dtype=jnp.int32) < n_tiles * TILE
    factor = jnp.tanh(gate[0])
    query_blk = queries.reshape(txt_rows, local_kv, per_kv, HD)
    scaled = jnp.where(live_rows[:, None], factor * d_out.astype(jnp.float32), 0.0).astype(
        jnp.bfloat16
    )
    scaled_blk = scaled.reshape(txt_rows, local_kv, per_kv, HD)
    score = (
        jnp.einsum("tkgd,jkd->kgtj", query_blk, whole_keys, preferred_element_type=jnp.float32)
        * scale
    )
    score = jnp.where(live_cols, score, -1e30)
    top = jnp.max(score, axis=-1, keepdims=True)
    expo = jnp.exp(score - top)
    prob = expo / jnp.sum(expo, axis=-1, keepdims=True)
    prob_b = prob.astype(jnp.bfloat16)
    attn = jnp.einsum("kgtj,jkd->tkgd", prob_b, whole_values, preferred_element_type=jnp.float32)
    delta = jnp.transpose(jnp.sum(scaled_blk.astype(jnp.float32) * attn, axis=-1), (1, 2, 0))
    dprob = jnp.einsum(
        "tkgd,jkd->kgtj", scaled_blk, whole_values, preferred_element_type=jnp.float32
    )
    dscore = (prob * (dprob - delta[..., None]) * scale).astype(jnp.bfloat16)
    d_queries = jnp.einsum("kgtj,jkd->tkgd", dscore, whole_keys, preferred_element_type=jnp.float32)
    d_queries = d_queries.astype(jnp.bfloat16).reshape(txt_rows, local_q * HD)
    key_terms = jnp.einsum("kgtj,tkgd->jkd", dscore, query_blk, preferred_element_type=jnp.float32)
    value_terms = jnp.einsum(
        "kgtj,tkgd->jkd", prob_b, scaled_blk, preferred_element_type=jnp.float32
    )
    partial_value = jnp.stack(
        [key_terms.reshape(img_rows, width), value_terms.reshape(img_rows, width)]
    )
    own_rows = img_rows // group
    for bit in range(section_bits):
        partial_value = partial_value + from_partner(
            partial_value.astype(jnp.bfloat16), "section", bit
        ).astype(partial_value.dtype)
    partial_value = lax.dynamic_slice_in_dim(partial_value, place * own_rows, own_rows, 1)
    spread = lax.all_to_all(
        partial_value.astype(jnp.bfloat16), "tensor", split_axis=1, concat_axis=2, tiled=True
    ).astype(partial_value.dtype)
    out_rows = spread.shape[1]
    result = jnp.sum(spread.reshape(2, out_rows, KVH, sharing, HD), axis=3).reshape(
        2, out_rows, KVH * HD
    )
    return (d_queries, result[0], result[1])


def solution(mesh):
    in_specs = (
        P("section", "tensor"),
        P("section", None),
        P("section", None),
        P("section", "tensor"),
        P(),
        P(),
        P(),
    )
    out_specs = (
        P("section", "tensor"),
        P(("section", "tensor"), None),
        P(("section", "tensor"), None),
    )
    return jax.shard_map(local, mesh=mesh, in_specs=in_specs, out_specs=out_specs, check_vma=False)
```

profile of v0, /device:TPU:1, one launch (start us, length us, event | category | flops | bytes accessed | tf_op | source)
XLA Modules:
  0.0 81.6 jit_solution(9357057325039315453)
XLA Ops:
  0.6 0.0 copy-start
  0.7 0.8 %fusion.40 = bf16[2,128,128]{2,1,0:T(8,128)(2,1)S(1)} fusion(s32[]{:T(128)S(6)} %select_n.57, bf16[1,128,1024]{2,1,0:T(8,128)(2,1)} %bitcast.156, bf16[1,128,1024]{2,1,0:T(8,128)(2,1)} %bitcast.157), kind=kLoop, calls=%fused_computation.43 | loop fusion | flops 131072 | bytes 589828 | tf_op jit(solution)/shard_map/stack | solution.py:32
  1.5 6.6 %collective-permute-start = (bf16[2,128,128]{2,1,0:T(8,128)(2,1)S(1)}, bf16[2,128,128]{2,1,0:T(8,128)(2,1)S(1)}, u32[]{:S(2)}, u32[]{:S(2)}) collective-permute-start(bf16[2,128,128]{2,1,0:T(8,128)(2,1)S(1)} %fusion.40), channel_id=1, source_target_pairs={{0,16},{16,0},{32,48},{48,32},{64,80},{80,64},{96,112},{112,96},{1... | collective-permute-start | bytes 196616 | tf_op jit(solution)/shard_map/ppermute | solution.py:15
  8.8 1.3 %fusion.41 = (s32[]{:T(128)}, s32[]{:T(128)}) fusion(s32[8]{0:T(128)} %param.12, s32[]{:T(128)S(6)} %select_n.60, s32[8]{0:T(128)} %param.13), kind=kLoop, calls=%fused_computation.49 | loop fusion | flops 38 | bytes 76 | tf_op jit(solution)/shard_map/reduce_sum | solution.py:47
  10.2 0.7 add_compare_fusion
  10.8 0.0 collective-permute-done
  10.9 8.8 %collective-permute-start.1 = (bf16[2,256,128]{2,1,0:T(8,128)(2,1)S(1)}, bf16[2,256,128]{2,1,0:T(8,128)(2,1)S(1)}, u32[]{:S(2)}, u32[]{:S(2)}) collective-permute-start(bf16[2,256,128]{2,1,0:T(8,128)(2,1)S(1)} %maximum_select_fusion.1), channel_id=1, source_target_pairs={{0,32},{16,48},{32,0},{48,16},{64,96},{80,112},{96,64},{112,80},{1... | collective-permute-start | bytes 393224 | tf_op jit(solution)/shard_map/ppermute | solution.py:15
  19.7 1.2 %select_convert_fusion = bf16[512,512]{1,0:T(8,128)(2,1)S(1)} fusion(bf16[512,512]{1,0:T(8,128)(2,1)} %param.10, f32[]{:T(128)} %bitcast.9, pred[512]{0:T(512)(128)(4,1)S(1)} %add_compare_fusion), kind=kLoop, calls=%fused_computation.25 | loop fusion | flops 1048576 | bytes 1049092 | tf_op jit(solution)/shard_map/convert_element_type | solution.py:53
  20.9 0.2 copy.57
  21.1 0.2 copy.37
  22.0 0.2 collective-permute-done.1
  22.2 0.1 maximum_select_fusion
  22.2 0.0 copy-done
  22.3 0.7 bitcast_reduce_fusion
  23.0 0.9 %fusion.5 = f32[4,512]{1,0:T(4,128)S(1)} fusion(f32[512,512,4]{1,0,2:T(8,128)S(1)} %get-tuple-element.17, f32[4,512]{1,0:T(4,128)S(1)} %get-tuple-element.16, pred[512]{0:T(512)(128)(4,1)S(1)} %iota_compare_fusion), kind=kLoop, calls=%fused_computation.9 | loop fusion | flops 4192256 | bytes 4211200 | tf_op jit(solution)/shard_map/reduce_sum | solution.py:64
  23.9 1.3 %fusion.24 = f32[512,4]{0,1:T(4,128)S(1)} fusion(f32[512,1,4,128]{0,3,2,1:T(8,128)S(1)} %bitcast.153, bf16[2,512,128]{2,1,0:T(8,128)(2,1)S(1)} %maximum_select_fusion, f32[4,512]{1,0:T(4,128)S(1)} %fusion.5, f32[4,512]{1,0:T(4,128)S(1)} %get-tuple-element.16, f32[512,512,4]{1,0,2:T(8,128)S(1)} %get-tuple-element.17, pred[512]{0:T(512)(128)(4,1)S(1)} %iota_compare_fusion), kind=kOutput, calls=%fused_computation.22 | convolution fusion | flops 274200576 | bytes 5399040 | tf_op jit(solution)/shard_map/kgtj,jkd->tkgd/dot_general | solution.py:66
  25.3 1.1 %fusion.27 = f32[1,512,128]{2,1,0:T(8,128)S(1)} fusion(bf16[512,4,128]{0,2,1:T(8,128)(2,1)S(1)} %bitcast.154, f32[4,512]{1,0:T(4,128)S(1)} %fusion.5, f32[4,512]{1,0:T(4,128)S(1)} %get-tuple-element.16, f32[512,512,4]{1,0,2:T(8,128)S(1)} %get-tuple-element.17, pred[512]{0:T(512)(128)(4,1)S(1)} %iota_compare_fusion), kind=kOutput, calls=%fused_computation.23 | convolution fusion | flops 273678336 | bytes 4997632 | tf_op jit(solution)/shard_map/kgtj,tkgd->jkd/dot_general | solution.py:75
  26.4 1.8 %fusion.2 = bf16[1,4,512,512]{2,3,1,0:T(8,128)(2,1)S(1)} fusion(bf16[512,4,128]{0,2,1:T(8,128)(2,1)S(1)} %bitcast.155, f32[4,512]{1,0:T(4,128)S(1)} %bitcast.160, f32[4,512]{1,0:T(4,128)S(1)} %fusion.5, f32[4,512]{1,0:T(4,128)S(1)} %get-tuple-element.16, f32[512,512,4]{1,0,2:T(8,128)S(1)} %get-tuple-element.17, pred[512]{0:T(512)(128)(4,1)S(1)} %iota_compare_fusion, ...), kind=kOutput, calls=%fused_computation.3 | convolution fusion | flops 276824064 | bytes 6971904 | tf_op jit(solution)/shard_map/tkgd,jkd->kgtj/dot_general | solution.py:68
  28.3 0.7 fusion.30
  29.0 5.3 %collective-permute-start.2 = (bf16[2,512,128]{2,1,0:T(8,128)(2,1)S(1)}, bf16[2,512,128]{2,1,0:T(8,128)(2,1)S(1)}, u32[]{:S(2)}, u32[]{:S(2)}) collective-permute-start(bf16[2,512,128]{2,1,0:T(8,128)(2,1)S(1)} %fusion.38), channel_id=1, source_target_pairs={{0,16},{16,0},{32,48},{48,32},{64,80},{80,64},{96,112},{112,96},{1... | collective-permute-start | bytes 786440 | tf_op jit(solution)/shard_map/ppermute | solution.py:15
  34.3 10.9 %collective-permute-done.2 = bf16[2,512,128]{2,1,0:T(8,128)(2,1)S(1)} collective-permute-done((bf16[2,512,128]{2,1,0:T(8,128)(2,1)S(1)}, bf16[2,512,128]{2,1,0:T(8,128)(2,1)S(1)}, u32[]{:S(2)}, u32[]{:S(2)}) %collective-permute-start.2) | collective-permute-done | bytes 262176 | tf_op jit(solution)/shard_map/ppermute | solution.py:15
  45.2 0.8 fusion.45
  46.0 9.6 %collective-permute-start.3 = (bf16[2,512,128]{2,1,0:T(8,128)(2,1)}, bf16[2,512,128]{2,1,0:T(8,128)(2,1)}, u32[]{:S(2)}, u32[]{:S(2)}) collective-permute-start(bf16[2,512,128]{2,1,0:T(8,128)(2,1)} %get-tuple-element.12), channel_id=1, source_target_pairs={{0,32},{16,48},{32,0},{48,16},{64,96},{80,112},{96,64},{112,80},{1... | collective-permute-start | bytes 786440 | tf_op jit(solution)/shard_map/ppermute | solution.py:15
  55.6 12.1 %collective-permute-done.3 = bf16[2,512,128]{2,1,0:T(8,128)(2,1)} collective-permute-done((bf16[2,512,128]{2,1,0:T(8,128)(2,1)}, bf16[2,512,128]{2,1,0:T(8,128)(2,1)}, u32[]{:S(2)}, u32[]{:S(2)}) %collective-permute-start.3) | collective-permute-done | bytes 262176 | tf_op jit(solution)/shard_map/ppermute | solution.py:15
  67.7 0.9 %fusion.39 = bf16[2,128,128]{2,1,0:T(8,128)(2,1)S(1)} fusion(f32[2,512,128]{2,1,0:T(8,128)S(1)} %get-tuple-element.13, s32[]{:T(128)S(6)} %select_n.67, bf16[2,512,128]{2,1,0:T(8,128)(2,1)} %collective-permute-done.3), kind=kLoop, calls=%fused_computation.38 | loop fusion | flops 98304 | bytes 262148 | tf_op jit(solution)/shard_map/convert_element_type | solution.py:88
  68.6 0.7 copy.46
  69.3 5.8 %all-to-all-start = ((bf16[2,128,128]{2,0,1:T(2,128)(2,1)}), bf16[2,128,128]{2,0,1:T(2,128)(2,1)S(1)}, u32[]{:S(2)}, u32[]{:S(2)}) async-start(bf16[2,128,128]{2,0,1:T(2,128)(2,1)} %copy.46), calls=%async_computation | async-start | bytes 131072 | tf_op jit(solution)/shard_map/all_to_all | solution.py:87
  75.0 0.5 fusion.21
  75.5 1.0 %copy.47 = bf16[512,512]{1,0:T(8,128)(2,1)} copy(bf16[512,512]{0,1:T(8,128)(2,1)S(1)} %bitcast.152) | data formatting | bytes 1048576
  76.5 4.3 %all-to-all-done = bf16[2,128,128]{2,0,1:T(2,128)(2,1)S(1)} async-done(((bf16[2,128,128]{2,0,1:T(2,128)(2,1)}), bf16[2,128,128]{2,0,1:T(2,128)(2,1)S(1)}, u32[]{:S(2)}, u32[]{:S(2)}) %all-to-all-start) | async-done | bytes 65568 | tf_op jit(solution)/shard_map/all_to_all | solution.py:87
  80.9 0.1 bitcast_reduce_fusion.1
  81.0 0.7 fusion.46
  (4 shorter events, 0.1 us)
Async XLA Ops:
  0.6 21.6 %copy-start = (bf16[512,512]{1,0:T(8,128)(2,1)S(1)}, bf16[512,512]{1,0:T(8,128)(2,1)}, u32[]{:S(2)}) copy-start(bf16[512,512]{1,0:T(8,128)(2,1)} %param.7) | copy-start | bytes 1572868
  1.5 9.3 %collective-permute-start = (bf16[2,128,128]{2,1,0:T(8,128)(2,1)S(1)}, bf16[2,128,128]{2,1,0:T(8,128)(2,1)S(1)}, u32[]{:S(2)}, u32[]{:S(2)}) collective-permute-start(bf16[2,128,128]{2,1,0:T(8,128)(2,1)S(1)} %fusion.40), channel_id=1, source_target_pairs={{0,16},{16,0},{32,48},{48,32},{64,80},{80,64},{96,112},{112,96},{1... | collective-permute-start | bytes 196616 | tf_op jit(solution)/shard_map/ppermute | solution.py:15
  10.9 11.3 %collective-permute-start.1 = (bf16[2,256,128]{2,1,0:T(8,128)(2,1)S(1)}, bf16[2,256,128]{2,1,0:T(8,128)(2,1)S(1)}, u32[]{:S(2)}, u32[]{:S(2)}) collective-permute-start(bf16[2,256,128]{2,1,0:T(8,128)(2,1)S(1)} %maximum_select_fusion.1), channel_id=1, source_target_pairs={{0,32},{16,48},{32,0},{48,16},{64,96},{80,112},{96,64},{112,80},{1... | collective-permute-start | bytes 393224 | tf_op jit(solution)/shard_map/ppermute | solution.py:15
  29.0 16.2 %collective-permute-start.2 = (bf16[2,512,128]{2,1,0:T(8,128)(2,1)S(1)}, bf16[2,512,128]{2,1,0:T(8,128)(2,1)S(1)}, u32[]{:S(2)}, u32[]{:S(2)}) collective-permute-start(bf16[2,512,128]{2,1,0:T(8,128)(2,1)S(1)} %fusion.38), channel_id=1, source_target_pairs={{0,16},{16,0},{32,48},{48,32},{64,80},{80,64},{96,112},{112,96},{1... | collective-permute-start | bytes 786440 | tf_op jit(solution)/shard_map/ppermute | solution.py:15
  46.0 21.7 %collective-permute-start.3 = (bf16[2,512,128]{2,1,0:T(8,128)(2,1)}, bf16[2,512,128]{2,1,0:T(8,128)(2,1)}, u32[]{:S(2)}, u32[]{:S(2)}) collective-permute-start(bf16[2,512,128]{2,1,0:T(8,128)(2,1)} %get-tuple-element.12), channel_id=1, source_target_pairs={{0,32},{16,48},{32,0},{48,16},{64,96},{80,112},{96,64},{112,80},{1... | collective-permute-start | bytes 786440 | tf_op jit(solution)/shard_map/ppermute | solution.py:15
  69.3 11.6 %all-to-all-start = ((bf16[2,128,128]{2,0,1:T(2,128)(2,1)}), bf16[2,128,128]{2,0,1:T(2,128)(2,1)S(1)}, u32[]{:S(2)}, u32[]{:S(2)}) async-start(bf16[2,128,128]{2,0,1:T(2,128)(2,1)} %copy.46), calls=%async_computation | async-start | bytes 131072 | tf_op jit(solution)/shard_map/all_to_all | solution.py:87
where the time goes:
time: 82.1 us; the launch traced here: 81.6 us
  starting transfers between devices  36.2 us (44%)
  waiting for transfers between devices  27.5 us (33%)
  other arithmetic  6.81 us (8%)
  matrix products  6.22 us (8%)
  local copies, waits for them, and re-layouts  2.8 us (3%)
  between operations  2.17 us (3%)
    ppermute x4, starting transfers between devices, from_partner(): return lax.ppermute(value, axis, pairs)  30.4 us
    ppermute x4, waiting for transfers between devices, from_partner(): return lax.ppermute(value, axis, pairs)  23.1 us
    all_to_all x1, starting transfers between devices, local(): lax.all_to_all(partial_value.astype(jnp.bfloat16), 'tensor', split_axis=1...  5.77 us
    all_to_all x1, waiting for transfers between devices, local(): lax.all_to_all(partial_value.astype(jnp.bfloat16), 'tensor', split_axis=1...  4.35 us
    dot_general x1, matrix products, local(): jnp.einsum('tkgd,jkd->kgtj', scaled_blk, whole_values, preferred_element_...  1.84 us
    convert_element_type x3, other arithmetic, local(): partial_value.astype(jnp.bfloat16)  1.68 us
  transfers between devices with their start and end apart: 5, of which 4 were waited for; matrix products, arithmetic and copies ran while one was open for 6% of the time, Pallas kernels for 0%

commit v1 on v0

v1 whole, which is shorter than its diff:
```python
import jax
import jax.numpy as jnp
from jax import lax
from jax.experimental import pallas as pl
from jax.experimental.pallas import tpu as pltpu
from jax.sharding import Mesh, PartitionSpec as P

HD = 128
TILE = 128
SCALE = HD**-0.5
LOG2E = 1.4426950408889634
AXES = ("y", "zh", "x", "zl", "c")
SIZES = (8, 4, 4, 2, 2)
BLOCKS = 4
HEADS_X = 2
PLANE = 64
GROUPS = ((1, 2, 4, 7), (0, 3, 5, 6))
NT = (((1,), (1,)), ((), ()))
VMEM = pl.BlockSpec(memory_space=pltpu.VMEM)
SMEM = pl.BlockSpec(memory_space=pltpu.SMEM)
ANY = pl.BlockSpec(memory_space=pl.ANY)


def pick_kernel(keys, values, out, sems):
    x, zh, zl = lax.axis_index("x"), lax.axis_index("zh"), lax.axis_index("zl")
    first = [z % 2 for z in GROUPS[0]]
    mine = jnp.where((zh == 0) | (zh == 3), 1, 0)
    group = jnp.where(mine == zl, 0, 1)
    copies = []
    for j in range(BLOCKS):
        lo = jnp.where(group == 0, first[j], 1 - first[j])
        column = pl.ds(pl.multiple_of((x * HEADS_X + lo) * HD, HD), HD)
        for k, source in enumerate((keys, values)):
            copies.append(
                pltpu.make_async_copy(source.at[:, column], out.at[j, k], sems.at[j, k])
            )
    for copy in copies:
        copy.start()
    for copy in copies:
        copy.wait()


def main_kernel(tiles, text_len, gate, kv, queries, d_out, d_queries, partial, keys_t, acc_k, acc_v):
    f32, bf16 = jnp.float32, jnp.bfloat16
    y, zh = lax.axis_index("y"), lax.axis_index("zh")
    n_tiles, n_text = tiles[y], text_len[y]
    rows, heads = queries.shape[0], queries.shape[1] // HD
    factor = jnp.tanh(jnp.full((8, HD), gate[0], f32))[0:1, 0:1]
    keys = jnp.concatenate([kv[b, 0] for b in range(BLOCKS)], 0)
    values = jnp.concatenate([kv[b, 1] for b in range(BLOCKS)], 0)
    keys_t[...] = keys.T
    live = lax.broadcasted_iota(jnp.int32, (rows, HD), 0) + zh * rows < n_text
    for h in range(heads):
        cols = pl.ds(h * HD, HD)
        q = queries[:, cols]
        s = jnp.where(live, factor * d_out[:, cols].astype(f32), 0.0).astype(bf16)
        score = lax.dot_general(keys, q, NT, preferred_element_type=f32)
        d_prob = lax.dot_general(values, s, NT, preferred_element_type=f32)
        blocks = [score[b * TILE : (b + 1) * TILE] for b in range(BLOCKS)]
        top = jnp.max(blocks[0], axis=0, keepdims=True)
        for b in range(1, BLOCKS):
            top = jnp.maximum(
                top, jnp.where(b < n_tiles, jnp.max(blocks[b], axis=0, keepdims=True), -3e38)
            )
        expo = []
        for b in range(BLOCKS):
            shift = top if b == 0 else jnp.where(b < n_tiles, top, 1e30)
            expo.append(jnp.exp2((blocks[b] - shift) * (SCALE * LOG2E)))
        expo = jnp.concatenate(expo, 0)
        prob = expo * (1.0 / jnp.sum(expo, axis=0, keepdims=True))
        delta = jnp.sum(prob * d_prob, axis=0, keepdims=True)
        d_score = (prob * (d_prob - delta) * SCALE).astype(bf16)
        term_k = jnp.dot(d_score, q, preferred_element_type=f32)
        term_v = jnp.dot(prob.astype(bf16), s, preferred_element_type=f32)
        if h == 0:
            acc_k[...] = term_k
            acc_v[...] = term_v
        else:
            acc_k[...] += term_k
            acc_v[...] += term_v
        d_q = jnp.dot(keys_t[...], d_score, preferred_element_type=f32)
        d_queries[:, cols] = d_q.T.astype(bf16)
    both = [acc[...].reshape(PLANE, 8, HD) for acc in (acc_k, acc_v)]
    partial[...] = jnp.concatenate(both, 1).astype(bf16)


def sum_kernel(pieces, d_keys, d_values):
    _, zhs, xs, zls, cs = SIZES
    for head in range(xs * zls):
        total = None
        for zh in range(zhs):
            for c in range(cs):
                piece = pieces[(zh * xs * zls + head) * cs + c].astype(jnp.float32)
                total = piece if total is None else total + piece
        cols = pl.ds(head * HD, HD)
        d_keys[:, cols] = total[:8]
        d_values[:, cols] = total[8:]


def local(queries, keys, values, d_out, gate, tiles, text_len):
    f32, bf16 = jnp.float32, jnp.bfloat16
    block, width = keys.shape
    picked = pl.pallas_call(
        pick_kernel,
        out_shape=jax.ShapeDtypeStruct((BLOCKS, 2, block, HD), bf16),
        in_specs=[ANY, ANY],
        out_specs=ANY,
        scratch_shapes=[pltpu.SemaphoreType.DMA((BLOCKS, 2))],
        name="pick",
    )(keys, values)
    kv = lax.all_to_all(picked, ("zh", "zl"), 0, 0, axis_index_groups=GROUPS)
    image = BLOCKS * block
    d_queries, partial = pl.pallas_call(
        main_kernel,
        out_shape=(
            jax.ShapeDtypeStruct(queries.shape, bf16),
            jax.ShapeDtypeStruct((PLANE, 16, HD), bf16),
        ),
        in_specs=[SMEM, SMEM, SMEM, VMEM, VMEM, VMEM],
        out_specs=(VMEM, VMEM),
        scratch_shapes=[
            pltpu.VMEM((HD, image), bf16),
            pltpu.VMEM((image, HD), f32),
            pltpu.VMEM((image, HD), f32),
        ],
        compiler_params=pltpu.CompilerParams(vmem_limit_bytes=40 * 2**20),
        name="gradients",
    )(tiles, text_len, gate, kv, queries, d_out)
    pieces = lax.all_to_all(partial, ("zh", "x", "zl", "c"), 0, 0)
    d_keys, d_values = pl.pallas_call(
        sum_kernel,
        out_shape=(jax.ShapeDtypeStruct((8, width), f32),) * 2,
        in_specs=[VMEM],
        out_specs=(VMEM, VMEM),
        name="add_up",
    )(pieces)
    return d_queries, d_keys, d_values


def solution(mesh):
    mesh = Mesh(mesh.devices.reshape(SIZES), AXES)
    section, tensor = ("y", "zh"), ("x", "zl", "c")
    in_specs = (
        P(section, tensor),
        P(section, None),
        P(section, None),
        P(section, tensor),
        P(),
        P(),
        P(),
    )
    out_specs = (P(section, tensor), P(AXES, None), P(AXES, None))
    return jax.shard_map(local, mesh=mesh, in_specs=in_specs, out_specs=out_specs, check_vma=False)
```

time: 82.1 us -> 58 us (0.71)
  starting transfers between devices: 36.2 us -> 10.9 us
  blocking collectives: 0 us -> 22.7 us
  waiting for transfers between devices: 27.5 us -> 6.51 us
  Pallas kernels: 0 us -> 16.4 us
  other arithmetic: 6.81 us -> 0 us
  matrix products: 6.22 us -> 0 us
  local copies, waits for them, and re-layouts: 2.8 us -> 0.02 us
    ppermute x4 -> x0, starting transfers between devices: 30.4 us -> none  [from_partner(): return lax.ppermute(value, axis, pairs)]
    ppermute x4 -> x0, waiting for transfers between devices: 23.1 us -> none  [from_partner(): return lax.ppermute(value, axis, pairs)]
    all_to_all x0 -> x1, blocking collectives: none -> 22.7 us  [local(): pieces = lax.all_to_all(partial, ('zh', 'x', 'zl', 'c'), 0, 0)]
    pallas_call x0 -> x3, Pallas kernels: none -> 16.4 us  [the longest x1 9.13 us: local(): pl.pallas_call(pick_kernel, out_shape=jax.ShapeDtypeStruct((BLOCKS, 2, bl...]
    dot_general x6 -> x0, matrix products: 6.22 us -> none  [the longest x1 1.84 us: local(): jnp.einsum('tkgd,jkd->kgtj', scaled_blk, whole_values, preferred_element_...]
    all_to_all x1, starting transfers between devices: 5.77 us -> 10.9 us  [local(): kv = lax.all_to_all(picked, ('zh', 'zl'), 0, 0, axis_index_groups=GROUPS)]
    convert_element_type x5 -> x0, other arithmetic: 2.91 us -> none  [the longest x3 1.68 us: local(): partial_value.astype(jnp.bfloat16)]
    reduce_sum x3 -> x0, other arithmetic: 2.28 us -> none  [the longest x1 1.31 us: local(): n_tiles = jnp.sum(jnp.where(picked, tiles, 0))]
  transfers between devices with their start and end apart: 5 -> 1, of which waited for: 4 -> 1; matrix products, arithmetic and copies ran while one was open for 6% -> 0% of each run, Pallas kernels for 0% -> 0%
where the time goes in v1:
time: 58 us; the launch traced here: 57.8 us
  blocking collectives  22.7 us (39%)
  Pallas kernels  16.4 us (28%)
  starting transfers between devices  10.9 us (19%)
  waiting for transfers between devices  6.51 us (11%)
  between operations  1.35 us (2%)
    all_to_all x1, blocking collectives, local(): pieces = lax.all_to_all(partial, ('zh', 'x', 'zl', 'c'), 0, 0)  22.7 us
    all_to_all x1, starting transfers between devices, local(): kv = lax.all_to_all(picked, ('zh', 'zl'), 0, 0, axis_index_groups=GROUPS)  10.9 us
    pallas_call x1, Pallas kernels, local(): pl.pallas_call(pick_kernel, out_shape=jax.ShapeDtypeStruct((BLOCKS, 2, bl...  9.13 us
    all_to_all x1, waiting for transfers between devices, local(): kv = lax.all_to_all(picked, ('zh', 'zl'), 0, 0, axis_index_groups=GROUPS)  6.51 us
    pallas_call x1, Pallas kernels, local(): pl.pallas_call(main_kernel, out_shape=(jax.ShapeDtypeStruct(queries.shape...  5.61 us
    pallas_call x1, Pallas kernels, local(): pl.pallas_call(sum_kernel, out_shape=(jax.ShapeDtypeStruct((8, width), f3...  1.61 us
  transfers between devices with their start and end apart: 1, of which 1 were waited for; matrix products, arithmetic and copies ran while one was open for 0% of the time, Pallas kernels for 0%

profile of v1, /device:TPU:1, one launch (start us, length us, event | category | flops | bytes accessed | tf_op | source)
XLA Modules:
  0.0 57.8 jit_solution(5420863864037164295)
XLA Ops:
  0.6 0.0 copy-start.1
  0.6 0.0 copy-start
  0.7 9.1 %pick.1 = bf16[4,2,128,128]{3,2,1,0:T(8,128)(2,1)} custom-call(bf16[128,1024]{1,0:T(8,128)(2,1)} %keys.1, bf16[128,1024]{1,0:T(8,128)(2,1)} %values.1), custom_call_target="tpu_custom_call" | custom-call | tf_op jit(solution)/shard_map/pick/pallas_call | solution.py:103
  9.8 10.9 %all-to-all-start = ((bf16[4,2,128,128]{3,2,1,0:T(8,128)(2,1)}), bf16[4,2,128,128]{3,2,1,0:T(8,128)(2,1)S(1)}, u32[]{:S(2)}, u32[]{:S(2)}) async-start(bf16[4,2,128,128]{3,2,1,0:T(8,128)(2,1)} %pick.1), calls=%async_computation | async-start | bytes 524288 | tf_op jit(solution)/shard_map/all_to_all | solution.py:111
  20.7 0.0 copy-start.2
  20.7 0.0 copy-start.3
  21.3 6.5 %all-to-all-done.kv = bf16[4,2,128,128]{3,2,1,0:T(8,128)(2,1)S(1)} async-done(((bf16[4,2,128,128]{3,2,1,0:T(8,128)(2,1)}), bf16[4,2,128,128]{3,2,1,0:T(8,128)(2,1)S(1)}, u32[]{:S(2)}, u32[]{:S(2)}) %all-to-all-start) | async-done | bytes 262176 | tf_op jit(solution)/shard_map/all_to_all | solution.py:111
  27.8 0.0 copy-done.1
  27.8 0.0 copy-done
  27.8 0.0 copy-done.2
  27.9 0.0 copy-done.3
  27.9 5.6 %gradients.1 = (bf16[512,512]{1,0:T(8,128)(2,1)}, bf16[64,16,128]{2,1,0:T(8,128)(2,1)S(1)}) custom-call(s32[8]{0:T(128)S(1)} %copy-done.2, s32[8]{0:T(128)S(1)} %copy-done.3, f32[1]{0:T(128)S(6)} %copy.10.gate, bf16[4,2,128,128]{3,2,1,0:T(8,128)(2,1)S(1)} %all-to-all-done.kv, bf16[512,512]{1,0:T(8,128)(2,1)S(1)} %copy-done, bf16[512,512]{1,0:T(8,128)(2,1)S(1)} %copy-done.1), custom_call_target="tpu_custom_call" | custom-call | tf_op jit(solution)/shard_map/gradients/pallas_call | solution.py:113
  33.5 22.7 %all_to_all.10.pieces = bf16[64,16,128]{2,1,0:T(8,128)(2,1)} all-to-all(bf16[64,16,128]{2,1,0:T(8,128)(2,1)S(1)} %get-tuple-element.8), channel_id=1, replica_groups=mesh['y'=8,'zh'=4,'x'=4,'zl'=2,'c'=2] {'zh','x','zl','c'}, dimensions={0} | all-to-all | bytes 524288 | tf_op jit(solution)/shard_map/all_to_all | solution.py:129
  56.2 1.6 %add_up.1 = (f32[8,1024]{1,0:T(8,128)}, f32[8,1024]{1,0:T(8,128)}) custom-call(bf16[64,16,128]{2,1,0:T(8,128)(2,1)} %all_to_all.10.pieces), custom_call_target="tpu_custom_call" | custom-call | tf_op jit(solution)/shard_map/add_up/pallas_call | solution.py:130
Async XLA Ops:
  0.6 27.2 %copy-start.1 = (bf16[512,512]{1,0:T(8,128)(2,1)S(1)}, bf16[512,512]{1,0:T(8,128)(2,1)}, u32[]{:S(2)}) copy-start(bf16[512,512]{1,0:T(8,128)(2,1)} %d_out.1) | copy-start | bytes 1572868
  0.6 27.2 %copy-start = (bf16[512,512]{1,0:T(8,128)(2,1)S(1)}, bf16[512,512]{1,0:T(8,128)(2,1)}, u32[]{:S(2)}) copy-start(bf16[512,512]{1,0:T(8,128)(2,1)} %queries.1) | copy-start | bytes 1572868
  9.8 18.0 %all-to-all-start = ((bf16[4,2,128,128]{3,2,1,0:T(8,128)(2,1)}), bf16[4,2,128,128]{3,2,1,0:T(8,128)(2,1)S(1)}, u32[]{:S(2)}, u32[]{:S(2)}) async-start(bf16[4,2,128,128]{3,2,1,0:T(8,128)(2,1)} %pick.1), calls=%async_computation | async-start | bytes 524288 | tf_op jit(solution)/shard_map/all_to_all | solution.py:111
  20.7 7.2 %copy-start.2 = (s32[8]{0:T(128)S(1)}, s32[8]{0:T(128)}, u32[]{:S(2)}) copy-start(s32[8]{0:T(128)} %tiles.1) | copy-start | bytes 100
  20.7 7.2 %copy-start.3 = (s32[8]{0:T(128)S(1)}, s32[8]{0:T(128)}, u32[]{:S(2)}) copy-start(s32[8]{0:T(128)} %text_len.1) | copy-start | bytes 100

commit v2 on v1

--- a/solution.py
+++ b/solution.py
@@ -45,7 +45,7 @@
     y, zh = lax.axis_index("y"), lax.axis_index("zh")
     n_tiles, n_text = tiles[y], text_len[y]
     rows, heads = queries.shape[0], queries.shape[1] // HD
-    factor = jnp.tanh(jnp.full((8, HD), gate[0], f32))[0:1, 0:1]
+    factor = jnp.tanh(gate[...])
     keys = jnp.concatenate([kv[b, 0] for b in range(BLOCKS)], 0)
     values = jnp.concatenate([kv[b, 1] for b in range(BLOCKS)], 0)
     keys_t[...] = keys.T
@@ -104,7 +104,7 @@
         pick_kernel,
         out_shape=jax.ShapeDtypeStruct((BLOCKS, 2, block, HD), bf16),
         in_specs=[ANY, ANY],
-        out_specs=ANY,
+        out_specs=VMEM,
         scratch_shapes=[pltpu.SemaphoreType.DMA((BLOCKS, 2))],
         name="pick",
     )(keys, values)
@@ -116,7 +116,7 @@
             jax.ShapeDtypeStruct(queries.shape, bf16),
             jax.ShapeDtypeStruct((PLANE, 16, HD), bf16),
         ),
-        in_specs=[SMEM, SMEM, SMEM, VMEM, VMEM, VMEM],
+        in_specs=[SMEM, SMEM, VMEM, VMEM, VMEM, VMEM],
         out_specs=(VMEM, VMEM),
         scratch_shapes=[
             pltpu.VMEM((HD, image), bf16),
@@ -125,7 +125,7 @@
         ],
         compiler_params=pltpu.CompilerParams(vmem_limit_bytes=40 * 2**20),
         name="gradients",
-    )(tiles, text_len, gate, kv, queries, d_out)
+    )(tiles, text_len, gate.reshape(1, 1), kv, queries, d_out)
     pieces = lax.all_to_all(partial, ("zh", "x", "zl", "c"), 0, 0)
     d_keys, d_values = pl.pallas_call(
         sum_kernel,

time: 58 us -> 50.7 us (0.87)
  Pallas kernels: 16.4 us -> 8.97 us
    pallas_call x1, Pallas kernels: 9.13 us -> 1.75 us  [local(): pl.pallas_call(pick_kernel, out_shape=jax.ShapeDtypeStruct((BLOCKS, 2, bl...]
where the time goes in v2:
time: 50.7 us; the launch traced here: 50.4 us
  blocking collectives  22.7 us (45%)
  starting transfers between devices  10.9 us (21%)
  Pallas kernels  8.97 us (18%)
  waiting for transfers between devices  6.51 us (13%)
  between operations  1.34 us (3%)
    all_to_all x1, blocking collectives, local(): pieces = lax.all_to_all(partial, ('zh', 'x', 'zl', 'c'), 0, 0)  22.7 us
    all_to_all x1, starting transfers between devices, local(): kv = lax.all_to_all(picked, ('zh', 'zl'), 0, 0, axis_index_groups=GROUPS)  10.9 us
    all_to_all x1, waiting for transfers between devices, local(): kv = lax.all_to_all(picked, ('zh', 'zl'), 0, 0, axis_index_groups=GROUPS)  6.51 us
    pallas_call x1, Pallas kernels, local(): pl.pallas_call(main_kernel, out_shape=(jax.ShapeDtypeStruct(queries.shape...  5.61 us
    pallas_call x1, Pallas kernels, local(): pl.pallas_call(pick_kernel, out_shape=jax.ShapeDtypeStruct((BLOCKS, 2, bl...  1.75 us
    pallas_call x1, Pallas kernels, local(): pl.pallas_call(sum_kernel, out_shape=(jax.ShapeDtypeStruct((8, width), f3...  1.61 us
  transfers between devices with their start and end apart: 1, of which 1 were waited for; matrix products, arithmetic and copies ran while one was open for 0% of the time, Pallas kernels for 0%

profile of v2, /device:TPU:1, one launch (start us, length us, event | category | flops | bytes accessed | tf_op | source)
XLA Modules:
  0.0 50.4 jit_solution(2190578630708283871)
XLA Ops:
  0.6 0.0 copy-start.1
  0.6 0.0 copy-start
  0.7 1.7 %pick.1 = bf16[4,2,128,128]{3,2,1,0:T(8,128)(2,1)} custom-call(bf16[128,1024]{1,0:T(8,128)(2,1)} %keys.1, bf16[128,1024]{1,0:T(8,128)(2,1)} %values.1), custom_call_target="tpu_custom_call" | custom-call | tf_op jit(solution)/shard_map/pick/pallas_call | solution.py:103
  2.4 10.9 %all-to-all-start = ((bf16[4,2,128,128]{3,2,1,0:T(8,128)(2,1)}), bf16[4,2,128,128]{3,2,1,0:T(8,128)(2,1)S(1)}, u32[]{:S(2)}, u32[]{:S(2)}) async-start(bf16[4,2,128,128]{3,2,1,0:T(8,128)(2,1)} %pick.1), calls=%async_computation | async-start | bytes 524288 | tf_op jit(solution)/shard_map/all_to_all | solution.py:111
  13.9 0.0 copy-start.2
  13.9 0.0 copy-start.3
  13.9 6.5 %all-to-all-done.kv = bf16[4,2,128,128]{3,2,1,0:T(8,128)(2,1)S(1)} async-done(((bf16[4,2,128,128]{3,2,1,0:T(8,128)(2,1)}), bf16[4,2,128,128]{3,2,1,0:T(8,128)(2,1)S(1)}, u32[]{:S(2)}, u32[]{:S(2)}) %all-to-all-start) | async-done | bytes 262176 | tf_op jit(solution)/shard_map/all_to_all | solution.py:111
  20.5 0.0 copy-done.1
  20.5 0.0 copy-done
  20.5 0.0 copy-done.2
  20.5 0.0 copy-done.3
  20.5 5.6 %gradients.1 = (bf16[512,512]{1,0:T(8,128)(2,1)}, bf16[64,16,128]{2,1,0:T(8,128)(2,1)S(1)}) custom-call(s32[8]{0:T(128)S(1)} %copy-done.2, s32[8]{0:T(128)S(1)} %copy-done.3, f32[1,1]{1,0:T(1,128)} %bitcast.1.gate, bf16[4,2,128,128]{3,2,1,0:T(8,128)(2,1)S(1)} %all-to-all-done.kv, bf16[512,512]{1,0:T(8,128)(2,1)S(1)} %copy-done, bf16[512,512]{1,0:T(8,128)(2,1)S(1)} %copy-done.1), custom_call_target="tpu_custom_call" | custom-call | tf_op jit(solution)/shard_map/gradients/pallas_call | solution.py:113
  26.1 22.7 %all_to_all.10.pieces = bf16[64,16,128]{2,1,0:T(8,128)(2,1)} all-to-all(bf16[64,16,128]{2,1,0:T(8,128)(2,1)S(1)} %get-tuple-element.8), channel_id=1, replica_groups=mesh['y'=8,'zh'=4,'x'=4,'zl'=2,'c'=2] {'zh','x','zl','c'}, dimensions={0} | all-to-all | bytes 524288 | tf_op jit(solution)/shard_map/all_to_all | solution.py:129
  48.8 1.6 %add_up.1 = (f32[8,1024]{1,0:T(8,128)}, f32[8,1024]{1,0:T(8,128)}) custom-call(bf16[64,16,128]{2,1,0:T(8,128)(2,1)} %all_to_all.10.pieces), custom_call_target="tpu_custom_call" | custom-call | tf_op jit(solution)/shard_map/add_up/pallas_call | solution.py:130
Async XLA Ops:
  0.6 19.8 %copy-start.1 = (bf16[512,512]{1,0:T(8,128)(2,1)S(1)}, bf16[512,512]{1,0:T(8,128)(2,1)}, u32[]{:S(2)}) copy-start(bf16[512,512]{1,0:T(8,128)(2,1)} %d_out.1) | copy-start | bytes 1572868
  0.6 19.8 %copy-start = (bf16[512,512]{1,0:T(8,128)(2,1)S(1)}, bf16[512,512]{1,0:T(8,128)(2,1)}, u32[]{:S(2)}) copy-start(bf16[512,512]{1,0:T(8,128)(2,1)} %queries.1) | copy-start | bytes 1572868
  2.4 18.0 %all-to-all-start = ((bf16[4,2,128,128]{3,2,1,0:T(8,128)(2,1)}), bf16[4,2,128,128]{3,2,1,0:T(8,128)(2,1)S(1)}, u32[]{:S(2)}, u32[]{:S(2)}) async-start(bf16[4,2,128,128]{3,2,1,0:T(8,128)(2,1)} %pick.1), calls=%async_computation | async-start | bytes 524288 | tf_op jit(solution)/shard_map/all_to_all | solution.py:111
  13.9 6.5 %copy-start.2 = (s32[8]{0:T(128)S(1)}, s32[8]{0:T(128)}, u32[]{:S(2)}) copy-start(s32[8]{0:T(128)} %tiles.1) | copy-start | bytes 100
  13.9 6.5 %copy-start.3 = (s32[8]{0:T(128)S(1)}, s32[8]{0:T(128)}, u32[]{:S(2)}) copy-start(s32[8]{0:T(128)} %text_len.1) | copy-start | bytes 100

commit v3 on v2

v3 whole, which is shorter than its diff:
```python
import jax
import jax.numpy as jnp
from jax import lax
from jax.experimental import pallas as pl
from jax.experimental.pallas import tpu as pltpu
from jax.sharding import Mesh, PartitionSpec as P

HD = 128
TILE = 128
SCALE = HD**-0.5
LOG2E = 1.4426950408889634
AXES = ("y", "zh", "x", "zl", "c")
SIZES = (8, 4, 4, 2, 2)
BLOCKS = 4
HEADS_X = 2
HEADS_STEP = 2
PLANE = 64
GROUPS = ((1, 2, 4, 7), (0, 3, 5, 6))
NT = (((1,), (1,)), ((), ()))
VMEM = pl.BlockSpec(memory_space=pltpu.VMEM)
SMEM = pl.BlockSpec(memory_space=pltpu.SMEM)


def pick_kernel(keys, values, out):
    x, zh, zl = lax.axis_index("x"), lax.axis_index("zh"), lax.axis_index("zl")
    first = [z % 2 for z in GROUPS[0]]
    mine = jnp.where((zh == 0) | (zh == 3), 1, 0)
    flip = jnp.where(mine == zl, 0, 1)
    for k, source in enumerate((keys, values)):
        for lo in range(2):
            head = x * HEADS_X + jnp.where(flip == 0, lo, 1 - lo)
            piece = source[:, pl.ds(pl.multiple_of(head * HD, HD), HD)]
            for j in range(BLOCKS):
                if first[j] == lo:
                    out[j, k] = piece


def main_kernel(tiles, text_len, gate, kv, queries, d_out, d_score, partial, acc_k, acc_v):
    f32, bf16 = jnp.float32, jnp.bfloat16
    y, zh = lax.axis_index("y"), lax.axis_index("zh")
    n_tiles, n_text = tiles[y], text_len[y]
    rows, heads = queries.shape[0], queries.shape[1] // HD
    steps = heads // HEADS_STEP
    factor = jnp.tanh(gate[...])
    keys = jnp.concatenate([kv[b, 0] for b in range(BLOCKS)], 0)
    values = jnp.concatenate([kv[b, 1] for b in range(BLOCKS)], 0)
    live = lax.broadcasted_iota(jnp.int32, (rows, HD), 0) + zh * rows < n_text

    def products(step):
        q, s = [], []
        for h in range(step * HEADS_STEP, (step + 1) * HEADS_STEP):
            cols = pl.ds(h * HD, HD)
            q.append(queries[:, cols])
            s.append(jnp.where(live, factor * d_out[:, cols].astype(f32), 0.0).astype(bf16))
        q, s = jnp.concatenate(q, 0), jnp.concatenate(s, 0)
        score = lax.dot_general(keys, q, NT, preferred_element_type=f32)
        d_prob = lax.dot_general(values, s, NT, preferred_element_type=f32)
        return q, s, score, d_prob

    ahead = products(0)
    for step in range(steps):
        q, s, score, d_prob = ahead
        if step < steps - 1:
            ahead = products(step + 1)
        blocks = [score[b * TILE : (b + 1) * TILE] for b in range(BLOCKS)]
        top = jnp.max(blocks[0], axis=0, keepdims=True)
        for b in range(1, BLOCKS):
            top = jnp.maximum(
                top, jnp.where(b < n_tiles, jnp.max(blocks[b], axis=0, keepdims=True), -3e38)
            )
        expo = []
        for b in range(BLOCKS):
            shift = top if b == 0 else jnp.where(b < n_tiles, top, 1e30)
            expo.append(jnp.exp2((blocks[b] - shift) * (SCALE * LOG2E)))
        expo = jnp.concatenate(expo, 0)
        inverse = 1.0 / jnp.sum(expo, axis=0, keepdims=True)
        delta = jnp.sum(expo * d_prob, axis=0, keepdims=True) * inverse
        prob = (expo * inverse).astype(bf16)
        d_s = prob * (d_prob - delta).astype(bf16)
        d_score[step] = d_s
        term_k = jnp.dot(d_s, q, preferred_element_type=f32)
        term_v = jnp.dot(prob, s, preferred_element_type=f32)
        if step == 0:
            acc_k[...] = term_k
            acc_v[...] = term_v
        else:
            acc_k[...] += term_k
            acc_v[...] += term_v
    both = [acc.reshape(PLANE, 8, HD) for acc in (acc_k[...] * SCALE, acc_v[...])]
    partial[...] = jnp.concatenate(both, 1).astype(bf16)


def query_kernel(kv, d_score, d_queries):
    keys = jnp.concatenate([kv[b, 0] for b in range(BLOCKS)], 0)
    keys_t = keys.T
    rows = d_queries.shape[0]
    for step in range(d_score.shape[0]):
        d_q = jnp.dot(keys_t, d_score[step], preferred_element_type=jnp.float32)
        d_q = (d_q * SCALE).T.astype(jnp.bfloat16)
        for i in range(HEADS_STEP):
            cols = pl.ds((step * HEADS_STEP + i) * HD, HD)
            d_queries[:, cols] = d_q[i * rows : (i + 1) * rows]


def sum_kernel(pieces, d_keys, d_values):
    _, zhs, xs, zls, cs = SIZES
    for head in range(xs * zls):
        total = None
        for zh in range(zhs):
            for c in range(cs):
                piece = pieces[(zh * xs * zls + head) * cs + c].astype(jnp.float32)
                total = piece if total is None else total + piece
        cols = pl.ds(head * HD, HD)
        d_keys[:, cols] = total[:8]
        d_values[:, cols] = total[8:]


def local(queries, keys, values, d_out, gate, tiles, text_len):
    f32, bf16 = jnp.float32, jnp.bfloat16
    block, width = keys.shape
    picked = pl.pallas_call(
        pick_kernel,
        out_shape=jax.ShapeDtypeStruct((BLOCKS, 2, block, HD), bf16),
        in_specs=[VMEM, VMEM],
        out_specs=VMEM,
        name="pick",
    )(keys, values)
    kv = lax.all_to_all(picked, ("zh", "zl"), 0, 0, axis_index_groups=GROUPS)
    image = BLOCKS * block
    rows, width_q = queries.shape
    steps = width_q // HD // HEADS_STEP
    d_score, partial = pl.pallas_call(
        main_kernel,
        out_shape=(
            jax.ShapeDtypeStruct((steps, image, rows * HEADS_STEP), bf16),
            jax.ShapeDtypeStruct((PLANE, 16, HD), bf16),
        ),
        in_specs=[SMEM, SMEM, VMEM, VMEM, VMEM, VMEM],
        out_specs=(VMEM, VMEM),
        scratch_shapes=[pltpu.VMEM((image, HD), f32), pltpu.VMEM((image, HD), f32)],
        compiler_params=pltpu.CompilerParams(vmem_limit_bytes=40 * 2**20),
        name="gradients",
    )(tiles, text_len, gate.reshape(1, 1), kv, queries, d_out)
    pieces = lax.all_to_all(partial, ("zh", "x", "zl", "c"), 0, 0)
    d_queries = pl.pallas_call(
        query_kernel,
        out_shape=jax.ShapeDtypeStruct(queries.shape, bf16),
        in_specs=[VMEM, VMEM],
        out_specs=VMEM,
        compiler_params=pltpu.CompilerParams(vmem_limit_bytes=16 * 2**20),
        cost_estimate=pl.CostEstimate(
            flops=2 * rows * width_q * image, bytes_accessed=4 * rows * width_q, transcendentals=0
        ),
        name="query_gradient",
    )(kv, d_score)
    d_keys, d_values = pl.pallas_call(
        sum_kernel,
        out_shape=(jax.ShapeDtypeStruct((8, width), f32),) * 2,
        in_specs=[VMEM],
        out_specs=(VMEM, VMEM),
        name="add_up",
    )(pieces)
    return d_queries, d_keys, d_values


def solution(mesh):
    mesh = Mesh(mesh.devices.reshape(SIZES), AXES)
    section, tensor = ("y", "zh"), ("x", "zl", "c")
    in_specs = (
        P(section, tensor),
        P(section, None),
        P(section, None),
        P(section, tensor),
        P(),
        P(),
        P(),
    )
    out_specs = (P(section, tensor), P(AXES, None), P(AXES, None))
    return jax.shard_map(local, mesh=mesh, in_specs=in_specs, out_specs=out_specs, check_vma=False)
```

time: 50.7 us -> 53.7 us (1.059)
  blocking collectives: 22.7 us -> 0 us
  waiting for transfers between devices: 6.51 us -> 17.5 us
  starting transfers between devices: 10.9 us -> 21.3 us
  local copies, waits for them, and re-layouts: 0.02 us -> 4.1 us
    all_to_all x1 -> x0, blocking collectives: 22.7 us -> none  [local(): pieces = lax.all_to_all(partial, ('zh', 'x', 'zl', 'c'), 0, 0)]
    all_to_all x0 -> x1, waiting for transfers between devices: none -> 11 us  [local(): pieces = lax.all_to_all(partial, ('zh', 'x', 'zl', 'c'), 0, 0)]
    all_to_all x0 -> x1, starting transfers between devices: none -> 10.5 us  [local(): pieces = lax.all_to_all(partial, ('zh', 'x', 'zl', 'c'), 0, 0)]
    unnamed x8 -> x10, local copies, waits for them, and re-layouts: 0.02 us -> 4.1 us
    pallas_call x1 -> x2, Pallas kernels: 5.61 us -> 5.6 us  [the longest x1 4.26 us: local(): pl.pallas_call(main_kernel, out_shape=(jax.ShapeDtypeStruct((steps, image...]
  transfers between devices with their start and end apart: 1 -> 2, of which waited for: 1 -> 2; matrix products, arithmetic and copies ran while one was open for 0% -> 0% of each run, Pallas kernels for 0% -> 3%
where the time goes in v3:
time: 53.7 us; the launch traced here: 53.2 us
  starting transfers between devices  21.3 us (40%)
  waiting for transfers between devices  17.5 us (33%)
  Pallas kernels  8.98 us (17%)
  local copies, waits for them, and re-layouts  4.1 us (8%)
  between operations  1.3 us (2%)
    all_to_all x1, waiting for transfers between devices, local(): pieces = lax.all_to_all(partial, ('zh', 'x', 'zl', 'c'), 0, 0)  11 us
    all_to_all x1, starting transfers between devices, local(): kv = lax.all_to_all(picked, ('zh', 'zl'), 0, 0, axis_index_groups=GROUPS)  10.8 us
    all_to_all x1, starting transfers between devices, local(): pieces = lax.all_to_all(partial, ('zh', 'x', 'zl', 'c'), 0, 0)  10.5 us
    all_to_all x1, waiting for transfers between devices, local(): kv = lax.all_to_all(picked, ('zh', 'zl'), 0, 0, axis_index_groups=GROUPS)  6.54 us
    pallas_call x1, Pallas kernels, local(): pl.pallas_call(main_kernel, out_shape=(jax.ShapeDtypeStruct((steps, image...  4.26 us
    unnamed x10, local copies, waits for them, and re-layouts  4.1 us
    pallas_call x1, Pallas kernels, local(): pl.pallas_call(pick_kernel, out_shape=jax.ShapeDtypeStruct((BLOCKS, 2, bl...  1.77 us
    pallas_call x1, Pallas kernels, local(): pl.pallas_call(sum_kernel, out_shape=(jax.ShapeDtypeStruct((8, width), f3...  1.61 us
  transfers between devices with their start and end apart: 2, of which 2 were waited for; matrix products, arithmetic and copies ran while one was open for 0% of the time, Pallas kernels for 3%

profile of v3, /device:TPU:1, one launch (start us, length us, event | category | flops | bytes accessed | tf_op | source)
XLA Modules:
  0.0 53.2 jit_solution(4337458662378192421)
XLA Ops:
  0.6 1.8 %pick.1 = bf16[4,2,128,128]{3,2,1,0:T(8,128)(2,1)} custom-call(bf16[128,1024]{1,0:T(8,128)(2,1)} %keys.1, bf16[128,1024]{1,0:T(8,128)(2,1)} %values.1), custom_call_target="tpu_custom_call" | custom-call | tf_op jit(solution)/shard_map/pick/pallas_call | solution.py:121
  2.4 10.8 %all-to-all-start = ((bf16[4,2,128,128]{3,2,1,0:T(8,128)(2,1)}), bf16[4,2,128,128]{3,2,1,0:T(8,128)(2,1)S(1)}, u32[]{:S(2)}, u32[]{:S(2)}) async-start(bf16[4,2,128,128]{3,2,1,0:T(8,128)(2,1)} %pick.1), calls=%async_computation | async-start | bytes 524288 | tf_op jit(solution)/shard_map/all_to_all | solution.py:128
  13.9 6.5 %all-to-all-done.kv = bf16[4,2,128,128]{3,2,1,0:T(8,128)(2,1)S(1)} async-done(((bf16[4,2,128,128]{3,2,1,0:T(8,128)(2,1)}), bf16[4,2,128,128]{3,2,1,0:T(8,128)(2,1)S(1)}, u32[]{:S(2)}, u32[]{:S(2)}) %all-to-all-start) | async-done | bytes 262176 | tf_op jit(solution)/shard_map/all_to_all | solution.py:128
  20.4 0.0 copy-start
  20.4 1.0 %copy-done = bf16[512,512]{1,0:T(8,128)(2,1)S(1)} copy-done((bf16[512,512]{1,0:T(8,128)(2,1)S(1)}, bf16[512,512]{1,0:T(8,128)(2,1)}, u32[]{:S(2)}) %copy-start) | copy-done | bytes 524312
  21.5 0.0 copy-start.1
  21.5 1.0 %copy-done.1 = bf16[512,512]{1,0:T(8,128)(2,1)S(1)} copy-done((bf16[512,512]{1,0:T(8,128)(2,1)S(1)}, bf16[512,512]{1,0:T(8,128)(2,1)}, u32[]{:S(2)}) %copy-start.1) | copy-done | bytes 524312
  22.5 0.0 copy-start.2
  22.5 0.7 %copy-done.2 = s32[8]{0:T(128)S(1)} copy-done((s32[8]{0:T(128)S(1)}, s32[8]{0:T(128)}, u32[]{:S(2)}) %copy-start.2) | copy-done | bytes 56
  23.2 0.0 copy-start.3
  23.2 0.7 %copy-done.3 = s32[8]{0:T(128)S(1)} copy-done((s32[8]{0:T(128)S(1)}, s32[8]{0:T(128)}, u32[]{:S(2)}) %copy-start.3) | copy-done | bytes 56
  23.8 4.3 %gradients.1 = (bf16[2,512,1024]{2,1,0:T(8,128)(2,1)S(1)}, bf16[64,16,128]{2,1,0:T(8,128)(2,1)}) custom-call(s32[8]{0:T(128)S(1)} %copy-done.2, s32[8]{0:T(128)S(1)} %copy-done.3, f32[1,1]{1,0:T(1,128)} %bitcast.1.gate, bf16[4,2,128,128]{3,2,1,0:T(8,128)(2,1)S(1)} %all-to-all-done.kv, bf16[512,512]{1,0:T(8,128)(2,1)S(1)} %copy-done, ...), custom_call_target="tpu_custom_call" | custom-call | tf_op jit(solution)/shard_map/gradients/pallas_call | solution.py:132
  28.1 10.5 %all-to-all-start.1 = ((bf16[64,16,128]{2,1,0:T(8,128)(2,1)}), bf16[64,16,128]{2,1,0:T(8,128)(2,1)S(1)}, u32[]{:S(2)}, u32[]{:S(2)}) async-start(bf16[64,16,128]{2,1,0:T(8,128)(2,1)} %get-tuple-element.8), calls=%async_computation.1 | async-start | bytes 524288 | tf_op jit(solution)/shard_map/all_to_all | solution.py:144
  38.6 1.3 %query_gradient.1 = bf16[512,512]{1,0:T(8,128)(2,1)} custom-call(bf16[4,2,128,128]{3,2,1,0:T(8,128)(2,1)S(1)} %all-to-all-done.kv, bf16[2,512,1024]{2,1,0:T(8,128)(2,1)S(1)} %get-tuple-element.7.d_score), custom_call_target="tpu_custom_call" | custom-call | flops 268435456 | bytes 1048576 | tf_op jit(solution)/shard_map/query_gradient/pallas_call | solution.py:145
  39.9 11.0 %all-to-all-done.1.pieces = bf16[64,16,128]{2,1,0:T(8,128)(2,1)S(1)} async-done(((bf16[64,16,128]{2,1,0:T(8,128)(2,1)}), bf16[64,16,128]{2,1,0:T(8,128)(2,1)S(1)}, u32[]{:S(2)}, u32[]{:S(2)}) %all-to-all-start.1) | async-done | bytes 262176 | tf_op jit(solution)/shard_map/all_to_all | solution.py:144
  50.9 0.0 copy-start.4
  50.9 0.7 %copy-done.4 = bf16[64,16,128]{2,1,0:T(8,128)(2,1)} copy-done((bf16[64,16,128]{2,1,0:T(8,128)(2,1)}, bf16[64,16,128]{2,1,0:T(8,128)(2,1)S(1)}, u32[]{:S(2)}) %copy-start.4) | copy-done | bytes 262168
  51.6 1.6 %add_up.1 = (f32[8,1024]{1,0:T(8,128)}, f32[8,1024]{1,0:T(8,128)}) custom-call(bf16[64,16,128]{2,1,0:T(8,128)(2,1)} %copy-done.4), custom_call_target="tpu_custom_call" | custom-call | tf_op jit(solution)/shard_map/add_up/pallas_call | solution.py:156
Async XLA Ops:
  2.4 18.0 %all-to-all-start = ((bf16[4,2,128,128]{3,2,1,0:T(8,128)(2,1)}), bf16[4,2,128,128]{3,2,1,0:T(8,128)(2,1)S(1)}, u32[]{:S(2)}, u32[]{:S(2)}) async-start(bf16[4,2,128,128]{3,2,1,0:T(8,128)(2,1)} %pick.1), calls=%async_computation | async-start | bytes 524288 | tf_op jit(solution)/shard_map/all_to_all | solution.py:128
  20.4 1.0 %copy-start = (bf16[512,512]{1,0:T(8,128)(2,1)S(1)}, bf16[512,512]{1,0:T(8,128)(2,1)}, u32[]{:S(2)}) copy-start(bf16[512,512]{1,0:T(8,128)(2,1)} %queries.1) | copy-start | bytes 1572868
  21.5 1.0 %copy-start.1 = (bf16[512,512]{1,0:T(8,128)(2,1)S(1)}, bf16[512,512]{1,0:T(8,128)(2,1)}, u32[]{:S(2)}) copy-start(bf16[512,512]{1,0:T(8,128)(2,1)} %d_out.1) | copy-start | bytes 1572868
  22.5 0.7 %copy-start.2 = (s32[8]{0:T(128)S(1)}, s32[8]{0:T(128)}, u32[]{:S(2)}) copy-start(s32[8]{0:T(128)} %tiles.1) | copy-start | bytes 100
  23.2 0.7 %copy-start.3 = (s32[8]{0:T(128)S(1)}, s32[8]{0:T(128)}, u32[]{:S(2)}) copy-start(s32[8]{0:T(128)} %text_len.1) | copy-start | bytes 100
  28.1 22.8 %all-to-all-start.1 = ((bf16[64,16,128]{2,1,0:T(8,128)(2,1)}), bf16[64,16,128]{2,1,0:T(8,128)(2,1)S(1)}, u32[]{:S(2)}, u32[]{:S(2)}) async-start(bf16[64,16,128]{2,1,0:T(8,128)(2,1)} %get-tuple-element.8), calls=%async_computation.1 | async-start | bytes 524288 | tf_op jit(solution)/shard_map/all_to_all | solution.py:144
  50.9 0.7 %copy-start.4 = (bf16[64,16,128]{2,1,0:T(8,128)(2,1)}, bf16[64,16,128]{2,1,0:T(8,128)(2,1)S(1)}, u32[]{:S(2)}) copy-start(bf16[64,16,128]{2,1,0:T(8,128)(2,1)S(1)} %all-to-all-done.1.pieces) | copy-start | bytes 786436

commit v4 on v3

--- a/solution.py
+++ b/solution.py
@@ -18,7 +18,6 @@
 GROUPS = ((1, 2, 4, 7), (0, 3, 5, 6))
 NT = (((1,), (1,)), ((), ()))
 VMEM = pl.BlockSpec(memory_space=pltpu.VMEM)
-SMEM = pl.BlockSpec(memory_space=pltpu.SMEM)
 
 
 def pick_kernel(keys, values, out):
@@ -35,24 +34,32 @@
                     out[j, k] = piece
 
 
-def main_kernel(tiles, text_len, gate, kv, queries, d_out, d_score, partial, acc_k, acc_v):
+def prepare_kernel(tiles, text_len, gate, queries, d_out, q_out, s_out, live_tiles):
     f32, bf16 = jnp.float32, jnp.bfloat16
     y, zh = lax.axis_index("y"), lax.axis_index("zh")
-    n_tiles, n_text = tiles[y], text_len[y]
+    picked = lax.broadcasted_iota(jnp.int32, tiles.shape, 1) == y
+    n_tiles = jnp.sum(jnp.where(picked, tiles[...], 0), axis=1, keepdims=True)
+    n_text = jnp.sum(jnp.where(picked, text_len[...], 0), axis=1, keepdims=True)
+    live_tiles[...] = jnp.broadcast_to(n_tiles, live_tiles.shape)
     rows, heads = queries.shape[0], queries.shape[1] // HD
-    steps = heads // HEADS_STEP
     factor = jnp.tanh(gate[...])
+    live = lax.broadcasted_iota(jnp.int32, (rows, HD), 0) + zh * rows < n_text
+    for h in range(heads):
+        cols = pl.ds(h * HD, HD)
+        step, place = h // HEADS_STEP, pl.ds(h % HEADS_STEP * rows, rows)
+        q_out[step, place] = queries[:, cols]
+        s_out[step, place] = jnp.where(live, factor * d_out[:, cols].astype(f32), 0.0).astype(bf16)
+
+
+def main_kernel(live_tiles, kv, queries, scaled, d_score, partial, acc_k, acc_v):
+    f32, bf16 = jnp.float32, jnp.bfloat16
+    n_tiles = live_tiles[0:1, 0:1]
+    steps = queries.shape[0]
     keys = jnp.concatenate([kv[b, 0] for b in range(BLOCKS)], 0)
     values = jnp.concatenate([kv[b, 1] for b in range(BLOCKS)], 0)
-    live = lax.broadcasted_iota(jnp.int32, (rows, HD), 0) + zh * rows < n_text
 
     def products(step):
-        q, s = [], []
-        for h in range(step * HEADS_STEP, (step + 1) * HEADS_STEP):
-            cols = pl.ds(h * HD, HD)
-            q.append(queries[:, cols])
-            s.append(jnp.where(live, factor * d_out[:, cols].astype(f32), 0.0).astype(bf16))
-        q, s = jnp.concatenate(q, 0), jnp.concatenate(s, 0)
+        q, s = queries[step], scaled[step]
         score = lax.dot_general(keys, q, NT, preferred_element_type=f32)
         d_prob = lax.dot_general(values, s, NT, preferred_element_type=f32)
         return q, s, score, d_prob
@@ -115,32 +122,52 @@
         d_values[:, cols] = total[8:]
 
 
+def in_vmem(array):
+    return pltpu.with_memory_space_constraint(array, pltpu.VMEM)
+
+
 def local(queries, keys, values, d_out, gate, tiles, text_len):
     f32, bf16 = jnp.float32, jnp.bfloat16
     block, width = keys.shape
+    rows, width_q = queries.shape
+    steps = width_q // HD // HEADS_STEP
+    image = BLOCKS * block
     picked = pl.pallas_call(
         pick_kernel,
-        out_shape=jax.ShapeDtypeStruct((BLOCKS, 2, block, HD), bf16),
+        out_shape=pltpu.VMEM((BLOCKS, 2, block, HD), bf16),
         in_specs=[VMEM, VMEM],
         out_specs=VMEM,
         name="pick",
     )(keys, values)
-    kv = lax.all_to_all(picked, ("zh", "zl"), 0, 0, axis_index_groups=GROUPS)
-    image = BLOCKS * block
-    rows, width_q = queries.shape
-    steps = width_q // HD // HEADS_STEP
+    kv = in_vmem(lax.all_to_all(picked, ("zh", "zl"), 0, 0, axis_index_groups=GROUPS))
+    by_step = (steps, rows * HEADS_STEP, HD)
+    q, scaled, live_tiles = pl.pallas_call(
+        prepare_kernel,
+        out_shape=(
+            pltpu.VMEM(by_step, bf16),
+            pltpu.VMEM(by_step, bf16),
+            pltpu.VMEM((8, HD), jnp.int32),
+        ),
+        in_specs=[VMEM] * 5,
+        out_specs=(VMEM,) * 3,
+        compiler_params=pltpu.CompilerParams(vmem_limit_bytes=16 * 2**20),
+        cost_estimate=pl.CostEstimate(
+            flops=4 * rows * width_q, bytes_accessed=8 * rows * width_q, transcendentals=0
+        ),
+        name="prepare",
+    )(tiles.reshape(1, -1), text_len.reshape(1, -1), gate.reshape(1, 1), queries, d_out)
     d_score, partial = pl.pallas_call(
         main_kernel,
         out_shape=(
-            jax.ShapeDtypeStruct((steps, image, rows * HEADS_STEP), bf16),
-            jax.ShapeDtypeStruct((PLANE, 16, HD), bf16),
-        ),
-        in_specs=[SMEM, SMEM, VMEM, VMEM, VMEM, VMEM],
+            pltpu.VMEM((steps, image, rows * HEADS_STEP), bf16),
+            pltpu.VMEM((PLANE, 16, HD), bf16),
+        ),
+        in_specs=[VMEM] * 4,
         out_specs=(VMEM, VMEM),
         scratch_shapes=[pltpu.VMEM((image, HD), f32), pltpu.VMEM((image, HD), f32)],
         compiler_params=pltpu.CompilerParams(vmem_limit_bytes=40 * 2**20),
         name="gradients",
-    )(tiles, text_len, gate.reshape(1, 1), kv, queries, d_out)
+    )(in_vmem(live_tiles), kv, in_vmem(q), in_vmem(scaled))
     pieces = lax.all_to_all(partial, ("zh", "x", "zl", "c"), 0, 0)
     d_queries = pl.pallas_call(
         query_kernel,
@@ -152,14 +179,14 @@
             flops=2 * rows * width_q * image, bytes_accessed=4 * rows * width_q, transcendentals=0
         ),
         name="query_gradient",
-    )(kv, d_score)
+    )(kv, in_vmem(d_score))
     d_keys, d_values = pl.pallas_call(
         sum_kernel,
         out_shape=(jax.ShapeDtypeStruct((8, width), f32),) * 2,
         in_specs=[VMEM],
         out_specs=(VMEM, VMEM),
         name="add_up",
-    )(pieces)
+    )(in_vmem(pieces))
     return d_queries, d_keys, d_values
 
 

time: 53.7 us -> 48 us (0.89)
  waiting for transfers between devices: 17.5 us -> 13.8 us
  Pallas kernels: 8.98 us -> 7.02 us
    all_to_all x1, waiting for transfers between devices: 6.54 us -> 2.84 us  [local(): lax.all_to_all(picked, ('zh', 'zl'), 0, 0, axis_index_groups=GROUPS)]
    pallas_call x2 -> x3, Pallas kernels: 6.03 us -> 5.03 us  [the longest x1 2.96 us: local(): pl.pallas_call(main_kernel, out_shape=(pltpu.VMEM((steps, image, rows * H...]
    pallas_call x1, Pallas kernels: 1.61 us -> 0.66 us  [local(): pl.pallas_call(sum_kernel, out_shape=(jax.ShapeDtypeStruct((8, width), f3...]
where the time goes in v4:
time: 48 us; the launch traced here: 47.6 us
  starting transfers between devices  21.4 us (45%)
  waiting for transfers between devices  13.8 us (29%)
  Pallas kernels  7.02 us (15%)
  local copies, waits for them, and re-layouts  4.09 us (9%)
  between operations  1.32 us (3%)
    all_to_all x1, waiting for transfers between devices, local(): pieces = lax.all_to_all(partial, ('zh', 'x', 'zl', 'c'), 0, 0)  11 us
    all_to_all x1, starting transfers between devices, local(): lax.all_to_all(picked, ('zh', 'zl'), 0, 0, axis_index_groups=GROUPS)  10.8 us
    all_to_all x1, starting transfers between devices, local(): pieces = lax.all_to_all(partial, ('zh', 'x', 'zl', 'c'), 0, 0)  10.5 us
    unnamed x10, local copies, waits for them, and re-layouts  4.09 us
    pallas_call x1, Pallas kernels, local(): pl.pallas_call(main_kernel, out_shape=(pltpu.VMEM((steps, image, rows * H...  2.96 us
    all_to_all x1, waiting for transfers between devices, local(): lax.all_to_all(picked, ('zh', 'zl'), 0, 0, axis_index_groups=GROUPS)  2.84 us
    pallas_call x1, Pallas kernels, local(): pl.pallas_call(pick_kernel, out_shape=pltpu.VMEM((BLOCKS, 2, block, HD),...  1.77 us
    pallas_call x1, Pallas kernels, local(): pl.pallas_call(query_kernel, out_shape=jax.ShapeDtypeStruct(queries.shape...  1.34 us
  transfers between devices with their start and end apart: 2, of which 2 were waited for; matrix products, arithmetic and copies ran while one was open for 0% of the time, Pallas kernels for 3%

profile of v4, /device:TPU:1, one launch (start us, length us, event | category | flops | bytes accessed | tf_op | source)
XLA Modules:
  0.0 47.6 jit_solution(13094702417049378215)
XLA Ops:
  0.6 1.8 %pick.1 = bf16[4,2,128,128]{3,2,1,0:T(8,128)(2,1)} custom-call(bf16[128,1024]{1,0:T(8,128)(2,1)} %keys.1, bf16[128,1024]{1,0:T(8,128)(2,1)} %values.1), custom_call_target="tpu_custom_call" | custom-call | tf_op jit(solution)/shard_map/pick/pallas_call | solution.py:135
  2.4 10.8 %all-to-all-start = ((bf16[4,2,128,128]{3,2,1,0:T(8,128)(2,1)}), bf16[4,2,128,128]{3,2,1,0:T(8,128)(2,1)S(1)}, u32[]{:S(2)}, u32[]{:S(2)}) async-start(bf16[4,2,128,128]{3,2,1,0:T(8,128)(2,1)} %pick.1), calls=%async_computation | async-start | bytes 524288 | tf_op jit(solution)/shard_map/all_to_all | solution.py:142
  13.9 0.0 copy-start
  13.9 1.0 %copy-done = bf16[512,512]{1,0:T(8,128)(2,1)S(1)} copy-done((bf16[512,512]{1,0:T(8,128)(2,1)S(1)}, bf16[512,512]{1,0:T(8,128)(2,1)}, u32[]{:S(2)}) %copy-start) | copy-done | bytes 524312
  14.9 0.0 copy-start.1
  14.9 1.0 %copy-done.1 = bf16[512,512]{1,0:T(8,128)(2,1)S(1)} copy-done((bf16[512,512]{1,0:T(8,128)(2,1)S(1)}, bf16[512,512]{1,0:T(8,128)(2,1)}, u32[]{:S(2)}) %copy-start.1) | copy-done | bytes 524312
  16.0 0.0 copy-start.3
  16.0 0.7 %copy-done.3 = s32[8]{0:T(128)S(1)} copy-done((s32[8]{0:T(128)S(1)}, s32[8]{0:T(128)}, u32[]{:S(2)}) %copy-start.3) | copy-done | bytes 56
  16.6 0.0 copy-start.4
  16.6 0.7 %copy-done.4 = s32[8]{0:T(128)S(1)} copy-done((s32[8]{0:T(128)S(1)}, s32[8]{0:T(128)}, u32[]{:S(2)}) %copy-start.4) | copy-done | bytes 56
  17.3 0.3 prepare.1
  17.6 2.8 %all-to-all-done.kv = bf16[4,2,128,128]{3,2,1,0:T(8,128)(2,1)S(1)} async-done(((bf16[4,2,128,128]{3,2,1,0:T(8,128)(2,1)}), bf16[4,2,128,128]{3,2,1,0:T(8,128)(2,1)S(1)}, u32[]{:S(2)}, u32[]{:S(2)}) %all-to-all-start) | async-done | bytes 262176 | tf_op jit(solution)/shard_map/all_to_all | solution.py:142
  20.4 3.0 %gradients.1 = (bf16[2,512,1024]{2,1,0:T(8,128)(2,1)S(1)}, bf16[64,16,128]{2,1,0:T(8,128)(2,1)S(1)}) custom-call(s32[8,128]{1,0:T(8,128)S(1)} %get-tuple-element.10.live_tiles, bf16[4,2,128,128]{3,2,1,0:T(8,128)(2,1)S(1)} %all-to-all-done.kv, bf16[2,1024,128]{2,1,0:T(8,128)(2,1)S(1)} %get-tuple-element.11.queries, ...), custom_call_target="tpu_custom_call" | custom-call | tf_op jit(solution)/shard_map/gradients/pallas_call | solution.py:159
  23.4 0.0 copy-start.2
  23.4 0.7 %copy-done.2 = bf16[64,16,128]{2,1,0:T(8,128)(2,1)} copy-done((bf16[64,16,128]{2,1,0:T(8,128)(2,1)}, bf16[64,16,128]{2,1,0:T(8,128)(2,1)S(1)}, u32[]{:S(2)}) %copy-start.2) | copy-done | bytes 262168
  24.1 10.5 %all-to-all-start.1 = ((bf16[64,16,128]{2,1,0:T(8,128)(2,1)}), bf16[64,16,128]{2,1,0:T(8,128)(2,1)S(1)}, u32[]{:S(2)}, u32[]{:S(2)}) async-start(bf16[64,16,128]{2,1,0:T(8,128)(2,1)} %copy-done.2), calls=%async_computation.1 | async-start | bytes 524288 | tf_op jit(solution)/shard_map/all_to_all | solution.py:171
  34.6 1.3 %query_gradient.1 = bf16[512,512]{1,0:T(8,128)(2,1)} custom-call(bf16[4,2,128,128]{3,2,1,0:T(8,128)(2,1)S(1)} %all-to-all-done.kv, bf16[2,512,1024]{2,1,0:T(8,128)(2,1)S(1)} %get-tuple-element.13.d_score), custom_call_target="tpu_custom_call" | custom-call | flops 268435456 | bytes 1048576 | tf_op jit(solution)/shard_map/query_gradient/pallas_call | solution.py:172
  36.0 11.0 %all-to-all-done.1.pieces = bf16[64,16,128]{2,1,0:T(8,128)(2,1)S(1)} async-done(((bf16[64,16,128]{2,1,0:T(8,128)(2,1)}), bf16[64,16,128]{2,1,0:T(8,128)(2,1)S(1)}, u32[]{:S(2)}, u32[]{:S(2)}) %all-to-all-start.1) | async-done | bytes 262176 | tf_op jit(solution)/shard_map/all_to_all | solution.py:171
  46.9 0.7 %add_up.1 = (f32[8,1024]{1,0:T(8,128)}, f32[8,1024]{1,0:T(8,128)}) custom-call(bf16[64,16,128]{2,1,0:T(8,128)(2,1)S(1)} %all-to-all-done.1.pieces), custom_call_target="tpu_custom_call" | custom-call | tf_op jit(solution)/shard_map/add_up/pallas_call | solution.py:183
Async XLA Ops:
  2.4 18.0 %all-to-all-start = ((bf16[4,2,128,128]{3,2,1,0:T(8,128)(2,1)}), bf16[4,2,128,128]{3,2,1,0:T(8,128)(2,1)S(1)}, u32[]{:S(2)}, u32[]{:S(2)}) async-start(bf16[4,2,128,128]{3,2,1,0:T(8,128)(2,1)} %pick.1), calls=%async_computation | async-start | bytes 524288 | tf_op jit(solution)/shard_map/all_to_all | solution.py:142
  13.9 1.0 %copy-start = (bf16[512,512]{1,0:T(8,128)(2,1)S(1)}, bf16[512,512]{1,0:T(8,128)(2,1)}, u32[]{:S(2)}) copy-start(bf16[512,512]{1,0:T(8,128)(2,1)} %queries.1) | copy-start | bytes 1572868
  14.9 1.0 %copy-start.1 = (bf16[512,512]{1,0:T(8,128)(2,1)S(1)}, bf16[512,512]{1,0:T(8,128)(2,1)}, u32[]{:S(2)}) copy-start(bf16[512,512]{1,0:T(8,128)(2,1)} %d_out.1) | copy-start | bytes 1572868
  16.0 0.7 %copy-start.3 = (s32[8]{0:T(128)S(1)}, s32[8]{0:T(128)}, u32[]{:S(2)}) copy-start(s32[8]{0:T(128)} %param.12) | copy-start | bytes 100
  16.6 0.7 %copy-start.4 = (s32[8]{0:T(128)S(1)}, s32[8]{0:T(128)}, u32[]{:S(2)}) copy-start(s32[8]{0:T(128)} %param.13) | copy-start | bytes 100
  23.4 0.7 %copy-start.2 = (bf16[64,16,128]{2,1,0:T(8,128)(2,1)}, bf16[64,16,128]{2,1,0:T(8,128)(2,1)S(1)}, u32[]{:S(2)}) copy-start(bf16[64,16,128]{2,1,0:T(8,128)(2,1)S(1)} %get-tuple-element.14) | copy-start | bytes 786436
  24.1 22.8 %all-to-all-start.1 = ((bf16[64,16,128]{2,1,0:T(8,128)(2,1)}), bf16[64,16,128]{2,1,0:T(8,128)(2,1)S(1)}, u32[]{:S(2)}, u32[]{:S(2)}) async-start(bf16[64,16,128]{2,1,0:T(8,128)(2,1)} %copy-done.2), calls=%async_computation.1 | async-start | bytes 524288 | tf_op jit(solution)/shard_map/all_to_all | solution.py:171

commit v5 on v4

v5 whole, which is shorter than its diff:
```python
import jax
import jax.numpy as jnp
from jax import lax
from jax.experimental import pallas as pl
from jax.experimental.pallas import tpu as pltpu
from jax.sharding import Mesh, PartitionSpec as P

HD = 128
TILE = 128
SCALE = HD**-0.5
LOG2E = 1.4426950408889634
AXES = ("y", "zh", "x", "zl", "c")
SIZES = (8, 4, 4, 2, 2)
BLOCKS = 4
HEADS_X = 2
HEADS_STEP = 2
PLANE = 64
GROUPS = ((1, 2, 4, 7), (0, 3, 5, 6))
NT = (((1,), (1,)), ((), ()))
VMEM = pl.BlockSpec(memory_space=pltpu.VMEM)
HBM = pl.BlockSpec(memory_space=pltpu.HBM)


def partner(zh, c):
    return lax.bitwise_xor(zh, 2 + c)


def end_of(zh):
    return jnp.where((zh == 0) | (zh == BLOCKS - 1), 1, 0)


def pick_kernel(keys, values, own, first, second, blocks, sems):
    x, zh, zl, c = (lax.axis_index(axis) for axis in ("x", "zh", "zl", "c"))
    copies = [
        pltpu.make_async_copy(source, blocks.at[k], sems.at[k])
        for k, source in enumerate((keys, values))
    ]
    for copy in copies:
        copy.start()
    flip = lax.rem(end_of(zh) + zl, 2)
    for k in range(2):
        copies[k].wait()
        for section, out in ((zh, own), (partner(zh, c), first), (lax.bitwise_xor(zh, 1), second)):
            head = x * HEADS_X + lax.rem(end_of(section) + flip, 2)
            out[k] = blocks[k, :, pl.ds(pl.multiple_of(head * HD, HD), HD)]


def prepare_kernel(
    tiles, text_len, queries, d_out, q_out, d_live, live_tiles, s_tiles, s_text, q, d, sems
):
    pairs = ((d_out, d), (queries, q), (text_len, s_text), (tiles, s_tiles))
    copies = [pltpu.make_async_copy(*pair, sems.at[i]) for i, pair in enumerate(pairs)]
    for copy in copies:
        copy.start()
    for copy in copies:
        copy.wait()
    y, zh = lax.axis_index("y"), lax.axis_index("zh")
    live_tiles[...] = jnp.full(live_tiles.shape, s_tiles[y], jnp.int32)
    rows, heads = queries.shape[0], queries.shape[1] // HD
    live = lax.broadcasted_iota(jnp.int32, (rows, HD), 0) + zh * rows < s_text[y]
    for h in range(heads):
        cols = pl.ds(h * HD, HD)
        step, place = h // HEADS_STEP, pl.ds(h % HEADS_STEP * rows, rows)
        q_out[step, place] = q[:, cols]
        d_live[step, place] = jnp.where(live, d[:, cols].astype(jnp.float32), 0.0).astype(jnp.bfloat16)


def stacked(parts, k):
    return jnp.concatenate([part[k] for part in parts], 0)


def products(parts, q, s):
    score = lax.dot_general(stacked(parts, 0), q, NT, preferred_element_type=jnp.float32)
    d_prob = lax.dot_general(stacked(parts, 1), s, NT, preferred_element_type=jnp.float32)
    return score, d_prob


def largest(score, live):
    top = -3e38
    for b in range(len(live)):
        part = jnp.max(score[b * TILE : (b + 1) * TILE], axis=0, keepdims=True)
        top = jnp.maximum(top, jnp.where(live[b], part, -3e38))
    return top


def exponentials(score, top, live):
    parts = []
    for b in range(len(live)):
        shift = jnp.where(live[b], top, 1e30)
        parts.append(jnp.exp2((score[b * TILE : (b + 1) * TILE] - shift) * (SCALE * LOG2E)))
    return jnp.concatenate(parts, 0)


def places():
    zh, c = lax.axis_index("zh"), lax.axis_index("c")
    return zh, partner(zh, c), lax.bitwise_xor(zh, 1), partner(zh, 1 - c)


def first_kernel(live_tiles, kv_0, kv_1, queries, d_out, expo_out, d_prob_out, stats):
    live = [place < live_tiles[0:1, 0:1] for place in places()[:2]]
    kv = (kv_0, kv_1)
    steps = queries.shape[0]
    ahead = products(kv, queries[0], d_out[0])
    for step in range(steps):
        score, d_prob = ahead
        if step < steps - 1:
            ahead = products(kv, queries[step + 1], d_out[step + 1])
        top = largest(score, live)
        expo = exponentials(score, top, live)
        expo_out[step] = expo
        d_prob_out[step] = d_prob
        stats[step, 0:1] = top
        stats[step, 1:2] = jnp.sum(expo, axis=0, keepdims=True)
        stats[step, 2:3] = jnp.sum(expo * d_prob, axis=0, keepdims=True)


def main_kernel(
    live_tiles, expo_1, d_prob_1, stats, kv_2, kv_3, queries, d_out, d_score, partial, acc_k, acc_v
):
    f32, bf16 = jnp.float32, jnp.bfloat16
    live = [place < live_tiles[0:1, 0:1] for place in places()[2:]]
    kv = (kv_2, kv_3)
    steps, half = queries.shape[0], expo_1.shape[1]
    ahead = products(kv, queries[0], d_out[0])
    for step in range(steps):
        q, s = queries[step], d_out[step]
        score, d_prob = ahead
        if step < steps - 1:
            ahead = products(kv, queries[step + 1], d_out[step + 1])
        top_1, sum_1, dot_1 = (stats[step, i : i + 1] for i in range(3))
        top = jnp.maximum(top_1, largest(score, live))
        expo = exponentials(score, top, live)
        weight = jnp.exp2((top_1 - top) * (SCALE * LOG2E))
        inverse = 1.0 / (sum_1 * weight + jnp.sum(expo, axis=0, keepdims=True))
        delta = (dot_1 * weight + jnp.sum(expo * d_prob, axis=0, keepdims=True)) * inverse
        prob_1 = (expo_1[step] * (weight * inverse)).astype(bf16)
        prob_2 = (expo * inverse).astype(bf16)
        d_s_1 = prob_1 * (d_prob_1[step] - delta).astype(bf16)
        d_s_2 = prob_2 * (d_prob - delta).astype(bf16)
        d_score[step, :half] = d_s_1
        d_score[step, half:] = d_s_2
        term_k = jnp.dot(jnp.concatenate([d_s_1, d_s_2], 0), q, preferred_element_type=f32)
        term_v = jnp.dot(jnp.concatenate([prob_1, prob_2], 0), s, preferred_element_type=f32)
        if step == 0:
            acc_k[...] = term_k
            acc_v[...] = term_v
        else:
            acc_k[...] += term_k
            acc_v[...] += term_v
    both = [acc.reshape(PLANE, 8, HD) for acc in (acc_k[...], acc_v[...])]
    both = jnp.concatenate(both, 1).astype(bf16)
    run = PLANE // BLOCKS
    for b, place in enumerate(places()):
        partial[pl.ds(place * run, run)] = both[b * run : (b + 1) * run]


def query_kernel(gate, kv_0, kv_1, kv_2, kv_3, d_score, d_queries):
    factor = jnp.tanh(gate[...]) * SCALE
    keys_t = stacked((kv_0, kv_1, kv_2, kv_3), 0).T
    rows = d_queries.shape[0]
    for step in range(d_score.shape[0]):
        d_q = jnp.dot(keys_t, d_score[step], preferred_element_type=jnp.float32)
        d_q = (d_q * factor).T.astype(jnp.bfloat16)
        for i in range(HEADS_STEP):
            cols = pl.ds((step * HEADS_STEP + i) * HD, HD)
            d_queries[:, cols] = d_q[i * rows : (i + 1) * rows]


def sum_kernel(gate, pieces, d_keys, d_values):
    factor = jnp.tanh(gate[...])
    _, zhs, xs, zls, cs = SIZES
    for head in range(xs * zls):
        total = None
        for zh in range(zhs):
            for c in range(cs):
                piece = pieces[(zh * xs * zls + head) * cs + c].astype(jnp.float32)
                total = piece if total is None else total + piece
        cols = pl.ds(head * HD, HD)
        d_keys[:, cols] = total[:8] * (factor * SCALE)
        d_values[:, cols] = total[8:] * factor


def in_vmem(array):
    return pltpu.with_memory_space_constraint(array, pltpu.VMEM)


def in_hbm(array):
    return pltpu.with_memory_space_constraint(array, pltpu.HBM)


def swap(value, step):
    pairs = []
    for c in range(2):
        for group in GROUPS:
            pairs += [(2 * group[i] + c, 2 * group[i ^ step[c]] + c) for i in range(BLOCKS)]
    return in_vmem(lax.ppermute(value, ("zh", "zl", "c"), pairs))


def local(queries, keys, values, d_out, gate, tiles, text_len):
    f32, bf16 = jnp.float32, jnp.bfloat16
    gate = gate.reshape(1, 1)
    block, width = keys.shape
    rows, width_q = queries.shape
    steps = width_q // HD // HEADS_STEP
    image = BLOCKS * block
    own, first, second = pl.pallas_call(
        pick_kernel,
        out_shape=(pltpu.VMEM((2, block, HD), bf16),) * 3,
        in_specs=[HBM, HBM],
        out_specs=(VMEM,) * 3,
        scratch_shapes=[pltpu.VMEM((2, block, width), bf16), pltpu.SemaphoreType.DMA((2,))],
        name="pick",
    )(in_hbm(keys), in_hbm(values))
    kv_0, kv_1, kv_2 = in_vmem(own), swap(first, (2, 3)), swap(second, (1, 1))
    kv_3 = in_vmem(lax.ppermute(kv_1, "c", [(0, 1), (1, 0)]))
    by_step = (steps, rows * HEADS_STEP, HD)
    q, d_live, live_tiles = pl.pallas_call(
        prepare_kernel,
        out_shape=(
            pltpu.VMEM(by_step, bf16),
            pltpu.VMEM(by_step, bf16),
            pltpu.VMEM((8, HD), jnp.int32),
        ),
        in_specs=[HBM] * 4,
        out_specs=(VMEM,) * 3,
        scratch_shapes=[
            pltpu.SMEM(tiles.shape, jnp.int32),
            pltpu.SMEM(text_len.shape, jnp.int32),
            pltpu.VMEM(queries.shape, bf16),
            pltpu.VMEM(queries.shape, bf16),
            pltpu.SemaphoreType.DMA((4,)),
        ],
        compiler_params=pltpu.CompilerParams(vmem_limit_bytes=16 * 2**20),
        cost_estimate=pl.CostEstimate(
            flops=4 * rows * width_q, bytes_accessed=8 * rows * width_q, transcendentals=0
        ),
        name="prepare",
    )(*(in_hbm(array) for array in (tiles, text_len, queries, d_out)))
    q, d_live, live_tiles = in_vmem(q), in_vmem(d_live), in_vmem(live_tiles)
    by_half = (steps, image // 2, rows * HEADS_STEP)
    expo, d_prob, stats = pl.pallas_call(
        first_kernel,
        out_shape=(
            pltpu.VMEM(by_half, f32),
            pltpu.VMEM(by_half, f32),
            pltpu.VMEM((steps, 8, rows * HEADS_STEP), f32),
        ),
        in_specs=[VMEM] * 5,
        out_specs=(VMEM,) * 3,
        compiler_params=pltpu.CompilerParams(vmem_limit_bytes=24 * 2**20),
        cost_estimate=pl.CostEstimate(
            flops=40 * rows * width_q * image, bytes_accessed=rows * width_q, transcendentals=0
        ),
        name="first_half",
    )(live_tiles, kv_0, kv_1, q, d_live)
    d_score, partial = pl.pallas_call(
        main_kernel,
        out_shape=(
            pltpu.VMEM((steps, image, rows * HEADS_STEP), bf16),
            pltpu.VMEM((PLANE, 16, HD), bf16),
        ),
        in_specs=[VMEM] * 8,
        out_specs=(VMEM, VMEM),
        scratch_shapes=[pltpu.VMEM((image, HD), f32), pltpu.VMEM((image, HD), f32)],
        compiler_params=pltpu.CompilerParams(vmem_limit_bytes=36 * 2**20),
        name="gradients",
    )(live_tiles, in_vmem(expo), in_vmem(d_prob), in_vmem(stats), kv_2, kv_3, q, d_live)
    pieces = lax.all_to_all(partial, ("zh", "x", "zl", "c"), 0, 0)
    d_queries = pl.pallas_call(
        query_kernel,
        out_shape=jax.ShapeDtypeStruct(queries.shape, bf16),
        in_specs=[VMEM] * 6,
        out_specs=VMEM,
        compiler_params=pltpu.CompilerParams(vmem_limit_bytes=16 * 2**20),
        cost_estimate=pl.CostEstimate(
            flops=2 * rows * width_q * image, bytes_accessed=4 * rows * width_q, transcendentals=0
        ),
        name="query_gradient",
    )(gate, kv_0, kv_1, kv_2, kv_3, in_vmem(d_score))
    d_keys, d_values = pl.pallas_call(
        sum_kernel,
        out_shape=(jax.ShapeDtypeStruct((8, width), f32),) * 2,
        in_specs=[VMEM, VMEM],
        out_specs=(VMEM, VMEM),
        name="add_up",
    )(gate, in_vmem(pieces))
    return d_queries, d_keys, d_values


def solution(mesh):
    mesh = Mesh(mesh.devices.reshape(SIZES), AXES)
    section, tensor = ("y", "zh"), ("x", "zl", "c")
    in_specs = (
        P(section, tensor),
        P(section, None),
        P(section, None),
        P(section, tensor),
        P(),
        P(),
        P(),
    )
    out_specs = (P(section, tensor), P(AXES, None), P(AXES, None))
    return jax.shard_map(local, mesh=mesh, in_specs=in_specs, out_specs=out_specs, check_vma=False)
```

time: 48 us -> 46.3 us (0.965)
  starting transfers between devices: 21.4 us -> 25.5 us
  local copies, waits for them, and re-layouts: 4.09 us -> 0 us
  waiting for transfers between devices: 13.8 us -> 10.4 us
  Pallas kernels: 7.02 us -> 8.73 us
    ppermute x0 -> x3, starting transfers between devices: none -> 18.6 us  [the longest x2 14.6 us: swap(): return in_vmem(lax.ppermute(value, ('zh', 'zl', 'c'), pairs))]
    all_to_all x1 -> x0, starting transfers between devices: 10.8 us -> none  [local(): lax.all_to_all(picked, ('zh', 'zl'), 0, 0, axis_index_groups=GROUPS)]
    unnamed x10 -> x0, local copies, waits for them, and re-layouts: 4.09 us -> none
    all_to_all x1, starting transfers between devices: 10.5 us -> 6.93 us  [local(): pieces = lax.all_to_all(partial, ('zh', 'x', 'zl', 'c'), 0, 0)]
    all_to_all x1 -> x0, waiting for transfers between devices: 2.84 us -> none  [local(): lax.all_to_all(picked, ('zh', 'zl'), 0, 0, axis_index_groups=GROUPS)]
    pallas_call x1, Pallas kernels: 0.3 us -> 1.44 us  [local(): pl.pallas_call(prepare_kernel, out_shape=(pltpu.VMEM(by_step, bf16), pltp...]
    all_to_all x1, waiting for transfers between devices: 11 us -> 10.3 us  [local(): pieces = lax.all_to_all(partial, ('zh', 'x', 'zl', 'c'), 0, 0)]
    pallas_call x1 -> x2, Pallas kernels: 1.77 us -> 1.89 us  [the longest x1 1.07 us: local(): pl.pallas_call(pick_kernel, out_shape=(pltpu.VMEM((2, block, HD), bf16),)...]
  transfers between devices with their start and end apart: 2 -> 4, of which waited for: 2 -> 1; matrix products, arithmetic and copies ran while one was open for 0% -> 0% of each run, Pallas kernels for 3% -> 8%
where the time goes in v5:
time: 46.3 us; the launch traced here: 46 us
  starting transfers between devices  25.5 us (55%)
  waiting for transfers between devices  10.4 us (22%)
  Pallas kernels  8.73 us (19%)
  between operations  1.35 us (3%)
    ppermute x2, starting transfers between devices, swap(): return in_vmem(lax.ppermute(value, ('zh', 'zl', 'c'), pairs))  14.6 us
    all_to_all x1, waiting for transfers between devices, local(): pieces = lax.all_to_all(partial, ('zh', 'x', 'zl', 'c'), 0, 0)  10.3 us
    all_to_all x1, starting transfers between devices, local(): pieces = lax.all_to_all(partial, ('zh', 'x', 'zl', 'c'), 0, 0)  6.93 us
    ppermute x1, starting transfers between devices, local(): kv_3 = in_vmem(lax.ppermute(kv_1, 'c', [(0, 1), (1, 0)]))  4.05 us
    pallas_call x1, Pallas kernels, local(): pl.pallas_call(main_kernel, out_shape=(pltpu.VMEM((steps, image, rows * H...  3.35 us
    pallas_call x1, Pallas kernels, local(): pl.pallas_call(prepare_kernel, out_shape=(pltpu.VMEM(by_step, bf16), pltp...  1.44 us
    pallas_call x1, Pallas kernels, local(): pl.pallas_call(query_kernel, out_shape=jax.ShapeDtypeStruct(queries.shape...  1.34 us
    pallas_call x1, Pallas kernels, local(): pl.pallas_call(pick_kernel, out_shape=(pltpu.VMEM((2, block, HD), bf16),)...  1.07 us
  transfers between devices with their start and end apart: 4, of which 1 were waited for; matrix products, arithmetic and copies ran while one was open for 0% of the time, Pallas kernels for 8%

profile of v5, /device:TPU:1, one launch (start us, length us, event | category | flops | bytes accessed | tf_op | source)
XLA Modules:
  0.0 46.0 jit_solution(4375577659356342896)
XLA Ops:
  0.6 1.1 %pick.1 = (bf16[2,128,128]{2,1,0:T(8,128)(2,1)S(1)}, bf16[2,128,128]{2,1,0:T(8,128)(2,1)S(1)}, bf16[2,128,128]{2,1,0:T(8,128)(2,1)S(1)}) custom-call(bf16[128,1024]{1,0:T(8,128)(2,1)} %keys.1, bf16[128,1024]{1,0:T(8,128)(2,1)} %values.1), custom_call_target="tpu_custom_call" | custom-call | tf_op jit(solution)/shard_map/pick/pallas_call | solution.py:206
  1.7 11.5 %collective-permute-start = (bf16[2,128,128]{2,1,0:T(8,128)(2,1)S(1)}, bf16[2,128,128]{2,1,0:T(8,128)(2,1)S(1)}, u32[]{:S(2)}, u32[]{:S(2)}) collective-permute-start(bf16[2,128,128]{2,1,0:T(8,128)(2,1)S(1)} %get-tuple-element.17), channel_id=1, source_target_pairs={{2,32},{16,50},{32,2},{50,16},{0,34},{18,48},{34,0},{48,18},{3,51}... | collective-permute-start | bytes 196616 | tf_op jit(solution)/shard_map/ppermute | solution.py:196
  13.2 3.1 %collective-permute-start.1 = (bf16[2,128,128]{2,1,0:T(8,128)(2,1)S(1)}, bf16[2,128,128]{2,1,0:T(8,128)(2,1)S(1)}, u32[]{:S(2)}, u32[]{:S(2)}) collective-permute-start(bf16[2,128,128]{2,1,0:T(8,128)(2,1)S(1)} %get-tuple-element.18), channel_id=1, source_target_pairs={{2,16},{16,2},{32,50},{50,32},{0,18},{18,0},{34,48},{48,34},{3,17}... | collective-permute-start | bytes 196616 | tf_op jit(solution)/shard_map/ppermute | solution.py:196
  16.3 1.4 %prepare.1 = (bf16[2,1024,128]{2,1,0:T(8,128)(2,1)S(1)}, bf16[2,1024,128]{2,1,0:T(8,128)(2,1)S(1)}, s32[8,128]{1,0:T(8,128)S(1)}) custom-call(s32[8]{0:T(128)} %tiles.1, s32[8]{0:T(128)} %text_len.1, bf16[512,512]{1,0:T(8,128)(2,1)} %queries.1, bf16[512,512]{1,0:T(8,128)(2,1)} %d_out.1), custom_call_target="tpu_custom_call" | custom-call | flops 1048576 | bytes 2097152 | tf_op jit(solution)/shard_map/prepare/pallas_call | solution.py:217
  17.7 0.0 collective-permute-done.kv_1
  17.8 4.1 %collective-permute-start.2 = (bf16[2,128,128]{2,1,0:T(8,128)(2,1)S(1)}, bf16[2,128,128]{2,1,0:T(8,128)(2,1)S(1)}, u32[]{:S(2)}, u32[]{:S(2)}) collective-permute-start(bf16[2,128,128]{2,1,0:T(8,128)(2,1)S(1)} %collective-permute-done.kv_1), channel_id=1, source_target_pairs={{0,1},{1,0},{2,3},{3,2},{4,5},{5,4},{6,7},{7,6},{8,9},{9,8},{10,11... | collective-permute-start | bytes 196616 | tf_op jit(solution)/shard_map/ppermute | solution.py:215
  21.8 0.8 %first_half.1 = (f32[2,256,1024]{2,1,0:T(8,128)S(1)}, f32[2,256,1024]{2,1,0:T(8,128)S(1)}, f32[2,8,1024]{2,1,0:T(8,128)S(1)}) custom-call(s32[8,128]{1,0:T(8,128)S(1)} %get-tuple-element.19.live_tiles, bf16[2,128,128]{2,1,0:T(8,128)(2,1)S(1)} %get-tuple-element.16.kv_0, bf16[2,128,128]{2,1,0:T(8,128)(2,1)S(1)} %collective-permute-done.kv_1, ...), custom_call_target="tpu_custom_call" | custom-call | flops 5368709120 | bytes 262144 | tf_op jit(solution)/shard_map/first_half/pallas_call | solution.py:241
  22.6 0.0 collective-permute-done.1.kv_2
  22.7 0.0 collective-permute-done.2.kv_3
  22.7 3.3 %gradients.1 = (bf16[2,512,1024]{2,1,0:T(8,128)(2,1)S(1)}, bf16[64,16,128]{2,1,0:T(8,128)(2,1)}) custom-call(s32[8,128]{1,0:T(8,128)S(1)} %get-tuple-element.19.live_tiles, f32[2,256,1024]{2,1,0:T(8,128)S(1)} %get-tuple-element.22.expo_1, f32[2,256,1024]{2,1,0:T(8,128)S(1)} %get-tuple-element.23.d_prob_1, f32[2,8,1024]{2,1,0:T(8,128)S(1)} %get-tuple-element.24.stats, ...), custom_call_target="tpu_custom_call" | custom-call | tf_op jit(solution)/shard_map/gradients/pallas_call | solution.py:256
  26.0 6.9 %all-to-all-start = ((bf16[64,16,128]{2,1,0:T(8,128)(2,1)}), bf16[64,16,128]{2,1,0:T(8,128)(2,1)S(1)}, u32[]{:S(2)}, u32[]{:S(2)}) async-start(bf16[64,16,128]{2,1,0:T(8,128)(2,1)} %get-tuple-element.26), calls=%async_computation | async-start | bytes 524288 | tf_op jit(solution)/shard_map/all_to_all | solution.py:268
  33.6 1.3 %query_gradient.1 = bf16[512,512]{1,0:T(8,128)(2,1)} custom-call(f32[1,1]{1,0:T(1,128)} %bitcast.1.gate, bf16[2,128,128]{2,1,0:T(8,128)(2,1)S(1)} %get-tuple-element.16.kv_0, bf16[2,128,128]{2,1,0:T(8,128)(2,1)S(1)} %collective-permute-done.kv_1, bf16[2,128,128]{2,1,0:T(8,128)(2,1)S(1)} %collective-permute-done.1.kv_2, ...), custom_call_target="tpu_custom_call" | custom-call | flops 268435456 | bytes 1048576 | tf_op jit(solution)/shard_map/query_gradient/pallas_call | solution.py:269
  35.0 10.3 %all-to-all-done.pieces = bf16[64,16,128]{2,1,0:T(8,128)(2,1)S(1)} async-done(((bf16[64,16,128]{2,1,0:T(8,128)(2,1)}), bf16[64,16,128]{2,1,0:T(8,128)(2,1)S(1)}, u32[]{:S(2)}, u32[]{:S(2)}) %all-to-all-start) | async-done | bytes 262176 | tf_op jit(solution)/shard_map/all_to_all | solution.py:268
  45.3 0.7 %add_up.1 = (f32[8,1024]{1,0:T(8,128)}, f32[8,1024]{1,0:T(8,128)}) custom-call(f32[1,1]{1,0:T(1,128)} %bitcast.2.gate, bf16[64,16,128]{2,1,0:T(8,128)(2,1)S(1)} %all-to-all-done.pieces), custom_call_target="tpu_custom_call" | custom-call | tf_op jit(solution)/shard_map/add_up/pallas_call | solution.py:280
Async XLA Ops:
  1.7 16.0 %collective-permute-start = (bf16[2,128,128]{2,1,0:T(8,128)(2,1)S(1)}, bf16[2,128,128]{2,1,0:T(8,128)(2,1)S(1)}, u32[]{:S(2)}, u32[]{:S(2)}) collective-permute-start(bf16[2,128,128]{2,1,0:T(8,128)(2,1)S(1)} %get-tuple-element.17), channel_id=1, source_target_pairs={{2,32},{16,50},{32,2},{50,16},{0,34},{18,48},{34,0},{48,18},{3,51}... | collective-permute-start | bytes 196616 | tf_op jit(solution)/shard_map/ppermute | solution.py:196
  13.2 9.4 %collective-permute-start.1 = (bf16[2,128,128]{2,1,0:T(8,128)(2,1)S(1)}, bf16[2,128,128]{2,1,0:T(8,128)(2,1)S(1)}, u32[]{:S(2)}, u32[]{:S(2)}) collective-permute-start(bf16[2,128,128]{2,1,0:T(8,128)(2,1)S(1)} %get-tuple-element.18), channel_id=1, source_target_pairs={{2,16},{16,2},{32,50},{50,32},{0,18},{18,0},{34,48},{48,34},{3,17}... | collective-permute-start | bytes 196616 | tf_op jit(solution)/shard_map/ppermute | solution.py:196
  17.8 4.9 %collective-permute-start.2 = (bf16[2,128,128]{2,1,0:T(8,128)(2,1)S(1)}, bf16[2,128,128]{2,1,0:T(8,128)(2,1)S(1)}, u32[]{:S(2)}, u32[]{:S(2)}) collective-permute-start(bf16[2,128,128]{2,1,0:T(8,128)(2,1)S(1)} %collective-permute-done.kv_1), channel_id=1, source_target_pairs={{0,1},{1,0},{2,3},{3,2},{4,5},{5,4},{6,7},{7,6},{8,9},{9,8},{10,11... | collective-permute-start | bytes 196616 | tf_op jit(solution)/shard_map/ppermute | solution.py:215
  26.0 19.3 %all-to-all-start = ((bf16[64,16,128]{2,1,0:T(8,128)(2,1)}), bf16[64,16,128]{2,1,0:T(8,128)(2,1)S(1)}, u32[]{:S(2)}, u32[]{:S(2)}) async-start(bf16[64,16,128]{2,1,0:T(8,128)(2,1)} %get-tuple-element.26), calls=%async_computation | async-start | bytes 524288 | tf_op jit(solution)/shard_map/all_to_all | solution.py:268

commit v6 on v5

--- a/solution.py
+++ b/solution.py
@@ -16,6 +16,7 @@
 HEADS_STEP = 2
 PLANE = 64
 GROUPS = ((1, 2, 4, 7), (0, 3, 5, 6))
+FIRST_ZH, FIRST_X = 2, 2
 NT = (((1,), (1,)), ((), ()))
 VMEM = pl.BlockSpec(memory_space=pltpu.VMEM)
 HBM = pl.BlockSpec(memory_space=pltpu.HBM)
@@ -96,9 +97,9 @@
     return zh, partner(zh, c), lax.bitwise_xor(zh, 1), partner(zh, 1 - c)
 
 
-def first_kernel(live_tiles, kv_0, kv_1, queries, d_out, expo_out, d_prob_out, stats):
-    live = [place < live_tiles[0:1, 0:1] for place in places()[:2]]
-    kv = (kv_0, kv_1)
+def first_kernel(live_tiles, kv_0, kv_1, kv_2, queries, d_out, expo_out, d_prob_out, stats):
+    live = [place < live_tiles[0:1, 0:1] for place in places()[:3]]
+    kv = (kv_0, kv_1, kv_2)
     steps = queries.shape[0]
     ahead = products(kv, queries[0], d_out[0])
     for step in range(steps):
@@ -115,12 +116,12 @@
 
 
 def main_kernel(
-    live_tiles, expo_1, d_prob_1, stats, kv_2, kv_3, queries, d_out, d_score, partial, acc_k, acc_v
+    live_tiles, expo_1, d_prob_1, stats, kv_3, queries, d_out, d_score, partial, acc_k, acc_v
 ):
     f32, bf16 = jnp.float32, jnp.bfloat16
-    live = [place < live_tiles[0:1, 0:1] for place in places()[2:]]
-    kv = (kv_2, kv_3)
-    steps, half = queries.shape[0], expo_1.shape[1]
+    live = [place < live_tiles[0:1, 0:1] for place in places()[3:]]
+    kv = (kv_3,)
+    steps, before = queries.shape[0], expo_1.shape[1]
     ahead = products(kv, queries[0], d_out[0])
     for step in range(steps):
         q, s = queries[step], d_out[step]
@@ -137,8 +138,8 @@
         prob_2 = (expo * inverse).astype(bf16)
         d_s_1 = prob_1 * (d_prob_1[step] - delta).astype(bf16)
         d_s_2 = prob_2 * (d_prob - delta).astype(bf16)
-        d_score[step, :half] = d_s_1
-        d_score[step, half:] = d_s_2
+        d_score[step, :before] = d_s_1
+        d_score[step, before:] = d_s_2
         term_k = jnp.dot(jnp.concatenate([d_s_1, d_s_2], 0), q, preferred_element_type=f32)
         term_v = jnp.dot(jnp.concatenate([prob_1, prob_2], 0), s, preferred_element_type=f32)
         if step == 0:
@@ -150,8 +151,11 @@
     both = [acc.reshape(PLANE, 8, HD) for acc in (acc_k[...], acc_v[...])]
     both = jnp.concatenate(both, 1).astype(bf16)
     run = PLANE // BLOCKS
+    part = run // SIZES[2]
     for b, place in enumerate(places()):
-        partial[pl.ds(place * run, run)] = both[b * run : (b + 1) * run]
+        for x in range(SIZES[2]):
+            at = lax.bitwise_xor(place, FIRST_ZH) * run + (x ^ FIRST_X) * part
+            partial[pl.ds(at, part)] = both[b * run + x * part : b * run + (x + 1) * part]
 
 
 def query_kernel(gate, kv_0, kv_1, kv_2, kv_3, d_score, d_queries):
@@ -170,10 +174,11 @@
     factor = jnp.tanh(gate[...])
     _, zhs, xs, zls, cs = SIZES
     for head in range(xs * zls):
+        place = ((head // zls) ^ FIRST_X) * zls + head % zls
         total = None
         for zh in range(zhs):
             for c in range(cs):
-                piece = pieces[(zh * xs * zls + head) * cs + c].astype(jnp.float32)
+                piece = pieces[(zh * xs * zls + place) * cs + c].astype(jnp.float32)
                 total = piece if total is None else total + piece
         cols = pl.ds(head * HD, HD)
         d_keys[:, cols] = total[:8] * (factor * SCALE)
@@ -237,35 +242,42 @@
         name="prepare",
     )(*(in_hbm(array) for array in (tiles, text_len, queries, d_out)))
     q, d_live, live_tiles = in_vmem(q), in_vmem(d_live), in_vmem(live_tiles)
-    by_half = (steps, image // 2, rows * HEADS_STEP)
+    by_part = (steps, image - block, rows * HEADS_STEP)
     expo, d_prob, stats = pl.pallas_call(
         first_kernel,
         out_shape=(
-            pltpu.VMEM(by_half, f32),
-            pltpu.VMEM(by_half, f32),
+            pltpu.VMEM(by_part, f32),
+            pltpu.VMEM(by_part, f32),
             pltpu.VMEM((steps, 8, rows * HEADS_STEP), f32),
         ),
-        in_specs=[VMEM] * 5,
+        in_specs=[VMEM] * 6,
         out_specs=(VMEM,) * 3,
         compiler_params=pltpu.CompilerParams(vmem_limit_bytes=24 * 2**20),
         cost_estimate=pl.CostEstimate(
             flops=40 * rows * width_q * image, bytes_accessed=rows * width_q, transcendentals=0
         ),
-        name="first_half",
-    )(live_tiles, kv_0, kv_1, q, d_live)
+        name="three_blocks",
+    )(live_tiles, kv_0, kv_1, kv_2, q, d_live)
     d_score, partial = pl.pallas_call(
         main_kernel,
         out_shape=(
             pltpu.VMEM((steps, image, rows * HEADS_STEP), bf16),
             pltpu.VMEM((PLANE, 16, HD), bf16),
         ),
-        in_specs=[VMEM] * 8,
+        in_specs=[VMEM] * 7,
         out_specs=(VMEM, VMEM),
         scratch_shapes=[pltpu.VMEM((image, HD), f32), pltpu.VMEM((image, HD), f32)],
         compiler_params=pltpu.CompilerParams(vmem_limit_bytes=36 * 2**20),
         name="gradients",
-    )(live_tiles, in_vmem(expo), in_vmem(d_prob), in_vmem(stats), kv_2, kv_3, q, d_live)
-    pieces = lax.all_to_all(partial, ("zh", "x", "zl", "c"), 0, 0)
+    )(live_tiles, in_vmem(expo), in_vmem(d_prob), in_vmem(stats), kv_3, q, d_live)
+    _, zhs, xs, zls, cs = SIZES
+    members = [
+        ((zh ^ FIRST_ZH) * xs + (x ^ FIRST_X)) * zls * cs + i
+        for zh in range(zhs)
+        for x in range(xs)
+        for i in range(zls * cs)
+    ]
+    pieces = lax.all_to_all(partial, ("zh", "x", "zl", "c"), 0, 0, axis_index_groups=[members])
     d_queries = pl.pallas_call(
         query_kernel,
         out_shape=jax.ShapeDtypeStruct(queries.shape, bf16),

time: 46.3 us -> 44.3 us (0.957)
  waiting for transfers between devices: 10.4 us -> 4.69 us
  starting transfers between devices: 25.5 us -> 29.6 us
    all_to_all x1, waiting for transfers between devices: 10.3 us -> 4.68 us  [local(): lax.all_to_all(partial, ('zh', 'x', 'zl', 'c'), 0, 0, axis_index_groups=[...]
    all_to_all x1, starting transfers between devices: 6.93 us -> 10.9 us  [local(): lax.all_to_all(partial, ('zh', 'x', 'zl', 'c'), 0, 0, axis_index_groups=[...]
    pallas_call x1, Pallas kernels: 3.35 us -> 2.69 us  [local(): pl.pallas_call(main_kernel, out_shape=(pltpu.VMEM((steps, image, rows * H...]
  transfers between devices with their start and end apart: 4 -> 4, of which waited for: 1 -> 1; matrix products, arithmetic and copies ran while one was open for 0% -> 0% of each run, Pallas kernels for 8% -> 9%
where the time goes in v6:
time: 44.3 us; the launch traced here: 44 us
  starting transfers between devices  29.6 us (67%)
  Pallas kernels  8.41 us (19%)
  waiting for transfers between devices  4.69 us (11%)
  between operations  1.36 us (3%)
    ppermute x2, starting transfers between devices, swap(): return in_vmem(lax.ppermute(value, ('zh', 'zl', 'c'), pairs))  14.6 us
    all_to_all x1, starting transfers between devices, local(): lax.all_to_all(partial, ('zh', 'x', 'zl', 'c'), 0, 0, axis_index_groups=[...  10.9 us
    all_to_all x1, waiting for transfers between devices, local(): lax.all_to_all(partial, ('zh', 'x', 'zl', 'c'), 0, 0, axis_index_groups=[...  4.68 us
    ppermute x1, starting transfers between devices, local(): kv_3 = in_vmem(lax.ppermute(kv_1, 'c', [(0, 1), (1, 0)]))  4.05 us
    pallas_call x1, Pallas kernels, local(): pl.pallas_call(main_kernel, out_shape=(pltpu.VMEM((steps, image, rows * H...  2.69 us
    pallas_call x1, Pallas kernels, local(): pl.pallas_call(prepare_kernel, out_shape=(pltpu.VMEM(by_step, bf16), pltp...  1.44 us
    pallas_call x1, Pallas kernels, local(): pl.pallas_call(query_kernel, out_shape=jax.ShapeDtypeStruct(queries.shape...  1.34 us
    pallas_call x1, Pallas kernels, local(): pl.pallas_call(first_kernel, out_shape=(pltpu.VMEM(by_part, f32), pltpu.V...  1.16 us
  transfers between devices with their start and end apart: 4, of which 1 were waited for; matrix products, arithmetic and copies ran while one was open for 0% of the time, Pallas kernels for 9%

profile of v6, /device:TPU:1, one launch (start us, length us, event | category | flops | bytes accessed | tf_op | source)
XLA Modules:
  0.0 44.0 jit_solution(5397680331792767032)
XLA Ops:
  0.6 1.1 %pick.1 = (bf16[2,128,128]{2,1,0:T(8,128)(2,1)S(1)}, bf16[2,128,128]{2,1,0:T(8,128)(2,1)S(1)}, bf16[2,128,128]{2,1,0:T(8,128)(2,1)S(1)}) custom-call(bf16[128,1024]{1,0:T(8,128)(2,1)} %keys.1, bf16[128,1024]{1,0:T(8,128)(2,1)} %values.1), custom_call_target="tpu_custom_call" | custom-call | tf_op jit(solution)/shard_map/pick/pallas_call | solution.py:211
  1.7 11.5 %collective-permute-start = (bf16[2,128,128]{2,1,0:T(8,128)(2,1)S(1)}, bf16[2,128,128]{2,1,0:T(8,128)(2,1)S(1)}, u32[]{:S(2)}, u32[]{:S(2)}) collective-permute-start(bf16[2,128,128]{2,1,0:T(8,128)(2,1)S(1)} %get-tuple-element.17), channel_id=1, source_target_pairs={{2,32},{16,50},{32,2},{50,16},{0,34},{18,48},{34,0},{48,18},{3,51}... | collective-permute-start | bytes 196616 | tf_op jit(solution)/shard_map/ppermute | solution.py:201
  13.2 3.1 %collective-permute-start.1 = (bf16[2,128,128]{2,1,0:T(8,128)(2,1)S(1)}, bf16[2,128,128]{2,1,0:T(8,128)(2,1)S(1)}, u32[]{:S(2)}, u32[]{:S(2)}) collective-permute-start(bf16[2,128,128]{2,1,0:T(8,128)(2,1)S(1)} %get-tuple-element.18), channel_id=1, source_target_pairs={{2,16},{16,2},{32,50},{50,32},{0,18},{18,0},{34,48},{48,34},{3,17}... | collective-permute-start | bytes 196616 | tf_op jit(solution)/shard_map/ppermute | solution.py:201
  16.3 1.4 %prepare.1 = (bf16[2,1024,128]{2,1,0:T(8,128)(2,1)S(1)}, bf16[2,1024,128]{2,1,0:T(8,128)(2,1)S(1)}, s32[8,128]{1,0:T(8,128)S(1)}) custom-call(s32[8]{0:T(128)} %tiles.1, s32[8]{0:T(128)} %text_len.1, bf16[512,512]{1,0:T(8,128)(2,1)} %queries.1, bf16[512,512]{1,0:T(8,128)(2,1)} %d_out.1), custom_call_target="tpu_custom_call" | custom-call | flops 1048576 | bytes 2097152 | tf_op jit(solution)/shard_map/prepare/pallas_call | solution.py:222
  17.7 0.0 collective-permute-done.kv_1
  17.8 4.1 %collective-permute-start.2 = (bf16[2,128,128]{2,1,0:T(8,128)(2,1)S(1)}, bf16[2,128,128]{2,1,0:T(8,128)(2,1)S(1)}, u32[]{:S(2)}, u32[]{:S(2)}) collective-permute-start(bf16[2,128,128]{2,1,0:T(8,128)(2,1)S(1)} %collective-permute-done.kv_1), channel_id=1, source_target_pairs={{0,1},{1,0},{2,3},{3,2},{4,5},{5,4},{6,7},{7,6},{8,9},{9,8},{10,11... | collective-permute-start | bytes 196616 | tf_op jit(solution)/shard_map/ppermute | solution.py:220
  21.8 0.0 collective-permute-done.1.kv_2
  21.8 1.2 %three_blocks.1 = (f32[2,384,1024]{2,1,0:T(8,128)S(1)}, f32[2,384,1024]{2,1,0:T(8,128)S(1)}, f32[2,8,1024]{2,1,0:T(8,128)S(1)}) custom-call(s32[8,128]{1,0:T(8,128)S(1)} %get-tuple-element.19.live_tiles, bf16[2,128,128]{2,1,0:T(8,128)(2,1)S(1)} %get-tuple-element.16.kv_0, bf16[2,128,128]{2,1,0:T(8,128)(2,1)S(1)} %collective-permute-done.kv_1, ...), custom_call_target="tpu_custom_call" | custom-call | flops 5368709120 | bytes 262144 | tf_op jit(solution)/shard_map/three_blocks/pallas_call | solution.py:246
  23.0 0.0 collective-permute-done.2.kv_3
  23.0 2.7 %gradients.1 = (bf16[2,512,1024]{2,1,0:T(8,128)(2,1)S(1)}, bf16[64,16,128]{2,1,0:T(8,128)(2,1)}) custom-call(s32[8,128]{1,0:T(8,128)S(1)} %get-tuple-element.19.live_tiles, f32[2,384,1024]{2,1,0:T(8,128)S(1)} %get-tuple-element.22.expo_1, f32[2,384,1024]{2,1,0:T(8,128)S(1)} %get-tuple-element.23.d_prob_1, f32[2,8,1024]{2,1,0:T(8,128)S(1)} %get-tuple-element.24.stats, ...), custom_call_target="tpu_custom_call" | custom-call | tf_op jit(solution)/shard_map/gradients/pallas_call | solution.py:261
  25.7 10.9 %all-to-all-start = ((bf16[64,16,128]{2,1,0:T(8,128)(2,1)}), bf16[64,16,128]{2,1,0:T(8,128)(2,1)S(1)}, u32[]{:S(2)}, u32[]{:S(2)}) async-start(bf16[64,16,128]{2,1,0:T(8,128)(2,1)} %get-tuple-element.26), calls=%async_computation | async-start | bytes 524288 | tf_op jit(solution)/shard_map/all_to_all | solution.py:280
  37.3 1.3 %query_gradient.1 = bf16[512,512]{1,0:T(8,128)(2,1)} custom-call(f32[1,1]{1,0:T(1,128)} %bitcast.1.gate, bf16[2,128,128]{2,1,0:T(8,128)(2,1)S(1)} %get-tuple-element.16.kv_0, bf16[2,128,128]{2,1,0:T(8,128)(2,1)S(1)} %collective-permute-done.kv_1, bf16[2,128,128]{2,1,0:T(8,128)(2,1)S(1)} %collective-permute-done.1.kv_2, ...), custom_call_target="tpu_custom_call" | custom-call | flops 268435456 | bytes 1048576 | tf_op jit(solution)/shard_map/query_gradient/pallas_call | solution.py:281
  38.6 4.7 %all-to-all-done.pieces = bf16[64,16,128]{2,1,0:T(8,128)(2,1)S(1)} async-done(((bf16[64,16,128]{2,1,0:T(8,128)(2,1)}), bf16[64,16,128]{2,1,0:T(8,128)(2,1)S(1)}, u32[]{:S(2)}, u32[]{:S(2)}) %all-to-all-start) | async-done | bytes 262176 | tf_op jit(solution)/shard_map/all_to_all | solution.py:280
  43.3 0.7 %add_up.1 = (f32[8,1024]{1,0:T(8,128)}, f32[8,1024]{1,0:T(8,128)}) custom-call(f32[1,1]{1,0:T(1,128)} %bitcast.2.gate, bf16[64,16,128]{2,1,0:T(8,128)(2,1)S(1)} %all-to-all-done.pieces), custom_call_target="tpu_custom_call" | custom-call | tf_op jit(solution)/shard_map/add_up/pallas_call | solution.py:292
Async XLA Ops:
  1.7 16.0 %collective-permute-start = (bf16[2,128,128]{2,1,0:T(8,128)(2,1)S(1)}, bf16[2,128,128]{2,1,0:T(8,128)(2,1)S(1)}, u32[]{:S(2)}, u32[]{:S(2)}) collective-permute-start(bf16[2,128,128]{2,1,0:T(8,128)(2,1)S(1)} %get-tuple-element.17), channel_id=1, source_target_pairs={{2,32},{16,50},{32,2},{50,16},{0,34},{18,48},{34,0},{48,18},{3,51}... | collective-permute-start | bytes 196616 | tf_op jit(solution)/shard_map/ppermute | solution.py:201
  13.2 8.6 %collective-permute-start.1 = (bf16[2,128,128]{2,1,0:T(8,128)(2,1)S(1)}, bf16[2,128,128]{2,1,0:T(8,128)(2,1)S(1)}, u32[]{:S(2)}, u32[]{:S(2)}) collective-permute-start(bf16[2,128,128]{2,1,0:T(8,128)(2,1)S(1)} %get-tuple-element.18), channel_id=1, source_target_pairs={{2,16},{16,2},{32,50},{50,32},{0,18},{18,0},{34,48},{48,34},{3,17}... | collective-permute-start | bytes 196616 | tf_op jit(solution)/shard_map/ppermute | solution.py:201
  17.8 5.2 %collective-permute-start.2 = (bf16[2,128,128]{2,1,0:T(8,128)(2,1)S(1)}, bf16[2,128,128]{2,1,0:T(8,128)(2,1)S(1)}, u32[]{:S(2)}, u32[]{:S(2)}) collective-permute-start(bf16[2,128,128]{2,1,0:T(8,128)(2,1)S(1)} %collective-permute-done.kv_1), channel_id=1, source_target_pairs={{0,1},{1,0},{2,3},{3,2},{4,5},{5,4},{6,7},{7,6},{8,9},{9,8},{10,11... | collective-permute-start | bytes 196616 | tf_op jit(solution)/shard_map/ppermute | solution.py:220
  25.7 17.6 %all-to-all-start = ((bf16[64,16,128]{2,1,0:T(8,128)(2,1)}), bf16[64,16,128]{2,1,0:T(8,128)(2,1)S(1)}, u32[]{:S(2)}, u32[]{:S(2)}) async-start(bf16[64,16,128]{2,1,0:T(8,128)(2,1)} %get-tuple-element.26), calls=%async_computation | async-start | bytes 524288 | tf_op jit(solution)/shard_map/all_to_all | solution.py:280

commit v7 on v6

--- a/solution.py
+++ b/solution.py
@@ -16,7 +16,7 @@
 HEADS_STEP = 2
 PLANE = 64
 GROUPS = ((1, 2, 4, 7), (0, 3, 5, 6))
-FIRST_ZH, FIRST_X = 2, 2
+FIRST_ZH, FIRST_IN = 2, 9
 NT = (((1,), (1,)), ((), ()))
 VMEM = pl.BlockSpec(memory_space=pltpu.VMEM)
 HBM = pl.BlockSpec(memory_space=pltpu.HBM)
@@ -151,11 +151,10 @@
     both = [acc.reshape(PLANE, 8, HD) for acc in (acc_k[...], acc_v[...])]
     both = jnp.concatenate(both, 1).astype(bf16)
     run = PLANE // BLOCKS
-    part = run // SIZES[2]
     for b, place in enumerate(places()):
-        for x in range(SIZES[2]):
-            at = lax.bitwise_xor(place, FIRST_ZH) * run + (x ^ FIRST_X) * part
-            partial[pl.ds(at, part)] = both[b * run + x * part : b * run + (x + 1) * part]
+        for i in range(run):
+            at = lax.bitwise_xor(place, FIRST_ZH) * run + (i ^ FIRST_IN)
+            partial[pl.ds(at, 1)] = both[b * run + i : b * run + i + 1]
 
 
 def query_kernel(gate, kv_0, kv_1, kv_2, kv_3, d_score, d_queries):
@@ -172,13 +171,12 @@
 
 def sum_kernel(gate, pieces, d_keys, d_values):
     factor = jnp.tanh(gate[...])
-    _, zhs, xs, zls, cs = SIZES
-    for head in range(xs * zls):
-        place = ((head // zls) ^ FIRST_X) * zls + head % zls
+    heads = PLANE // BLOCKS // 2
+    for head in range(heads):
         total = None
-        for zh in range(zhs):
-            for c in range(cs):
-                piece = pieces[(zh * xs * zls + place) * cs + c].astype(jnp.float32)
+        for zh in range(BLOCKS):
+            for c in range(2):
+                piece = pieces[(zh * heads + (head ^ FIRST_IN // 2)) * 2 + c].astype(jnp.float32)
                 total = piece if total is None else total + piece
         cols = pl.ds(head * HD, HD)
         d_keys[:, cols] = total[:8] * (factor * SCALE)
@@ -270,13 +268,8 @@
         compiler_params=pltpu.CompilerParams(vmem_limit_bytes=36 * 2**20),
         name="gradients",
     )(live_tiles, in_vmem(expo), in_vmem(d_prob), in_vmem(stats), kv_3, q, d_live)
-    _, zhs, xs, zls, cs = SIZES
-    members = [
-        ((zh ^ FIRST_ZH) * xs + (x ^ FIRST_X)) * zls * cs + i
-        for zh in range(zhs)
-        for x in range(xs)
-        for i in range(zls * cs)
-    ]
+    run = PLANE // BLOCKS
+    members = [(zh ^ FIRST_ZH) * run + (i ^ FIRST_IN) for zh in range(BLOCKS) for i in range(run)]
     pieces = lax.all_to_all(partial, ("zh", "x", "zl", "c"), 0, 0, axis_index_groups=[members])
     d_queries = pl.pallas_call(
         query_kernel,

time: 44.3 us -> 43.8 us (0.989)
  no operation moved by 1% of the time
where the time goes in v7:
time: 43.8 us; the launch traced here: 43.5 us
  starting transfers between devices  29.2 us (67%)
  Pallas kernels  8.41 us (19%)
  waiting for transfers between devices  4.54 us (10%)
  between operations  1.36 us (3%)
    ppermute x2, starting transfers between devices, swap(): return in_vmem(lax.ppermute(value, ('zh', 'zl', 'c'), pairs))  14.6 us
    all_to_all x1, starting transfers between devices, local(): lax.all_to_all(partial, ('zh', 'x', 'zl', 'c'), 0, 0, axis_index_groups=[...  10.6 us
    all_to_all x1, waiting for transfers between devices, local(): lax.all_to_all(partial, ('zh', 'x', 'zl', 'c'), 0, 0, axis_index_groups=[...  4.53 us
    ppermute x1, starting transfers between devices, local(): kv_3 = in_vmem(lax.ppermute(kv_1, 'c', [(0, 1), (1, 0)]))  4.05 us
    pallas_call x1, Pallas kernels, local(): pl.pallas_call(main_kernel, out_shape=(pltpu.VMEM((steps, image, rows * H...  2.69 us
    pallas_call x1, Pallas kernels, local(): pl.pallas_call(prepare_kernel, out_shape=(pltpu.VMEM(by_step, bf16), pltp...  1.44 us
    pallas_call x1, Pallas kernels, local(): pl.pallas_call(query_kernel, out_shape=jax.ShapeDtypeStruct(queries.shape...  1.34 us
    pallas_call x1, Pallas kernels, local(): pl.pallas_call(first_kernel, out_shape=(pltpu.VMEM(by_part, f32), pltpu.V...  1.16 us
  transfers between devices with their start and end apart: 4, of which 1 were waited for; matrix products, arithmetic and copies ran while one was open for 0% of the time, Pallas kernels for 9%

profile of v7, /device:TPU:1, one launch (start us, length us, event | category | flops | bytes accessed | tf_op | source)
XLA Modules:
  0.0 43.5 jit_solution(12197043569418917708)
XLA Ops:
  0.6 1.1 %pick.1 = (bf16[2,128,128]{2,1,0:T(8,128)(2,1)S(1)}, bf16[2,128,128]{2,1,0:T(8,128)(2,1)S(1)}, bf16[2,128,128]{2,1,0:T(8,128)(2,1)S(1)}) custom-call(bf16[128,1024]{1,0:T(8,128)(2,1)} %keys.1, bf16[128,1024]{1,0:T(8,128)(2,1)} %values.1), custom_call_target="tpu_custom_call" | custom-call | tf_op jit(solution)/shard_map/pick/pallas_call | solution.py:209
  1.7 11.5 %collective-permute-start = (bf16[2,128,128]{2,1,0:T(8,128)(2,1)S(1)}, bf16[2,128,128]{2,1,0:T(8,128)(2,1)S(1)}, u32[]{:S(2)}, u32[]{:S(2)}) collective-permute-start(bf16[2,128,128]{2,1,0:T(8,128)(2,1)S(1)} %get-tuple-element.17), channel_id=1, source_target_pairs={{2,32},{16,50},{32,2},{50,16},{0,34},{18,48},{34,0},{48,18},{3,51}... | collective-permute-start | bytes 196616 | tf_op jit(solution)/shard_map/ppermute | solution.py:199
  13.2 3.1 %collective-permute-start.1 = (bf16[2,128,128]{2,1,0:T(8,128)(2,1)S(1)}, bf16[2,128,128]{2,1,0:T(8,128)(2,1)S(1)}, u32[]{:S(2)}, u32[]{:S(2)}) collective-permute-start(bf16[2,128,128]{2,1,0:T(8,128)(2,1)S(1)} %get-tuple-element.18), channel_id=1, source_target_pairs={{2,16},{16,2},{32,50},{50,32},{0,18},{18,0},{34,48},{48,34},{3,17}... | collective-permute-start | bytes 196616 | tf_op jit(solution)/shard_map/ppermute | solution.py:199
  16.3 1.4 %prepare.1 = (bf16[2,1024,128]{2,1,0:T(8,128)(2,1)S(1)}, bf16[2,1024,128]{2,1,0:T(8,128)(2,1)S(1)}, s32[8,128]{1,0:T(8,128)S(1)}) custom-call(s32[8]{0:T(128)} %tiles.1, s32[8]{0:T(128)} %text_len.1, bf16[512,512]{1,0:T(8,128)(2,1)} %queries.1, bf16[512,512]{1,0:T(8,128)(2,1)} %d_out.1), custom_call_target="tpu_custom_call" | custom-call | flops 1048576 | bytes 2097152 | tf_op jit(solution)/shard_map/prepare/pallas_call | solution.py:220
  17.7 0.0 collective-permute-done.kv_1
  17.8 4.1 %collective-permute-start.2 = (bf16[2,128,128]{2,1,0:T(8,128)(2,1)S(1)}, bf16[2,128,128]{2,1,0:T(8,128)(2,1)S(1)}, u32[]{:S(2)}, u32[]{:S(2)}) collective-permute-start(bf16[2,128,128]{2,1,0:T(8,128)(2,1)S(1)} %collective-permute-done.kv_1), channel_id=1, source_target_pairs={{0,1},{1,0},{2,3},{3,2},{4,5},{5,4},{6,7},{7,6},{8,9},{9,8},{10,11... | collective-permute-start | bytes 196616 | tf_op jit(solution)/shard_map/ppermute | solution.py:218
  21.8 0.0 collective-permute-done.1.kv_2
  21.8 1.2 %three_blocks.1 = (f32[2,384,1024]{2,1,0:T(8,128)S(1)}, f32[2,384,1024]{2,1,0:T(8,128)S(1)}, f32[2,8,1024]{2,1,0:T(8,128)S(1)}) custom-call(s32[8,128]{1,0:T(8,128)S(1)} %get-tuple-element.19.live_tiles, bf16[2,128,128]{2,1,0:T(8,128)(2,1)S(1)} %get-tuple-element.16.kv_0, bf16[2,128,128]{2,1,0:T(8,128)(2,1)S(1)} %collective-permute-done.kv_1, ...), custom_call_target="tpu_custom_call" | custom-call | flops 5368709120 | bytes 262144 | tf_op jit(solution)/shard_map/three_blocks/pallas_call | solution.py:244
  23.0 0.0 collective-permute-done.2.kv_3
  23.0 2.7 %gradients.1 = (bf16[2,512,1024]{2,1,0:T(8,128)(2,1)S(1)}, bf16[64,16,128]{2,1,0:T(8,128)(2,1)}) custom-call(s32[8,128]{1,0:T(8,128)S(1)} %get-tuple-element.19.live_tiles, f32[2,384,1024]{2,1,0:T(8,128)S(1)} %get-tuple-element.22.expo_1, f32[2,384,1024]{2,1,0:T(8,128)S(1)} %get-tuple-element.23.d_prob_1, f32[2,8,1024]{2,1,0:T(8,128)S(1)} %get-tuple-element.24.stats, ...), custom_call_target="tpu_custom_call" | custom-call | tf_op jit(solution)/shard_map/gradients/pallas_call | solution.py:259
  25.7 10.6 %all-to-all-start = ((bf16[64,16,128]{2,1,0:T(8,128)(2,1)}), bf16[64,16,128]{2,1,0:T(8,128)(2,1)S(1)}, u32[]{:S(2)}, u32[]{:S(2)}) async-start(bf16[64,16,128]{2,1,0:T(8,128)(2,1)} %get-tuple-element.26), calls=%async_computation | async-start | bytes 524288 | tf_op jit(solution)/shard_map/all_to_all | solution.py:273
  37.0 1.3 %query_gradient.1 = bf16[512,512]{1,0:T(8,128)(2,1)} custom-call(f32[1,1]{1,0:T(1,128)} %bitcast.1.gate, bf16[2,128,128]{2,1,0:T(8,128)(2,1)S(1)} %get-tuple-element.16.kv_0, bf16[2,128,128]{2,1,0:T(8,128)(2,1)S(1)} %collective-permute-done.kv_1, bf16[2,128,128]{2,1,0:T(8,128)(2,1)S(1)} %collective-permute-done.1.kv_2, ...), custom_call_target="tpu_custom_call" | custom-call | flops 268435456 | bytes 1048576 | tf_op jit(solution)/shard_map/query_gradient/pallas_call | solution.py:274
  38.3 4.5 %all-to-all-done.pieces = bf16[64,16,128]{2,1,0:T(8,128)(2,1)S(1)} async-done(((bf16[64,16,128]{2,1,0:T(8,128)(2,1)}), bf16[64,16,128]{2,1,0:T(8,128)(2,1)S(1)}, u32[]{:S(2)}, u32[]{:S(2)}) %all-to-all-start) | async-done | bytes 262176 | tf_op jit(solution)/shard_map/all_to_all | solution.py:273
  42.8 0.7 %add_up.1 = (f32[8,1024]{1,0:T(8,128)}, f32[8,1024]{1,0:T(8,128)}) custom-call(f32[1,1]{1,0:T(1,128)} %bitcast.2.gate, bf16[64,16,128]{2,1,0:T(8,128)(2,1)S(1)} %all-to-all-done.pieces), custom_call_target="tpu_custom_call" | custom-call | tf_op jit(solution)/shard_map/add_up/pallas_call | solution.py:285
Async XLA Ops:
  1.7 16.0 %collective-permute-start = (bf16[2,128,128]{2,1,0:T(8,128)(2,1)S(1)}, bf16[2,128,128]{2,1,0:T(8,128)(2,1)S(1)}, u32[]{:S(2)}, u32[]{:S(2)}) collective-permute-start(bf16[2,128,128]{2,1,0:T(8,128)(2,1)S(1)} %get-tuple-element.17), channel_id=1, source_target_pairs={{2,32},{16,50},{32,2},{50,16},{0,34},{18,48},{34,0},{48,18},{3,51}... | collective-permute-start | bytes 196616 | tf_op jit(solution)/shard_map/ppermute | solution.py:199
  13.2 8.6 %collective-permute-start.1 = (bf16[2,128,128]{2,1,0:T(8,128)(2,1)S(1)}, bf16[2,128,128]{2,1,0:T(8,128)(2,1)S(1)}, u32[]{:S(2)}, u32[]{:S(2)}) collective-permute-start(bf16[2,128,128]{2,1,0:T(8,128)(2,1)S(1)} %get-tuple-element.18), channel_id=1, source_target_pairs={{2,16},{16,2},{32,50},{50,32},{0,18},{18,0},{34,48},{48,34},{3,17}... | collective-permute-start | bytes 196616 | tf_op jit(solution)/shard_map/ppermute | solution.py:199
  17.8 5.2 %collective-permute-start.2 = (bf16[2,128,128]{2,1,0:T(8,128)(2,1)S(1)}, bf16[2,128,128]{2,1,0:T(8,128)(2,1)S(1)}, u32[]{:S(2)}, u32[]{:S(2)}) collective-permute-start(bf16[2,128,128]{2,1,0:T(8,128)(2,1)S(1)} %collective-permute-done.kv_1), channel_id=1, source_target_pairs={{0,1},{1,0},{2,3},{3,2},{4,5},{5,4},{6,7},{7,6},{8,9},{9,8},{10,11... | collective-permute-start | bytes 196616 | tf_op jit(solution)/shard_map/ppermute | solution.py:218
  25.7 17.1 %all-to-all-start = ((bf16[64,16,128]{2,1,0:T(8,128)(2,1)}), bf16[64,16,128]{2,1,0:T(8,128)(2,1)S(1)}, u32[]{:S(2)}, u32[]{:S(2)}) async-start(bf16[64,16,128]{2,1,0:T(8,128)(2,1)} %get-tuple-element.26), calls=%async_computation | async-start | bytes 524288 | tf_op jit(solution)/shard_map/all_to_all | solution.py:273

commit v8 on v7

--- a/solution.py
+++ b/solution.py
@@ -14,9 +14,9 @@
 BLOCKS = 4
 HEADS_X = 2
 HEADS_STEP = 2
-PLANE = 64
+CHIPS = 32
 GROUPS = ((1, 2, 4, 7), (0, 3, 5, 6))
-FIRST_ZH, FIRST_IN = 2, 9
+FIRST_ZH, FIRST_IN = 2, 5
 NT = (((1,), (1,)), ((), ()))
 VMEM = pl.BlockSpec(memory_space=pltpu.VMEM)
 HBM = pl.BlockSpec(memory_space=pltpu.HBM)
@@ -116,7 +116,7 @@
 
 
 def main_kernel(
-    live_tiles, expo_1, d_prob_1, stats, kv_3, queries, d_out, d_score, partial, acc_k, acc_v
+    live_tiles, expo_1, d_prob_1, stats, kv_3, queries, d_out, d_score, keep, send, acc_k, acc_v
 ):
     f32, bf16 = jnp.float32, jnp.bfloat16
     live = [place < live_tiles[0:1, 0:1] for place in places()[3:]]
@@ -148,13 +148,21 @@
         else:
             acc_k[...] += term_k
             acc_v[...] += term_v
-    both = [acc.reshape(PLANE, 8, HD) for acc in (acc_k[...], acc_v[...])]
-    both = jnp.concatenate(both, 1).astype(bf16)
-    run = PLANE // BLOCKS
+    both = [acc.reshape(CHIPS, 2, 8, HD) for acc in (acc_k[...], acc_v[...])]
+    both = jnp.concatenate(both, 2)
+    even = lax.axis_index("c") == 0
+    mine, other = jnp.where(even, both[:, 0], both[:, 1]), jnp.where(even, both[:, 1], both[:, 0])
+    other = other.astype(bf16)
+    run = CHIPS // BLOCKS
     for b, place in enumerate(places()):
         for i in range(run):
-            at = lax.bitwise_xor(place, FIRST_ZH) * run + (i ^ FIRST_IN)
-            partial[pl.ds(at, 1)] = both[b * run + i : b * run + i + 1]
+            at = pl.ds(lax.bitwise_xor(place, FIRST_ZH) * run + (i ^ FIRST_IN), 1)
+            keep[at] = mine[b * run + i : b * run + i + 1]
+            send[at] = other[b * run + i : b * run + i + 1]
+
+
+def chip_kernel(keep, other, partial):
+    partial[...] = (keep[...] + other[...].astype(jnp.float32)).astype(jnp.bfloat16)
 
 
 def query_kernel(gate, kv_0, kv_1, kv_2, kv_3, d_score, d_queries):
@@ -171,13 +179,12 @@
 
 def sum_kernel(gate, pieces, d_keys, d_values):
     factor = jnp.tanh(gate[...])
-    heads = PLANE // BLOCKS // 2
+    heads = CHIPS // BLOCKS
     for head in range(heads):
         total = None
         for zh in range(BLOCKS):
-            for c in range(2):
-                piece = pieces[(zh * heads + (head ^ FIRST_IN // 2)) * 2 + c].astype(jnp.float32)
-                total = piece if total is None else total + piece
+            piece = pieces[zh * heads + (head ^ FIRST_IN)].astype(jnp.float32)
+            total = piece if total is None else total + piece
         cols = pl.ds(head * HD, HD)
         d_keys[:, cols] = total[:8] * (factor * SCALE)
         d_values[:, cols] = total[8:] * factor
@@ -256,21 +263,30 @@
         ),
         name="three_blocks",
     )(live_tiles, kv_0, kv_1, kv_2, q, d_live)
-    d_score, partial = pl.pallas_call(
+    d_score, keep, send = pl.pallas_call(
         main_kernel,
         out_shape=(
             pltpu.VMEM((steps, image, rows * HEADS_STEP), bf16),
-            pltpu.VMEM((PLANE, 16, HD), bf16),
+            pltpu.VMEM((CHIPS, 16, HD), f32),
+            pltpu.VMEM((CHIPS, 16, HD), bf16),
         ),
         in_specs=[VMEM] * 7,
-        out_specs=(VMEM, VMEM),
+        out_specs=(VMEM,) * 3,
         scratch_shapes=[pltpu.VMEM((image, HD), f32), pltpu.VMEM((image, HD), f32)],
         compiler_params=pltpu.CompilerParams(vmem_limit_bytes=36 * 2**20),
         name="gradients",
     )(live_tiles, in_vmem(expo), in_vmem(d_prob), in_vmem(stats), kv_3, q, d_live)
-    run = PLANE // BLOCKS
+    other = lax.ppermute(send, "c", [(0, 1), (1, 0)])
+    partial = pl.pallas_call(
+        chip_kernel,
+        out_shape=jax.ShapeDtypeStruct((CHIPS, 16, HD), bf16),
+        in_specs=[VMEM, VMEM],
+        out_specs=VMEM,
+        name="add_cores",
+    )(in_vmem(keep), in_vmem(other))
+    run = CHIPS // BLOCKS
     members = [(zh ^ FIRST_ZH) * run + (i ^ FIRST_IN) for zh in range(BLOCKS) for i in range(run)]
-    pieces = lax.all_to_all(partial, ("zh", "x", "zl", "c"), 0, 0, axis_index_groups=[members])
+    pieces = lax.all_to_all(partial, ("zh", "x", "zl"), 0, 0, axis_index_groups=[members])
     d_queries = pl.pallas_call(
         query_kernel,
         out_shape=jax.ShapeDtypeStruct(queries.shape, bf16),

time: 43.8 us -> 43.1 us (0.984)
  waiting for transfers between devices: 4.54 us -> 3.15 us
  starting transfers between devices: 29.2 us -> 29.8 us
    all_to_all x1, waiting for transfers between devices: 4.53 us -> 2.09 us  [local(): lax.all_to_all(partial, ('zh', 'x', 'zl'), 0, 0, axis_index_groups=[membe...]
    ppermute x0 -> x1, starting transfers between devices: none -> 2.19 us  [local(): other = lax.ppermute(send, 'c', [(0, 1), (1, 0)])]
    all_to_all x1, starting transfers between devices: 10.6 us -> 9.03 us  [local(): lax.all_to_all(partial, ('zh', 'x', 'zl'), 0, 0, axis_index_groups=[membe...]
    ppermute x0 -> x1, waiting for transfers between devices: none -> 1.05 us  [local(): other = lax.ppermute(send, 'c', [(0, 1), (1, 0)])]
    pallas_call x1, Pallas kernels: 2.69 us -> 1.98 us  [local(): pl.pallas_call(main_kernel, out_shape=(pltpu.VMEM((steps, image, rows * H...]
    pallas_call x0 -> x1, Pallas kernels: none -> 0.67 us  [local(): pl.pallas_call(chip_kernel, out_shape=jax.ShapeDtypeStruct((CHIPS, 16, HD...]
  transfers between devices with their start and end apart: 4 -> 5, of which waited for: 1 -> 2; matrix products, arithmetic and copies ran while one was open for 0% -> 0% of each run, Pallas kernels for 9% -> 9%
where the time goes in v8:
time: 43.1 us; the launch traced here: 42.7 us
  starting transfers between devices  29.8 us (69%)
  Pallas kernels  8.37 us (19%)
  waiting for transfers between devices  3.15 us (7%)
  between operations  1.37 us (3%)
    ppermute x2, starting transfers between devices, swap(): return in_vmem(lax.ppermute(value, ('zh', 'zl', 'c'), pairs))  14.6 us
    all_to_all x1, starting transfers between devices, local(): lax.all_to_all(partial, ('zh', 'x', 'zl'), 0, 0, axis_index_groups=[membe...  9.03 us
    ppermute x1, starting transfers between devices, local(): kv_3 = in_vmem(lax.ppermute(kv_1, 'c', [(0, 1), (1, 0)]))  4.05 us
    ppermute x1, starting transfers between devices, local(): other = lax.ppermute(send, 'c', [(0, 1), (1, 0)])  2.19 us
    all_to_all x1, waiting for transfers between devices, local(): lax.all_to_all(partial, ('zh', 'x', 'zl'), 0, 0, axis_index_groups=[membe...  2.09 us
    pallas_call x1, Pallas kernels, local(): pl.pallas_call(main_kernel, out_shape=(pltpu.VMEM((steps, image, rows * H...  1.98 us
    pallas_call x1, Pallas kernels, local(): pl.pallas_call(prepare_kernel, out_shape=(pltpu.VMEM(by_step, bf16), pltp...  1.44 us
    pallas_call x1, Pallas kernels, local(): pl.pallas_call(query_kernel, out_shape=jax.ShapeDtypeStruct(queries.shape...  1.34 us
  transfers between devices with their start and end apart: 5, of which 2 were waited for; matrix products, arithmetic and copies ran while one was open for 0% of the time, Pallas kernels for 9%

profile of v8, /device:TPU:1, one launch (start us, length us, event | category | flops | bytes accessed | tf_op | source)
XLA Modules:
  0.0 42.7 jit_solution(13051269175636143589)
XLA Ops:
  0.6 1.1 %pick.1 = (bf16[2,128,128]{2,1,0:T(8,128)(2,1)S(1)}, bf16[2,128,128]{2,1,0:T(8,128)(2,1)S(1)}, bf16[2,128,128]{2,1,0:T(8,128)(2,1)S(1)}) custom-call(bf16[128,1024]{1,0:T(8,128)(2,1)} %keys.1, bf16[128,1024]{1,0:T(8,128)(2,1)} %values.1), custom_call_target="tpu_custom_call" | custom-call | tf_op jit(solution)/shard_map/pick/pallas_call | solution.py:216
  1.7 11.5 %collective-permute-start = (bf16[2,128,128]{2,1,0:T(8,128)(2,1)S(1)}, bf16[2,128,128]{2,1,0:T(8,128)(2,1)S(1)}, u32[]{:S(2)}, u32[]{:S(2)}) collective-permute-start(bf16[2,128,128]{2,1,0:T(8,128)(2,1)S(1)} %get-tuple-element.18), channel_id=1, source_target_pairs={{2,32},{16,50},{32,2},{50,16},{0,34},{18,48},{34,0},{48,18},{3,51}... | collective-permute-start | bytes 196616 | tf_op jit(solution)/shard_map/ppermute | solution.py:206
  13.2 3.1 %collective-permute-start.1 = (bf16[2,128,128]{2,1,0:T(8,128)(2,1)S(1)}, bf16[2,128,128]{2,1,0:T(8,128)(2,1)S(1)}, u32[]{:S(2)}, u32[]{:S(2)}) collective-permute-start(bf16[2,128,128]{2,1,0:T(8,128)(2,1)S(1)} %get-tuple-element.19), channel_id=1, source_target_pairs={{2,16},{16,2},{32,50},{50,32},{0,18},{18,0},{34,48},{48,34},{3,17}... | collective-permute-start | bytes 196616 | tf_op jit(solution)/shard_map/ppermute | solution.py:206
  16.3 1.4 %prepare.1 = (bf16[2,1024,128]{2,1,0:T(8,128)(2,1)S(1)}, bf16[2,1024,128]{2,1,0:T(8,128)(2,1)S(1)}, s32[8,128]{1,0:T(8,128)S(1)}) custom-call(s32[8]{0:T(128)} %tiles.1, s32[8]{0:T(128)} %text_len.1, bf16[512,512]{1,0:T(8,128)(2,1)} %queries.1, bf16[512,512]{1,0:T(8,128)(2,1)} %d_out.1), custom_call_target="tpu_custom_call" | custom-call | flops 1048576 | bytes 2097152 | tf_op jit(solution)/shard_map/prepare/pallas_call | solution.py:227
  17.7 0.0 collective-permute-done.kv_1
  17.8 4.1 %collective-permute-start.2 = (bf16[2,128,128]{2,1,0:T(8,128)(2,1)S(1)}, bf16[2,128,128]{2,1,0:T(8,128)(2,1)S(1)}, u32[]{:S(2)}, u32[]{:S(2)}) collective-permute-start(bf16[2,128,128]{2,1,0:T(8,128)(2,1)S(1)} %collective-permute-done.kv_1), channel_id=1, source_target_pairs={{0,1},{1,0},{2,3},{3,2},{4,5},{5,4},{6,7},{7,6},{8,9},{9,8},{10,11... | collective-permute-start | bytes 196616 | tf_op jit(solution)/shard_map/ppermute | solution.py:225
  21.8 0.0 collective-permute-done.1.kv_2
  21.8 1.2 %three_blocks.1 = (f32[2,384,1024]{2,1,0:T(8,128)S(1)}, f32[2,384,1024]{2,1,0:T(8,128)S(1)}, f32[2,8,1024]{2,1,0:T(8,128)S(1)}) custom-call(s32[8,128]{1,0:T(8,128)S(1)} %get-tuple-element.20.live_tiles, bf16[2,128,128]{2,1,0:T(8,128)(2,1)S(1)} %get-tuple-element.17.kv_0, bf16[2,128,128]{2,1,0:T(8,128)(2,1)S(1)} %collective-permute-done.kv_1, ...), custom_call_target="tpu_custom_call" | custom-call | flops 5368709120 | bytes 262144 | tf_op jit(solution)/shard_map/three_blocks/pallas_call | solution.py:251
  23.0 0.0 collective-permute-done.2.kv_3
  23.0 2.0 %gradients.1 = (bf16[2,512,1024]{2,1,0:T(8,128)(2,1)S(1)}, f32[32,16,128]{2,1,0:T(8,128)S(1)}, bf16[32,16,128]{2,1,0:T(8,128)(2,1)S(1)}) custom-call(s32[8,128]{1,0:T(8,128)S(1)} %get-tuple-element.20.live_tiles, f32[2,384,1024]{2,1,0:T(8,128)S(1)} %get-tuple-element.23.expo_1, f32[2,384,1024]{2,1,0:T(8,128)S(1)} %get-tuple-element.24.d_prob_1, ...), custom_call_target="tpu_custom_call" | custom-call | tf_op jit(solution)/shard_map/gradients/pallas_call | solution.py:266
  25.0 2.2 %collective-permute-start.3 = (bf16[32,16,128]{2,1,0:T(8,128)(2,1)S(1)}, bf16[32,16,128]{2,1,0:T(8,128)(2,1)S(1)}, u32[]{:S(2)}, u32[]{:S(2)}) collective-permute-start(bf16[32,16,128]{2,1,0:T(8,128)(2,1)S(1)} %get-tuple-element.28), channel_id=1, source_target_pairs={{0,1},{1,0},{2,3},{3,2},{4,5},{5,4},{6,7},{7,6},{8,9},{9,8},{10,11... | collective-permute-start | bytes 393224 | tf_op jit(solution)/shard_map/ppermute | solution.py:279
  27.2 1.0 %collective-permute-done.3.other = bf16[32,16,128]{2,1,0:T(8,128)(2,1)S(1)} collective-permute-done((bf16[32,16,128]{2,1,0:T(8,128)(2,1)S(1)}, bf16[32,16,128]{2,1,0:T(8,128)(2,1)S(1)}, u32[]{:S(2)}, u32[]{:S(2)}) %collective-permute-start.3) | collective-permute-done | bytes 131104 | tf_op jit(solution)/shard_map/ppermute | solution.py:279
  28.2 0.7 %add_cores.1 = bf16[32,16,128]{2,1,0:T(8,128)(2,1)} custom-call(f32[32,16,128]{2,1,0:T(8,128)S(1)} %get-tuple-element.27.keep, bf16[32,16,128]{2,1,0:T(8,128)(2,1)S(1)} %collective-permute-done.3.other), custom_call_target="tpu_custom_call" | custom-call | tf_op jit(solution)/shard_map/add_cores/pallas_call | solution.py:280
  28.9 9.0 %all-to-all-start = ((bf16[32,16,128]{2,1,0:T(8,128)(2,1)}), bf16[32,16,128]{2,1,0:T(8,128)(2,1)S(1)}, u32[]{:S(2)}, u32[]{:S(2)}) async-start(bf16[32,16,128]{2,1,0:T(8,128)(2,1)} %add_cores.1), calls=%async_computation | async-start | bytes 262144 | tf_op jit(solution)/shard_map/all_to_all | solution.py:289
  38.6 1.3 %query_gradient.1 = bf16[512,512]{1,0:T(8,128)(2,1)} custom-call(f32[1,1]{1,0:T(1,128)} %bitcast.1.gate, bf16[2,128,128]{2,1,0:T(8,128)(2,1)S(1)} %get-tuple-element.17.kv_0, bf16[2,128,128]{2,1,0:T(8,128)(2,1)S(1)} %collective-permute-done.kv_1, bf16[2,128,128]{2,1,0:T(8,128)(2,1)S(1)} %collective-permute-done.1.kv_2, ...), custom_call_target="tpu_custom_call" | custom-call | flops 268435456 | bytes 1048576 | tf_op jit(solution)/shard_map/query_gradient/pallas_call | solution.py:290
  39.9 2.1 %all-to-all-done.pieces = bf16[32,16,128]{2,1,0:T(8,128)(2,1)S(1)} async-done(((bf16[32,16,128]{2,1,0:T(8,128)(2,1)}), bf16[32,16,128]{2,1,0:T(8,128)(2,1)S(1)}, u32[]{:S(2)}, u32[]{:S(2)}) %all-to-all-start) | async-done | bytes 131104 | tf_op jit(solution)/shard_map/all_to_all | solution.py:289
  42.0 0.7 %add_up.1 = (f32[8,1024]{1,0:T(8,128)}, f32[8,1024]{1,0:T(8,128)}) custom-call(f32[1,1]{1,0:T(1,128)} %bitcast.2.gate, bf16[32,16,128]{2,1,0:T(8,128)(2,1)S(1)} %all-to-all-done.pieces), custom_call_target="tpu_custom_call" | custom-call | tf_op jit(solution)/shard_map/add_up/pallas_call | solution.py:301
Async XLA Ops:
  1.7 16.0 %collective-permute-start = (bf16[2,128,128]{2,1,0:T(8,128)(2,1)S(1)}, bf16[2,128,128]{2,1,0:T(8,128)(2,1)S(1)}, u32[]{:S(2)}, u32[]{:S(2)}) collective-permute-start(bf16[2,128,128]{2,1,0:T(8,128)(2,1)S(1)} %get-tuple-element.18), channel_id=1, source_target_pairs={{2,32},{16,50},{32,2},{50,16},{0,34},{18,48},{34,0},{48,18},{3,51}... | collective-permute-start | bytes 196616 | tf_op jit(solution)/shard_map/ppermute | solution.py:206
  13.2 8.6 %collective-permute-start.1 = (bf16[2,128,128]{2,1,0:T(8,128)(2,1)S(1)}, bf16[2,128,128]{2,1,0:T(8,128)(2,1)S(1)}, u32[]{:S(2)}, u32[]{:S(2)}) collective-permute-start(bf16[2,128,128]{2,1,0:T(8,128)(2,1)S(1)} %get-tuple-element.19), channel_id=1, source_target_pairs={{2,16},{16,2},{32,50},{50,32},{0,18},{18,0},{34,48},{48,34},{3,17}... | collective-permute-start | bytes 196616 | tf_op jit(solution)/shard_map/ppermute | solution.py:206
  17.8 5.2 %collective-permute-start.2 = (bf16[2,128,128]{2,1,0:T(8,128)(2,1)S(1)}, bf16[2,128,128]{2,1,0:T(8,128)(2,1)S(1)}, u32[]{:S(2)}, u32[]{:S(2)}) collective-permute-start(bf16[2,128,128]{2,1,0:T(8,128)(2,1)S(1)} %collective-permute-done.kv_1), channel_id=1, source_target_pairs={{0,1},{1,0},{2,3},{3,2},{4,5},{5,4},{6,7},{7,6},{8,9},{9,8},{10,11... | collective-permute-start | bytes 196616 | tf_op jit(solution)/shard_map/ppermute | solution.py:225
  25.0 3.2 %collective-permute-start.3 = (bf16[32,16,128]{2,1,0:T(8,128)(2,1)S(1)}, bf16[32,16,128]{2,1,0:T(8,128)(2,1)S(1)}, u32[]{:S(2)}, u32[]{:S(2)}) collective-permute-start(bf16[32,16,128]{2,1,0:T(8,128)(2,1)S(1)} %get-tuple-element.28), channel_id=1, source_target_pairs={{0,1},{1,0},{2,3},{3,2},{4,5},{5,4},{6,7},{7,6},{8,9},{9,8},{10,11... | collective-permute-start | bytes 393224 | tf_op jit(solution)/shard_map/ppermute | solution.py:279
  28.9 13.1 %all-to-all-start = ((bf16[32,16,128]{2,1,0:T(8,128)(2,1)}), bf16[32,16,128]{2,1,0:T(8,128)(2,1)S(1)}, u32[]{:S(2)}, u32[]{:S(2)}) async-start(bf16[32,16,128]{2,1,0:T(8,128)(2,1)} %add_cores.1), calls=%async_computation | async-start | bytes 262144 | tf_op jit(solution)/shard_map/all_to_all | solution.py:289

commit v9 on v8

--- a/solution.py
+++ b/solution.py
@@ -47,7 +47,7 @@
 
 
 def prepare_kernel(
-    tiles, text_len, queries, d_out, q_out, d_live, live_tiles, s_tiles, s_text, q, d, sems
+    tiles, text_len, queries, d_out, gate, q_out, d_live, live_tiles, factor, s_tiles, s_text, q, d, sems
 ):
     pairs = ((d_out, d), (queries, q), (text_len, s_text), (tiles, s_tiles))
     copies = [pltpu.make_async_copy(*pair, sems.at[i]) for i, pair in enumerate(pairs)]
@@ -57,6 +57,7 @@
         copy.wait()
     y, zh = lax.axis_index("y"), lax.axis_index("zh")
     live_tiles[...] = jnp.full(live_tiles.shape, s_tiles[y], jnp.int32)
+    factor[...] = jnp.broadcast_to(jnp.tanh(gate[...]), factor.shape)
     rows, heads = queries.shape[0], queries.shape[1] // HD
     live = lax.broadcasted_iota(jnp.int32, (rows, HD), 0) + zh * rows < s_text[y]
     for h in range(heads):
@@ -161,12 +162,12 @@
             send[at] = other[b * run + i : b * run + i + 1]
 
 
-def chip_kernel(keep, other, partial):
+def chip_kernel(keep, other, _, partial):
     partial[...] = (keep[...] + other[...].astype(jnp.float32)).astype(jnp.bfloat16)
 
 
-def query_kernel(gate, kv_0, kv_1, kv_2, kv_3, d_score, d_queries):
-    factor = jnp.tanh(gate[...]) * SCALE
+def query_kernel(gate_factor, kv_0, kv_1, kv_2, kv_3, d_score, d_queries):
+    factor = gate_factor[0:1, 0:1] * SCALE
     keys_t = stacked((kv_0, kv_1, kv_2, kv_3), 0).T
     rows = d_queries.shape[0]
     for step in range(d_score.shape[0]):
@@ -177,8 +178,8 @@
             d_queries[:, cols] = d_q[i * rows : (i + 1) * rows]
 
 
-def sum_kernel(gate, pieces, d_keys, d_values):
-    factor = jnp.tanh(gate[...])
+def sum_kernel(gate_factor, pieces, d_keys, d_values):
+    factor = gate_factor[0:1]
     heads = CHIPS // BLOCKS
     for head in range(heads):
         total = None
@@ -224,15 +225,16 @@
     kv_0, kv_1, kv_2 = in_vmem(own), swap(first, (2, 3)), swap(second, (1, 1))
     kv_3 = in_vmem(lax.ppermute(kv_1, "c", [(0, 1), (1, 0)]))
     by_step = (steps, rows * HEADS_STEP, HD)
-    q, d_live, live_tiles = pl.pallas_call(
+    q, d_live, live_tiles, factor = pl.pallas_call(
         prepare_kernel,
         out_shape=(
             pltpu.VMEM(by_step, bf16),
             pltpu.VMEM(by_step, bf16),
             pltpu.VMEM((8, HD), jnp.int32),
-        ),
-        in_specs=[HBM] * 4,
-        out_specs=(VMEM,) * 3,
+            pltpu.VMEM((8, HD), f32),
+        ),
+        in_specs=[HBM] * 4 + [VMEM],
+        out_specs=(VMEM,) * 4,
         scratch_shapes=[
             pltpu.SMEM(tiles.shape, jnp.int32),
             pltpu.SMEM(text_len.shape, jnp.int32),
@@ -245,8 +247,8 @@
             flops=4 * rows * width_q, bytes_accessed=8 * rows * width_q, transcendentals=0
         ),
         name="prepare",
-    )(*(in_hbm(array) for array in (tiles, text_len, queries, d_out)))
-    q, d_live, live_tiles = in_vmem(q), in_vmem(d_live), in_vmem(live_tiles)
+    )(*(in_hbm(array) for array in (tiles, text_len, queries, d_out)), gate)
+    q, d_live, live_tiles, factor = (in_vmem(array) for array in (q, d_live, live_tiles, factor))
     by_part = (steps, image - block, rows * HEADS_STEP)
     expo, d_prob, stats = pl.pallas_call(
         first_kernel,
@@ -277,16 +279,6 @@
         name="gradients",
     )(live_tiles, in_vmem(expo), in_vmem(d_prob), in_vmem(stats), kv_3, q, d_live)
     other = lax.ppermute(send, "c", [(0, 1), (1, 0)])
-    partial = pl.pallas_call(
-        chip_kernel,
-        out_shape=jax.ShapeDtypeStruct((CHIPS, 16, HD), bf16),
-        in_specs=[VMEM, VMEM],
-        out_specs=VMEM,
-        name="add_cores",
-    )(in_vmem(keep), in_vmem(other))
-    run = CHIPS // BLOCKS
-    members = [(zh ^ FIRST_ZH) * run + (i ^ FIRST_IN) for zh in range(BLOCKS) for i in range(run)]
-    pieces = lax.all_to_all(partial, ("zh", "x", "zl"), 0, 0, axis_index_groups=[members])
     d_queries = pl.pallas_call(
         query_kernel,
         out_shape=jax.ShapeDtypeStruct(queries.shape, bf16),
@@ -297,14 +289,24 @@
             flops=2 * rows * width_q * image, bytes_accessed=4 * rows * width_q, transcendentals=0
         ),
         name="query_gradient",
-    )(gate, kv_0, kv_1, kv_2, kv_3, in_vmem(d_score))
+    )(factor, kv_0, kv_1, kv_2, kv_3, in_vmem(d_score))
+    partial = pl.pallas_call(
+        chip_kernel,
+        out_shape=pltpu.VMEM((CHIPS, 16, HD), bf16),
+        in_specs=[VMEM, VMEM, HBM],
+        out_specs=VMEM,
+        name="add_cores",
+    )(in_vmem(keep), in_vmem(other), in_hbm(d_queries))
+    run = CHIPS // BLOCKS
+    members = [(zh ^ FIRST_ZH) * run + (i ^ FIRST_IN) for zh in range(BLOCKS) for i in range(run)]
+    pieces = lax.all_to_all(partial, ("zh", "x", "zl"), 0, 0, axis_index_groups=[members])
     d_keys, d_values = pl.pallas_call(
         sum_kernel,
         out_shape=(jax.ShapeDtypeStruct((8, width), f32),) * 2,
         in_specs=[VMEM, VMEM],
         out_specs=(VMEM, VMEM),
         name="add_up",
-    )(gate, in_vmem(pieces))
+    )(factor, in_vmem(pieces))
     return d_queries, d_keys, d_values
 
 

time: 43.1 us -> 43 us (level)
  blocking collectives: 0 us -> 12.7 us
  starting transfers between devices: 29.8 us -> 20.6 us
  waiting for transfers between devices: 3.15 us -> 0.01 us
  Pallas kernels: 8.37 us -> 7.74 us
    all_to_all x0 -> x1, blocking collectives: none -> 12.7 us  [local(): lax.all_to_all(partial, ('zh', 'x', 'zl'), 0, 0, axis_index_groups=[membe...]
    all_to_all x1 -> x0, starting transfers between devices: 9.03 us -> none  [local(): lax.all_to_all(partial, ('zh', 'x', 'zl'), 0, 0, axis_index_groups=[membe...]
    all_to_all x1 -> x0, waiting for transfers between devices: 2.09 us -> none  [local(): lax.all_to_all(partial, ('zh', 'x', 'zl'), 0, 0, axis_index_groups=[membe...]
    ppermute x1, waiting for transfers between devices: 1.05 us -> 0.01 us  [local(): other = lax.ppermute(send, 'c', [(0, 1), (1, 0)])]
    pallas_call x1, Pallas kernels: 0.67 us -> 0.03 us  [local(): pl.pallas_call(chip_kernel, out_shape=pltpu.VMEM((CHIPS, 16, HD), bf16),...]
  transfers between devices with their start and end apart: 5 -> 4, of which waited for: 2 -> 0; matrix products, arithmetic and copies ran while one was open for 0% -> 0% of each run, Pallas kernels for 9% -> 9%
where the time goes in v9:
time: 43 us; the launch traced here: 42.4 us
  starting transfers between devices  20.6 us (48%)
  blocking collectives  12.7 us (30%)
  Pallas kernels  7.74 us (18%)
  between operations  1.37 us (3%)
    ppermute x2, starting transfers between devices, swap(): return in_vmem(lax.ppermute(value, ('zh', 'zl', 'c'), pairs))  14.6 us
    all_to_all x1, blocking collectives, local(): lax.all_to_all(partial, ('zh', 'x', 'zl'), 0, 0, axis_index_groups=[membe...  12.7 us
    ppermute x1, starting transfers between devices, local(): kv_3 = in_vmem(lax.ppermute(kv_1, 'c', [(0, 1), (1, 0)]))  4.05 us
    pallas_call x1, Pallas kernels, local(): pl.pallas_call(main_kernel, out_shape=(pltpu.VMEM((steps, image, rows * H...  1.98 us
    ppermute x1, starting transfers between devices, local(): other = lax.ppermute(send, 'c', [(0, 1), (1, 0)])  1.95 us
    pallas_call x1, Pallas kernels, local(): pl.pallas_call(prepare_kernel, out_shape=(pltpu.VMEM(by_step, bf16), pltp...  1.51 us
    pallas_call x1, Pallas kernels, local(): pl.pallas_call(query_kernel, out_shape=jax.ShapeDtypeStruct(queries.shape...  1.34 us
    pallas_call x1, Pallas kernels, local(): pl.pallas_call(first_kernel, out_shape=(pltpu.VMEM(by_part, f32), pltpu.V...  1.16 us
  transfers between devices with their start and end apart: 4, of which 0 were waited for; matrix products, arithmetic and copies ran while one was open for 0% of the time, Pallas kernels for 9%

profile of v9, /device:TPU:1, one launch (start us, length us, event | category | flops | bytes accessed | tf_op | source)
XLA Modules:
  0.0 42.4 jit_solution(13032895493711992453)
XLA Ops:
  0.6 1.1 %pick.1 = (bf16[2,128,128]{2,1,0:T(8,128)(2,1)S(1)}, bf16[2,128,128]{2,1,0:T(8,128)(2,1)S(1)}, bf16[2,128,128]{2,1,0:T(8,128)(2,1)S(1)}) custom-call(bf16[128,1024]{1,0:T(8,128)(2,1)} %keys.1, bf16[128,1024]{1,0:T(8,128)(2,1)} %values.1), custom_call_target="tpu_custom_call" | custom-call | tf_op jit(solution)/shard_map/pick/pallas_call | solution.py:217
  1.7 11.5 %collective-permute-start = (bf16[2,128,128]{2,1,0:T(8,128)(2,1)S(1)}, bf16[2,128,128]{2,1,0:T(8,128)(2,1)S(1)}, u32[]{:S(2)}, u32[]{:S(2)}) collective-permute-start(bf16[2,128,128]{2,1,0:T(8,128)(2,1)S(1)} %get-tuple-element.20), channel_id=1, source_target_pairs={{2,32},{16,50},{32,2},{50,16},{0,34},{18,48},{34,0},{48,18},{3,51}... | collective-permute-start | bytes 196616 | tf_op jit(solution)/shard_map/ppermute | solution.py:207
  13.2 3.1 %collective-permute-start.1 = (bf16[2,128,128]{2,1,0:T(8,128)(2,1)S(1)}, bf16[2,128,128]{2,1,0:T(8,128)(2,1)S(1)}, u32[]{:S(2)}, u32[]{:S(2)}) collective-permute-start(bf16[2,128,128]{2,1,0:T(8,128)(2,1)S(1)} %get-tuple-element.21), channel_id=1, source_target_pairs={{2,16},{16,2},{32,50},{50,32},{0,18},{18,0},{34,48},{48,34},{3,17}... | collective-permute-start | bytes 196616 | tf_op jit(solution)/shard_map/ppermute | solution.py:207
  16.9 1.5 %prepare.1 = (bf16[2,1024,128]{2,1,0:T(8,128)(2,1)S(1)}, bf16[2,1024,128]{2,1,0:T(8,128)(2,1)S(1)}, s32[8,128]{1,0:T(8,128)S(1)}, f32[8,128]{1,0:T(8,128)S(1)}) custom-call(s32[8]{0:T(128)} %tiles.1, s32[8]{0:T(128)} %text_len.1, bf16[512,512]{1,0:T(8,128)(2,1)} %queries.1, bf16[512,512]{1,0:T(8,128)(2,1)} %d_out.1, f32[1,1]{1,0:T(1,128)} %bitcast.1.gate), custom_call_target="tpu_custom_call" | custom-call | flops 1048576 | bytes 2097152 | tf_op jit(solution)/shard_map/prepare/pallas_call | solution.py:228
  18.5 0.0 collective-permute-done.kv_1
  18.5 4.1 %collective-permute-start.2 = (bf16[2,128,128]{2,1,0:T(8,128)(2,1)S(1)}, bf16[2,128,128]{2,1,0:T(8,128)(2,1)S(1)}, u32[]{:S(2)}, u32[]{:S(2)}) collective-permute-start(bf16[2,128,128]{2,1,0:T(8,128)(2,1)S(1)} %collective-permute-done.kv_1), channel_id=1, source_target_pairs={{0,1},{1,0},{2,3},{3,2},{4,5},{5,4},{6,7},{7,6},{8,9},{9,8},{10,11... | collective-permute-start | bytes 196616 | tf_op jit(solution)/shard_map/ppermute | solution.py:226
  22.5 0.0 collective-permute-done.1.kv_2
  22.5 1.2 %three_blocks.1 = (f32[2,384,1024]{2,1,0:T(8,128)S(1)}, f32[2,384,1024]{2,1,0:T(8,128)S(1)}, f32[2,8,1024]{2,1,0:T(8,128)S(1)}) custom-call(s32[8,128]{1,0:T(8,128)S(1)} %get-tuple-element.22.live_tiles, bf16[2,128,128]{2,1,0:T(8,128)(2,1)S(1)} %get-tuple-element.19.kv_0, bf16[2,128,128]{2,1,0:T(8,128)(2,1)S(1)} %collective-permute-done.kv_1, ...), custom_call_target="tpu_custom_call" | custom-call | flops 5368709120 | bytes 262144 | tf_op jit(solution)/shard_map/three_blocks/pallas_call | solution.py:253
  23.7 0.0 collective-permute-done.2.kv_3
  23.7 2.0 %gradients.1 = (bf16[2,512,1024]{2,1,0:T(8,128)(2,1)S(1)}, f32[32,16,128]{2,1,0:T(8,128)S(1)}, bf16[32,16,128]{2,1,0:T(8,128)(2,1)S(1)}) custom-call(s32[8,128]{1,0:T(8,128)S(1)} %get-tuple-element.22.live_tiles, f32[2,384,1024]{2,1,0:T(8,128)S(1)} %get-tuple-element.25.expo_1, f32[2,384,1024]{2,1,0:T(8,128)S(1)} %get-tuple-element.26.d_prob_1, ...), custom_call_target="tpu_custom_call" | custom-call | tf_op jit(solution)/shard_map/gradients/pallas_call | solution.py:268
  25.7 2.0 %collective-permute-start.3 = (bf16[32,16,128]{2,1,0:T(8,128)(2,1)S(1)}, bf16[32,16,128]{2,1,0:T(8,128)(2,1)S(1)}, u32[]{:S(2)}, u32[]{:S(2)}) collective-permute-start(bf16[32,16,128]{2,1,0:T(8,128)(2,1)S(1)} %get-tuple-element.30), channel_id=1, source_target_pairs={{0,1},{1,0},{2,3},{3,2},{4,5},{5,4},{6,7},{7,6},{8,9},{9,8},{10,11... | collective-permute-start | bytes 393224 | tf_op jit(solution)/shard_map/ppermute | solution.py:281
  27.7 1.3 %query_gradient.1._ = bf16[512,512]{1,0:T(8,128)(2,1)} custom-call(f32[8,128]{1,0:T(8,128)S(1)} %get-tuple-element.18.gate_factor, bf16[2,128,128]{2,1,0:T(8,128)(2,1)S(1)} %get-tuple-element.19.kv_0, bf16[2,128,128]{2,1,0:T(8,128)(2,1)S(1)} %collective-permute-done.kv_1, bf16[2,128,128]{2,1,0:T(8,128)(2,1)S(1)} %collective-permute-done.1.kv_2, ...), custom_call_target="tpu_custom_call" | custom-call | flops 268435456 | bytes 1048576 | tf_op jit(solution)/shard_map/query_gradient/pallas_call | solution.py:282
  29.0 0.0 collective-permute-done.3.other
  29.0 12.7 %all_to_all.5.pieces = bf16[32,16,128]{2,1,0:T(8,128)(2,1)S(1)} all-to-all(bf16[32,16,128]{2,1,0:T(8,128)(2,1)S(1)} %add_cores.1), channel_id=1, replica_groups={{42,40,46,44,34,32,38,36,58,56,62,60,50,48,54,52,10,8,14,12,2,0,6,4,26,..., dimensions={0} | all-to-all | bytes 262144 | tf_op jit(solution)/shard_map/all_to_all | solution.py:302
  41.7 0.6 %add_up.1 = (f32[8,1024]{1,0:T(8,128)}, f32[8,1024]{1,0:T(8,128)}) custom-call(f32[8,128]{1,0:T(8,128)S(1)} %get-tuple-element.18.gate_factor, bf16[32,16,128]{2,1,0:T(8,128)(2,1)S(1)} %all_to_all.5.pieces), custom_call_target="tpu_custom_call" | custom-call | tf_op jit(solution)/shard_map/add_up/pallas_call | solution.py:303
  (1 shorter events, 0.0 us)
Async XLA Ops:
  1.7 16.7 %collective-permute-start = (bf16[2,128,128]{2,1,0:T(8,128)(2,1)S(1)}, bf16[2,128,128]{2,1,0:T(8,128)(2,1)S(1)}, u32[]{:S(2)}, u32[]{:S(2)}) collective-permute-start(bf16[2,128,128]{2,1,0:T(8,128)(2,1)S(1)} %get-tuple-element.20), channel_id=1, source_target_pairs={{2,32},{16,50},{32,2},{50,16},{0,34},{18,48},{34,0},{48,18},{3,51}... | collective-permute-start | bytes 196616 | tf_op jit(solution)/shard_map/ppermute | solution.py:207
  13.2 9.3 %collective-permute-start.1 = (bf16[2,128,128]{2,1,0:T(8,128)(2,1)S(1)}, bf16[2,128,128]{2,1,0:T(8,128)(2,1)S(1)}, u32[]{:S(2)}, u32[]{:S(2)}) collective-permute-start(bf16[2,128,128]{2,1,0:T(8,128)(2,1)S(1)} %get-tuple-element.21), channel_id=1, source_target_pairs={{2,16},{16,2},{32,50},{50,32},{0,18},{18,0},{34,48},{48,34},{3,17}... | collective-permute-start | bytes 196616 | tf_op jit(solution)/shard_map/ppermute | solution.py:207
  18.5 5.2 %collective-permute-start.2 = (bf16[2,128,128]{2,1,0:T(8,128)(2,1)S(1)}, bf16[2,128,128]{2,1,0:T(8,128)(2,1)S(1)}, u32[]{:S(2)}, u32[]{:S(2)}) collective-permute-start(bf16[2,128,128]{2,1,0:T(8,128)(2,1)S(1)} %collective-permute-done.kv_1), channel_id=1, source_target_pairs={{0,1},{1,0},{2,3},{3,2},{4,5},{5,4},{6,7},{7,6},{8,9},{9,8},{10,11... | collective-permute-start | bytes 196616 | tf_op jit(solution)/shard_map/ppermute | solution.py:226
  25.7 3.3 %collective-permute-start.3 = (bf16[32,16,128]{2,1,0:T(8,128)(2,1)S(1)}, bf16[32,16,128]{2,1,0:T(8,128)(2,1)S(1)}, u32[]{:S(2)}, u32[]{:S(2)}) collective-permute-start(bf16[32,16,128]{2,1,0:T(8,128)(2,1)S(1)} %get-tuple-element.30), channel_id=1, source_target_pairs={{0,1},{1,0},{2,3},{3,2},{4,5},{5,4},{6,7},{7,6},{8,9},{9,8},{10,11... | collective-permute-start | bytes 393224 | tf_op jit(solution)/shard_map/ppermute | solution.py:281

commit v10 on v9

--- a/solution.py
+++ b/solution.py
@@ -23,7 +23,7 @@
 
 
 def partner(zh, c):
-    return lax.bitwise_xor(zh, 2 + c)
+    return lax.bitwise_xor(zh, 3 - c)
 
 
 def end_of(zh):
@@ -222,7 +222,7 @@
         scratch_shapes=[pltpu.VMEM((2, block, width), bf16), pltpu.SemaphoreType.DMA((2,))],
         name="pick",
     )(in_hbm(keys), in_hbm(values))
-    kv_0, kv_1, kv_2 = in_vmem(own), swap(first, (2, 3)), swap(second, (1, 1))
+    kv_0, kv_1, kv_2 = in_vmem(own), swap(first, (3, 2)), swap(second, (1, 1))
     kv_3 = in_vmem(lax.ppermute(kv_1, "c", [(0, 1), (1, 0)]))
     by_step = (steps, rows * HEADS_STEP, HD)
     q, d_live, live_tiles, factor = pl.pallas_call(

time: 43 us -> 42.6 us (level)
  starting transfers between devices: 20.6 us -> 20.1 us
    ppermute x1, starting transfers between devices: 4.05 us -> 2.23 us  [local(): kv_3 = in_vmem(lax.ppermute(kv_1, 'c', [(0, 1), (1, 0)]))]
    ppermute x2, starting transfers between devices: 14.6 us -> 15.5 us  [swap(): return in_vmem(lax.ppermute(value, ('zh', 'zl', 'c'), pairs))]
    ppermute x1, starting transfers between devices: 1.95 us -> 2.39 us  [local(): other = lax.ppermute(send, 'c', [(0, 1), (1, 0)])]
where the time goes in v10:
time: 42.6 us; the launch traced here: 42.4 us
  starting transfers between devices  20.1 us (47%)
  blocking collectives  13.1 us (31%)
  Pallas kernels  7.74 us (18%)
  between operations  1.37 us (3%)
    ppermute x2, starting transfers between devices, swap(): return in_vmem(lax.ppermute(value, ('zh', 'zl', 'c'), pairs))  15.5 us
    all_to_all x1, blocking collectives, local(): lax.all_to_all(partial, ('zh', 'x', 'zl'), 0, 0, axis_index_groups=[membe...  13.1 us
    ppermute x1, starting transfers between devices, local(): other = lax.ppermute(send, 'c', [(0, 1), (1, 0)])  2.39 us
    ppermute x1, starting transfers between devices, local(): kv_3 = in_vmem(lax.ppermute(kv_1, 'c', [(0, 1), (1, 0)]))  2.23 us
    pallas_call x1, Pallas kernels, local(): pl.pallas_call(main_kernel, out_shape=(pltpu.VMEM((steps, image, rows * H...  1.98 us
    pallas_call x1, Pallas kernels, local(): pl.pallas_call(prepare_kernel, out_shape=(pltpu.VMEM(by_step, bf16), pltp...  1.51 us
    pallas_call x1, Pallas kernels, local(): pl.pallas_call(query_kernel, out_shape=jax.ShapeDtypeStruct(queries.shape...  1.34 us
    pallas_call x1, Pallas kernels, local(): pl.pallas_call(first_kernel, out_shape=(pltpu.VMEM(by_part, f32), pltpu.V...  1.16 us
  transfers between devices with their start and end apart: 4, of which 0 were waited for; matrix products, arithmetic and copies ran while one was open for 0% of the time, Pallas kernels for 9%

profile of v10, /device:TPU:1, one launch (start us, length us, event | category | flops | bytes accessed | tf_op | source)
XLA Modules:
  0.0 42.4 jit_solution(8975016102627784588)
XLA Ops:
  0.6 1.1 %pick.1 = (bf16[2,128,128]{2,1,0:T(8,128)(2,1)S(1)}, bf16[2,128,128]{2,1,0:T(8,128)(2,1)S(1)}, bf16[2,128,128]{2,1,0:T(8,128)(2,1)S(1)}) custom-call(bf16[128,1024]{1,0:T(8,128)(2,1)} %keys.1, bf16[128,1024]{1,0:T(8,128)(2,1)} %values.1), custom_call_target="tpu_custom_call" | custom-call | tf_op jit(solution)/shard_map/pick/pallas_call | solution.py:217
  1.7 11.5 %collective-permute-start = (bf16[2,128,128]{2,1,0:T(8,128)(2,1)S(1)}, bf16[2,128,128]{2,1,0:T(8,128)(2,1)S(1)}, u32[]{:S(2)}, u32[]{:S(2)}) collective-permute-start(bf16[2,128,128]{2,1,0:T(8,128)(2,1)S(1)} %get-tuple-element.20), channel_id=1, source_target_pairs={{2,50},{16,32},{32,16},{50,2},{0,48},{18,34},{34,18},{48,0},{3,33}... | collective-permute-start | bytes 196616 | tf_op jit(solution)/shard_map/ppermute | solution.py:207
  13.2 4.0 %collective-permute-start.1 = (bf16[2,128,128]{2,1,0:T(8,128)(2,1)S(1)}, bf16[2,128,128]{2,1,0:T(8,128)(2,1)S(1)}, u32[]{:S(2)}, u32[]{:S(2)}) collective-permute-start(bf16[2,128,128]{2,1,0:T(8,128)(2,1)S(1)} %get-tuple-element.21), channel_id=1, source_target_pairs={{2,16},{16,2},{32,50},{50,32},{0,18},{18,0},{34,48},{48,34},{3,17}... | collective-permute-start | bytes 196616 | tf_op jit(solution)/shard_map/ppermute | solution.py:207
  17.9 1.5 %prepare.1 = (bf16[2,1024,128]{2,1,0:T(8,128)(2,1)S(1)}, bf16[2,1024,128]{2,1,0:T(8,128)(2,1)S(1)}, s32[8,128]{1,0:T(8,128)S(1)}, f32[8,128]{1,0:T(8,128)S(1)}) custom-call(s32[8]{0:T(128)} %tiles.1, s32[8]{0:T(128)} %text_len.1, bf16[512,512]{1,0:T(8,128)(2,1)} %queries.1, bf16[512,512]{1,0:T(8,128)(2,1)} %d_out.1, f32[1,1]{1,0:T(1,128)} %bitcast.1.gate), custom_call_target="tpu_custom_call" | custom-call | flops 1048576 | bytes 2097152 | tf_op jit(solution)/shard_map/prepare/pallas_call | solution.py:228
  19.4 0.0 collective-permute-done.kv_1
  19.4 2.2 %collective-permute-start.2 = (bf16[2,128,128]{2,1,0:T(8,128)(2,1)S(1)}, bf16[2,128,128]{2,1,0:T(8,128)(2,1)S(1)}, u32[]{:S(2)}, u32[]{:S(2)}) collective-permute-start(bf16[2,128,128]{2,1,0:T(8,128)(2,1)S(1)} %collective-permute-done.kv_1), channel_id=1, source_target_pairs={{0,1},{1,0},{2,3},{3,2},{4,5},{5,4},{6,7},{7,6},{8,9},{9,8},{10,11... | collective-permute-start | bytes 196616 | tf_op jit(solution)/shard_map/ppermute | solution.py:226
  21.6 0.0 collective-permute-done.1.kv_2
  21.6 1.2 %three_blocks.1 = (f32[2,384,1024]{2,1,0:T(8,128)S(1)}, f32[2,384,1024]{2,1,0:T(8,128)S(1)}, f32[2,8,1024]{2,1,0:T(8,128)S(1)}) custom-call(s32[8,128]{1,0:T(8,128)S(1)} %get-tuple-element.22.live_tiles, bf16[2,128,128]{2,1,0:T(8,128)(2,1)S(1)} %get-tuple-element.19.kv_0, bf16[2,128,128]{2,1,0:T(8,128)(2,1)S(1)} %collective-permute-done.kv_1, ...), custom_call_target="tpu_custom_call" | custom-call | flops 5368709120 | bytes 262144 | tf_op jit(solution)/shard_map/three_blocks/pallas_call | solution.py:253
  22.8 0.0 collective-permute-done.2.kv_3
  22.8 2.0 %gradients.1 = (bf16[2,512,1024]{2,1,0:T(8,128)(2,1)S(1)}, f32[32,16,128]{2,1,0:T(8,128)S(1)}, bf16[32,16,128]{2,1,0:T(8,128)(2,1)S(1)}) custom-call(s32[8,128]{1,0:T(8,128)S(1)} %get-tuple-element.22.live_tiles, f32[2,384,1024]{2,1,0:T(8,128)S(1)} %get-tuple-element.25.expo_1, f32[2,384,1024]{2,1,0:T(8,128)S(1)} %get-tuple-element.26.d_prob_1, ...), custom_call_target="tpu_custom_call" | custom-call | tf_op jit(solution)/shard_map/gradients/pallas_call | solution.py:268
  24.8 2.4 %collective-permute-start.3 = (bf16[32,16,128]{2,1,0:T(8,128)(2,1)S(1)}, bf16[32,16,128]{2,1,0:T(8,128)(2,1)S(1)}, u32[]{:S(2)}, u32[]{:S(2)}) collective-permute-start(bf16[32,16,128]{2,1,0:T(8,128)(2,1)S(1)} %get-tuple-element.30), channel_id=1, source_target_pairs={{0,1},{1,0},{2,3},{3,2},{4,5},{5,4},{6,7},{7,6},{8,9},{9,8},{10,11... | collective-permute-start | bytes 393224 | tf_op jit(solution)/shard_map/ppermute | solution.py:281
  27.2 1.3 %query_gradient.1._ = bf16[512,512]{1,0:T(8,128)(2,1)} custom-call(f32[8,128]{1,0:T(8,128)S(1)} %get-tuple-element.18.gate_factor, bf16[2,128,128]{2,1,0:T(8,128)(2,1)S(1)} %get-tuple-element.19.kv_0, bf16[2,128,128]{2,1,0:T(8,128)(2,1)S(1)} %collective-permute-done.kv_1, bf16[2,128,128]{2,1,0:T(8,128)(2,1)S(1)} %collective-permute-done.1.kv_2, ...), custom_call_target="tpu_custom_call" | custom-call | flops 268435456 | bytes 1048576 | tf_op jit(solution)/shard_map/query_gradient/pallas_call | solution.py:282
  28.5 0.0 collective-permute-done.3.other
  28.6 13.1 %all_to_all.5.pieces = bf16[32,16,128]{2,1,0:T(8,128)(2,1)S(1)} all-to-all(bf16[32,16,128]{2,1,0:T(8,128)(2,1)S(1)} %add_cores.1), channel_id=1, replica_groups={{42,40,46,44,34,32,38,36,58,56,62,60,50,48,54,52,10,8,14,12,2,0,6,4,26,..., dimensions={0} | all-to-all | bytes 262144 | tf_op jit(solution)/shard_map/all_to_all | solution.py:302
  41.7 0.6 %add_up.1 = (f32[8,1024]{1,0:T(8,128)}, f32[8,1024]{1,0:T(8,128)}) custom-call(f32[8,128]{1,0:T(8,128)S(1)} %get-tuple-element.18.gate_factor, bf16[32,16,128]{2,1,0:T(8,128)(2,1)S(1)} %all_to_all.5.pieces), custom_call_target="tpu_custom_call" | custom-call | tf_op jit(solution)/shard_map/add_up/pallas_call | solution.py:303
  (1 shorter events, 0.0 us)
Async XLA Ops:
  1.7 17.7 %collective-permute-start = (bf16[2,128,128]{2,1,0:T(8,128)(2,1)S(1)}, bf16[2,128,128]{2,1,0:T(8,128)(2,1)S(1)}, u32[]{:S(2)}, u32[]{:S(2)}) collective-permute-start(bf16[2,128,128]{2,1,0:T(8,128)(2,1)S(1)} %get-tuple-element.20), channel_id=1, source_target_pairs={{2,50},{16,32},{32,16},{50,2},{0,48},{18,34},{34,18},{48,0},{3,33}... | collective-permute-start | bytes 196616 | tf_op jit(solution)/shard_map/ppermute | solution.py:207
  13.2 8.4 %collective-permute-start.1 = (bf16[2,128,128]{2,1,0:T(8,128)(2,1)S(1)}, bf16[2,128,128]{2,1,0:T(8,128)(2,1)S(1)}, u32[]{:S(2)}, u32[]{:S(2)}) collective-permute-start(bf16[2,128,128]{2,1,0:T(8,128)(2,1)S(1)} %get-tuple-element.21), channel_id=1, source_target_pairs={{2,16},{16,2},{32,50},{50,32},{0,18},{18,0},{34,48},{48,34},{3,17}... | collective-permute-start | bytes 196616 | tf_op jit(solution)/shard_map/ppermute | solution.py:207
  19.4 3.4 %collective-permute-start.2 = (bf16[2,128,128]{2,1,0:T(8,128)(2,1)S(1)}, bf16[2,128,128]{2,1,0:T(8,128)(2,1)S(1)}, u32[]{:S(2)}, u32[]{:S(2)}) collective-permute-start(bf16[2,128,128]{2,1,0:T(8,128)(2,1)S(1)} %collective-permute-done.kv_1), channel_id=1, source_target_pairs={{0,1},{1,0},{2,3},{3,2},{4,5},{5,4},{6,7},{7,6},{8,9},{9,8},{10,11... | collective-permute-start | bytes 196616 | tf_op jit(solution)/shard_map/ppermute | solution.py:226
  24.8 3.7 %collective-permute-start.3 = (bf16[32,16,128]{2,1,0:T(8,128)(2,1)S(1)}, bf16[32,16,128]{2,1,0:T(8,128)(2,1)S(1)}, u32[]{:S(2)}, u32[]{:S(2)}) collective-permute-start(bf16[32,16,128]{2,1,0:T(8,128)(2,1)S(1)} %get-tuple-element.30), channel_id=1, source_target_pairs={{0,1},{1,0},{2,3},{3,2},{4,5},{5,4},{6,7},{7,6},{8,9},{9,8},{10,11... | collective-permute-start | bytes 393224 | tf_op jit(solution)/shard_map/ppermute | solution.py:281

commit v11 on v10

--- a/solution.py
+++ b/solution.py
@@ -166,16 +166,22 @@
     partial[...] = (keep[...] + other[...].astype(jnp.float32)).astype(jnp.bfloat16)
 
 
-def query_kernel(gate_factor, kv_0, kv_1, kv_2, kv_3, d_score, d_queries):
+def query_kernel(gate_factor, kv_0, kv_1, kv_2, kv_3, d_score, d_queries, result, sems):
     factor = gate_factor[0:1, 0:1] * SCALE
     keys_t = stacked((kv_0, kv_1, kv_2, kv_3), 0).T
     rows = d_queries.shape[0]
+    copies = []
     for step in range(d_score.shape[0]):
         d_q = jnp.dot(keys_t, d_score[step], preferred_element_type=jnp.float32)
         d_q = (d_q * factor).T.astype(jnp.bfloat16)
         for i in range(HEADS_STEP):
             cols = pl.ds((step * HEADS_STEP + i) * HD, HD)
-            d_queries[:, cols] = d_q[i * rows : (i + 1) * rows]
+            result[:, cols] = d_q[i * rows : (i + 1) * rows]
+        cols = pl.ds(step * HEADS_STEP * HD, HEADS_STEP * HD)
+        copies.append(pltpu.make_async_copy(result.at[:, cols], d_queries.at[:, cols], sems.at[step]))
+        copies[-1].start()
+    for copy in copies:
+        copy.wait()
 
 
 def sum_kernel(gate_factor, pieces, d_keys, d_values):
@@ -283,7 +289,8 @@
         query_kernel,
         out_shape=jax.ShapeDtypeStruct(queries.shape, bf16),
         in_specs=[VMEM] * 6,
-        out_specs=VMEM,
+        out_specs=HBM,
+        scratch_shapes=[pltpu.VMEM(queries.shape, bf16), pltpu.SemaphoreType.DMA((steps,))],
         compiler_params=pltpu.CompilerParams(vmem_limit_bytes=16 * 2**20),
         cost_estimate=pl.CostEstimate(
             flops=2 * rows * width_q * image, bytes_accessed=4 * rows * width_q, transcendentals=0

time: 42.6 us -> 42.6 us (level)
  no operation moved by 1% of the time
where the time goes in v11:
time: 42.6 us; the launch traced here: 42.3 us
  starting transfers between devices  20.1 us (47%)
  blocking collectives  13.1 us (31%)
  Pallas kernels  7.67 us (18%)
  between operations  1.38 us (3%)
    ppermute x2, starting transfers between devices, swap(): return in_vmem(lax.ppermute(value, ('zh', 'zl', 'c'), pairs))  15.5 us
    all_to_all x1, blocking collectives, local(): lax.all_to_all(partial, ('zh', 'x', 'zl'), 0, 0, axis_index_groups=[membe...  13.1 us
    ppermute x1, starting transfers between devices, local(): other = lax.ppermute(send, 'c', [(0, 1), (1, 0)])  2.39 us
    ppermute x1, starting transfers between devices, local(): kv_3 = in_vmem(lax.ppermute(kv_1, 'c', [(0, 1), (1, 0)]))  2.23 us
    pallas_call x1, Pallas kernels, local(): pl.pallas_call(main_kernel, out_shape=(pltpu.VMEM((steps, image, rows * H...  1.98 us
    pallas_call x1, Pallas kernels, local(): pl.pallas_call(prepare_kernel, out_shape=(pltpu.VMEM(by_step, bf16), pltp...  1.51 us
    pallas_call x1, Pallas kernels, local(): pl.pallas_call(query_kernel, out_shape=jax.ShapeDtypeStruct(queries.shape...  1.27 us
    pallas_call x1, Pallas kernels, local(): pl.pallas_call(first_kernel, out_shape=(pltpu.VMEM(by_part, f32), pltpu.V...  1.16 us
  transfers between devices with their start and end apart: 4, of which 0 were waited for; matrix products, arithmetic and copies ran while one was open for 0% of the time, Pallas kernels for 9%

profile of v11, /device:TPU:1, one launch (start us, length us, event | category | flops | bytes accessed | tf_op | source)
XLA Modules:
  0.0 42.3 jit_solution(17478688628922526428)
XLA Ops:
  0.6 1.1 %pick.1 = (bf16[2,128,128]{2,1,0:T(8,128)(2,1)S(1)}, bf16[2,128,128]{2,1,0:T(8,128)(2,1)S(1)}, bf16[2,128,128]{2,1,0:T(8,128)(2,1)S(1)}) custom-call(bf16[128,1024]{1,0:T(8,128)(2,1)} %keys.1, bf16[128,1024]{1,0:T(8,128)(2,1)} %values.1), custom_call_target="tpu_custom_call" | custom-call | tf_op jit(solution)/shard_map/pick/pallas_call | solution.py:223
  1.7 11.5 %collective-permute-start = (bf16[2,128,128]{2,1,0:T(8,128)(2,1)S(1)}, bf16[2,128,128]{2,1,0:T(8,128)(2,1)S(1)}, u32[]{:S(2)}, u32[]{:S(2)}) collective-permute-start(bf16[2,128,128]{2,1,0:T(8,128)(2,1)S(1)} %get-tuple-element.20), channel_id=1, source_target_pairs={{2,50},{16,32},{32,16},{50,2},{0,48},{18,34},{34,18},{48,0},{3,33}... | collective-permute-start | bytes 196616 | tf_op jit(solution)/shard_map/ppermute | solution.py:213
  13.2 4.0 %collective-permute-start.1 = (bf16[2,128,128]{2,1,0:T(8,128)(2,1)S(1)}, bf16[2,128,128]{2,1,0:T(8,128)(2,1)S(1)}, u32[]{:S(2)}, u32[]{:S(2)}) collective-permute-start(bf16[2,128,128]{2,1,0:T(8,128)(2,1)S(1)} %get-tuple-element.21), channel_id=1, source_target_pairs={{2,16},{16,2},{32,50},{50,32},{0,18},{18,0},{34,48},{48,34},{3,17}... | collective-permute-start | bytes 196616 | tf_op jit(solution)/shard_map/ppermute | solution.py:213
  17.9 1.5 %prepare.1 = (bf16[2,1024,128]{2,1,0:T(8,128)(2,1)S(1)}, bf16[2,1024,128]{2,1,0:T(8,128)(2,1)S(1)}, s32[8,128]{1,0:T(8,128)S(1)}, f32[8,128]{1,0:T(8,128)S(1)}) custom-call(s32[8]{0:T(128)} %tiles.1, s32[8]{0:T(128)} %text_len.1, bf16[512,512]{1,0:T(8,128)(2,1)} %queries.1, bf16[512,512]{1,0:T(8,128)(2,1)} %d_out.1, f32[1,1]{1,0:T(1,128)} %bitcast.1.gate), custom_call_target="tpu_custom_call" | custom-call | flops 1048576 | bytes 2097152 | tf_op jit(solution)/shard_map/prepare/pallas_call | solution.py:234
  19.4 0.0 collective-permute-done.kv_1
  19.4 2.2 %collective-permute-start.2 = (bf16[2,128,128]{2,1,0:T(8,128)(2,1)S(1)}, bf16[2,128,128]{2,1,0:T(8,128)(2,1)S(1)}, u32[]{:S(2)}, u32[]{:S(2)}) collective-permute-start(bf16[2,128,128]{2,1,0:T(8,128)(2,1)S(1)} %collective-permute-done.kv_1), channel_id=1, source_target_pairs={{0,1},{1,0},{2,3},{3,2},{4,5},{5,4},{6,7},{7,6},{8,9},{9,8},{10,11... | collective-permute-start | bytes 196616 | tf_op jit(solution)/shard_map/ppermute | solution.py:232
  21.6 0.0 collective-permute-done.1.kv_2
  21.6 1.2 %three_blocks.1 = (f32[2,384,1024]{2,1,0:T(8,128)S(1)}, f32[2,384,1024]{2,1,0:T(8,128)S(1)}, f32[2,8,1024]{2,1,0:T(8,128)S(1)}) custom-call(s32[8,128]{1,0:T(8,128)S(1)} %get-tuple-element.22.live_tiles, bf16[2,128,128]{2,1,0:T(8,128)(2,1)S(1)} %get-tuple-element.19.kv_0, bf16[2,128,128]{2,1,0:T(8,128)(2,1)S(1)} %collective-permute-done.kv_1, ...), custom_call_target="tpu_custom_call" | custom-call | flops 5368709120 | bytes 262144 | tf_op jit(solution)/shard_map/three_blocks/pallas_call | solution.py:259
  22.8 0.0 collective-permute-done.2.kv_3
  22.8 2.0 %gradients.1 = (bf16[2,512,1024]{2,1,0:T(8,128)(2,1)S(1)}, f32[32,16,128]{2,1,0:T(8,128)S(1)}, bf16[32,16,128]{2,1,0:T(8,128)(2,1)S(1)}) custom-call(s32[8,128]{1,0:T(8,128)S(1)} %get-tuple-element.22.live_tiles, f32[2,384,1024]{2,1,0:T(8,128)S(1)} %get-tuple-element.25.expo_1, f32[2,384,1024]{2,1,0:T(8,128)S(1)} %get-tuple-element.26.d_prob_1, ...), custom_call_target="tpu_custom_call" | custom-call | tf_op jit(solution)/shard_map/gradients/pallas_call | solution.py:274
  24.8 2.4 %collective-permute-start.3 = (bf16[32,16,128]{2,1,0:T(8,128)(2,1)S(1)}, bf16[32,16,128]{2,1,0:T(8,128)(2,1)S(1)}, u32[]{:S(2)}, u32[]{:S(2)}) collective-permute-start(bf16[32,16,128]{2,1,0:T(8,128)(2,1)S(1)} %get-tuple-element.30), channel_id=1, source_target_pairs={{0,1},{1,0},{2,3},{3,2},{4,5},{5,4},{6,7},{7,6},{8,9},{9,8},{10,11... | collective-permute-start | bytes 393224 | tf_op jit(solution)/shard_map/ppermute | solution.py:287
  27.2 1.3 %query_gradient.1._ = bf16[512,512]{1,0:T(8,128)(2,1)} custom-call(f32[8,128]{1,0:T(8,128)S(1)} %get-tuple-element.18.gate_factor, bf16[2,128,128]{2,1,0:T(8,128)(2,1)S(1)} %get-tuple-element.19.kv_0, bf16[2,128,128]{2,1,0:T(8,128)(2,1)S(1)} %collective-permute-done.kv_1, bf16[2,128,128]{2,1,0:T(8,128)(2,1)S(1)} %collective-permute-done.1.kv_2, ...), custom_call_target="tpu_custom_call" | custom-call | flops 268435456 | bytes 1048576 | tf_op jit(solution)/shard_map/query_gradient/pallas_call | solution.py:288
  28.5 0.0 collective-permute-done.3.other
  28.5 13.1 %all_to_all.5.pieces = bf16[32,16,128]{2,1,0:T(8,128)(2,1)S(1)} all-to-all(bf16[32,16,128]{2,1,0:T(8,128)(2,1)S(1)} %add_cores.1), channel_id=1, replica_groups={{42,40,46,44,34,32,38,36,58,56,62,60,50,48,54,52,10,8,14,12,2,0,6,4,26,..., dimensions={0} | all-to-all | bytes 262144 | tf_op jit(solution)/shard_map/all_to_all | solution.py:309
  41.7 0.6 %add_up.1 = (f32[8,1024]{1,0:T(8,128)}, f32[8,1024]{1,0:T(8,128)}) custom-call(f32[8,128]{1,0:T(8,128)S(1)} %get-tuple-element.18.gate_factor, bf16[32,16,128]{2,1,0:T(8,128)(2,1)S(1)} %all_to_all.5.pieces), custom_call_target="tpu_custom_call" | custom-call | tf_op jit(solution)/shard_map/add_up/pallas_call | solution.py:310
  (1 shorter events, 0.0 us)
Async XLA Ops:
  1.7 17.7 %collective-permute-start = (bf16[2,128,128]{2,1,0:T(8,128)(2,1)S(1)}, bf16[2,128,128]{2,1,0:T(8,128)(2,1)S(1)}, u32[]{:S(2)}, u32[]{:S(2)}) collective-permute-start(bf16[2,128,128]{2,1,0:T(8,128)(2,1)S(1)} %get-tuple-element.20), channel_id=1, source_target_pairs={{2,50},{16,32},{32,16},{50,2},{0,48},{18,34},{34,18},{48,0},{3,33}... | collective-permute-start | bytes 196616 | tf_op jit(solution)/shard_map/ppermute | solution.py:213
  13.2 8.4 %collective-permute-start.1 = (bf16[2,128,128]{2,1,0:T(8,128)(2,1)S(1)}, bf16[2,128,128]{2,1,0:T(8,128)(2,1)S(1)}, u32[]{:S(2)}, u32[]{:S(2)}) collective-permute-start(bf16[2,128,128]{2,1,0:T(8,128)(2,1)S(1)} %get-tuple-element.21), channel_id=1, source_target_pairs={{2,16},{16,2},{32,50},{50,32},{0,18},{18,0},{34,48},{48,34},{3,17}... | collective-permute-start | bytes 196616 | tf_op jit(solution)/shard_map/ppermute | solution.py:213
  19.4 3.4 %collective-permute-start.2 = (bf16[2,128,128]{2,1,0:T(8,128)(2,1)S(1)}, bf16[2,128,128]{2,1,0:T(8,128)(2,1)S(1)}, u32[]{:S(2)}, u32[]{:S(2)}) collective-permute-start(bf16[2,128,128]{2,1,0:T(8,128)(2,1)S(1)} %collective-permute-done.kv_1), channel_id=1, source_target_pairs={{0,1},{1,0},{2,3},{3,2},{4,5},{5,4},{6,7},{7,6},{8,9},{9,8},{10,11... | collective-permute-start | bytes 196616 | tf_op jit(solution)/shard_map/ppermute | solution.py:232
  24.8 3.7 %collective-permute-start.3 = (bf16[32,16,128]{2,1,0:T(8,128)(2,1)S(1)}, bf16[32,16,128]{2,1,0:T(8,128)(2,1)S(1)}, u32[]{:S(2)}, u32[]{:S(2)}) collective-permute-start(bf16[32,16,128]{2,1,0:T(8,128)(2,1)S(1)} %get-tuple-element.30), channel_id=1, source_target_pairs={{0,1},{1,0},{2,3},{3,2},{4,5},{5,4},{6,7},{7,6},{8,9},{9,8},{10,11... | collective-permute-start | bytes 393224 | tf_op jit(solution)/shard_map/ppermute | solution.py:287
